TPU v7x, 32 devices: a whole 2x2x4 slice. The times are simulated.
32 devices in a mesh: dp: 8 (over z, x), chan: 4 (over y, core).
Axes of the slice: x: 2, y: 2, z: 4, core: 2. Of those that a mesh axis runs over, the one named last changes fastest.
Arguments:
- inputs: bfloat16 [768, 16384], P('chan', 'dp'), may hold values from -6 to 6
- seq_table: int32 [8, 2], P('dp'), may hold values from 1 to 2048, as said below
- mix_gain: float32 [2, 768], P(None, 'chan'), may hold values from 0.5 to 1.5
- mix_bias: float32 [2, 768], P(None, 'chan'), may hold values from -3 to 3
- in_proj: bfloat16 [2, 768, 3, 768], P(None, 'chan'), may hold values from -0.21875 to 0.21875
- short_conv: float32 [2, 3, 3, 768], P(None, None, None, 'chan'), may hold values from -1 to 1
- long_filter: float32 [2, 768, 2048], P(None, 'chan'), may hold values from -0.125 to 0.125
- cond_weight: float32 [2, 768], P(None, 'chan'), may hold values from 0.5 to 1.5
- out_proj: bfloat16 [2, 768, 768], P(None, 'chan'), may hold values from -0.21875 to 0.21875
- glu_gain: float32 [2, 768], P(None, 'chan'), may hold values from 0.5 to 1.5
- glu_bias: float32 [2, 768], P(None, 'chan'), may hold values from -3 to 3
- glu_in: bfloat16 [2, 768, 2, 3072], P(None, None, None, 'chan'), may hold values from -0.21875 to 0.21875
- glu_out: bfloat16 [2, 768, 3072], P(None, None, 'chan'), may hold values from -0.109375 to 0.109375
- cotangent: bfloat16 [768, 16384], P('chan', 'dp'), may hold values from -6 to 6
Outputs:
- outputs: float32 [768, 16384], P('chan', 'dp')
- input_grad: float32 [768, 16384], P('chan', 'dp')
- mix_gain_grad: float32 [2, 768], P(None, 'chan')
- mix_bias_grad: float32 [2, 768], P(None, 'chan')
- in_proj_grad: float32 [2, 768, 3, 768], P(None, ('chan', 'dp'))
- short_conv_grad: float32 [2, 3, 3, 768], P(None, None, None, 'chan')
- long_filter_grad: float32 [2, 768, 2048], P(None, ('chan', 'dp'))
- cond_weight_grad: float32 [2, 768], P(None, 'chan')
- out_proj_grad: float32 [2, 768, 768], P(None, ('chan', 'dp'))
- glu_gain_grad: float32 [2, 768], P(None, 'chan')
- glu_bias_grad: float32 [2, 768], P(None, 'chan')
- glu_in_grad: float32 [2, 768, 2, 3072], P(None, 'dp', None, 'chan')
- glu_out_grad: float32 [2, 768, 3072], P(None, 'dp', 'chan')
Inputs may be any that keep to these rules, and one draw needn't show every extreme that they name: `seq_table`: row r describes slab r: column 0 is a bucket length 512, 1024 or 2048, column 1 how many sequences of that length it holds (at least 1), and their product is at most 2048. Some row has length 2048, and some row has length 512 with 4 sequences.
All inputs are finite; a program needn't handle non-finite values.
Results may differ from a plain program's by a relative error of at most 0.025.
Values may be sent and summed in bfloat16 or wider, within the bound.
A program may use at most 384 MiB of HBM per device.

v0:
```python
from functools import partial
import math

import jax
import jax.numpy as jnp
from jax import lax
from jax.sharding import PartitionSpec as P

EPSILON = 1e-05
PRECISE = lax.Precision.HIGHEST


def segment_ids(table_row, slots):
    slot_index = jnp.arange(slots, dtype=jnp.int32)
    active = slot_index < table_row[0] * table_row[1]
    return jnp.where(active, slot_index // table_row[0], slots + slot_index)


def short_mix(stream, weights, segment):
    summed = stream * weights[0]
    for offset in (1, 2):
        shifted = jnp.concatenate(
            [jnp.zeros((offset,) + stream.shape[1:], stream.dtype), stream[:-offset]], axis=0
        )
        earlier = jnp.concatenate([jnp.full((offset,), -1, jnp.int32), segment[:-offset]], axis=0)
        same_seq = (earlier == segment).astype(stream.dtype)
        summed = summed + shifted * weights[offset] * same_seq[:, None, None]
    return summed


def dft_tables(block_len):
    period = 2 * block_len
    frequency = jnp.arange(block_len + 1, dtype=jnp.int32)
    position = jnp.arange(period, dtype=jnp.int32)
    phase = (frequency[:, None] * position[None, :] % period).astype(jnp.float32) * (
        2.0 * math.pi / period
    )
    cosine = jnp.cos(phase)
    sine_neg = -jnp.sin(phase)
    weighting = jnp.where((frequency == 0) | (frequency == block_len), 1.0, 2.0) / period
    back_cosine = (cosine * weighting[:, None]).T[:block_len]
    back_sine = (sine_neg * weighting[:, None]).T[:block_len]
    return (cosine, sine_neg, back_cosine, back_sine)


def pair_masks(table_row, block_len, blocks):
    block_index = jnp.arange(blocks, dtype=jnp.int32)
    start_slot = block_index * block_len
    active = start_slot < table_row[0] * table_row[1]
    masks_list = []
    for shift_by in range(blocks):
        source = block_index - shift_by
        same_seq = start_slot // table_row[0] == jnp.maximum(source, 0) * block_len // table_row[0]
        masks_list.append((active & (source >= 0) & same_seq).astype(jnp.float32))
    return jnp.stack(masks_list)


def member_table(segment, blocks):
    return (segment[:, None] == jnp.arange(blocks, dtype=jnp.int32)[None, :]).astype(jnp.float32)


def block_conv(signal, kernel, pair_mask, tables):
    cosine, sine_neg, back_cosine, back_sine = tables
    block_len = back_cosine.shape[0]
    blocks = signal.shape[0] // block_len
    channels = signal.shape[1]
    pieces = signal.reshape(blocks, block_len, channels)
    input_real = jnp.einsum("fb,jbc->jfc", cosine[:, :block_len], pieces, precision=PRECISE)
    input_imag = jnp.einsum("fb,jbc->jfc", sine_neg[:, :block_len], pieces, precision=PRECISE)
    padded = jnp.concatenate([jnp.zeros((block_len, channels), kernel.dtype), kernel], axis=0)
    lagged = jnp.stack(
        [
            jnp.concatenate(
                [
                    padded[(shift_by + 1) * block_len : (shift_by + 2) * block_len],
                    padded[shift_by * block_len : (shift_by + 1) * block_len],
                ],
                axis=0,
            )
            for shift_by in range(blocks)
        ]
    )
    kernel_real = jnp.einsum("fm,kmc->kfc", cosine, lagged, precision=PRECISE)
    kernel_imag = jnp.einsum("fm,kmc->kfc", sine_neg, lagged, precision=PRECISE)
    output_real = jnp.zeros_like(input_real)
    output_imag = jnp.zeros_like(input_imag)
    for shift_by in range(blocks):
        filler = jnp.zeros((shift_by, block_len + 1, channels), jnp.float32)
        source_real = jnp.concatenate([filler, input_real[: blocks - shift_by]], axis=0)
        source_imag = jnp.concatenate([filler, input_imag[: blocks - shift_by]], axis=0)
        weighting = pair_mask[shift_by][:, None, None]
        output_real = output_real + weighting * (
            kernel_real[shift_by] * source_real - kernel_imag[shift_by] * source_imag
        )
        output_imag = output_imag + weighting * (
            kernel_real[shift_by] * source_imag + kernel_imag[shift_by] * source_real
        )
    result = jnp.einsum("af,jfc->jac", back_cosine, output_real, precision=PRECISE) + jnp.einsum(
        "af,jfc->jac", back_sine, output_imag, precision=PRECISE
    )
    return result.reshape(blocks * block_len, channels)


def mixer_core(project, weights, kernel, cond_row, segment, pair_mask, tables, members):
    mixed_streams = short_mix(project, weights, segment)
    signal = mixed_streams[:, 1] * mixed_streams[:, 2]
    convolved = block_conv(signal, kernel.T, pair_mask, tables)
    energy_stream = mixed_streams[:, 2]
    counts = jnp.maximum(jnp.sum(members, axis=0), 1.0)
    energy = jnp.dot(members.T, energy_stream * energy_stream, precision=PRECISE) / counts[:, None]
    factor = 1.0 + cond_row * jnp.log(1.0 + energy)
    slot_factor = jnp.dot(members, factor, precision=PRECISE)
    return mixed_streams[:, 0] * (convolved * slot_factor)


def glu_units(gate_up):
    return jax.nn.gelu(gate_up[:, 0], approximate=False) * gate_up[:, 1]


def channel_sums(first_sum, second_sum):
    return lax.psum((first_sum, second_sum), "chan")


def gather_channels(values):
    return lax.all_gather(values, "chan", axis=1, tiled=True)


def sum_channels(summand):
    return lax.psum_scatter(
        summand.astype(jnp.bfloat16), "chan", scatter_dimension=1, tiled=True
    ).astype(jnp.float32)


def norm_forward(values, gain_row, shift_row, model_width):
    first_sum, second_sum = channel_sums(jnp.sum(values, axis=1), jnp.sum(values * values, axis=1))
    row_mean = first_sum / model_width
    spread = second_sum / model_width - row_mean * row_mean
    inverse = lax.rsqrt(spread + EPSILON)
    normal = (values - row_mean[:, None]) * inverse[:, None]
    return ((normal * gain_row + shift_row).astype(jnp.bfloat16), (normal, inverse))


def norm_backward(grad_norm, kept_norm, gain_row, model_width):
    normal, inverse = kept_norm
    gain_grad = jnp.sum(grad_norm * normal, axis=0)
    bias_grad = jnp.sum(grad_norm, axis=0)
    scaled = grad_norm * gain_row
    first_sum, second_sum = channel_sums(jnp.sum(scaled, axis=1), jnp.sum(scaled * normal, axis=1))
    result = inverse[:, None] * (
        scaled - first_sum[:, None] / model_width - normal * second_sum[:, None] / model_width
    )
    return (result, gain_grad, bias_grad)


def stack_layers(*pieces):
    return jnp.stack(pieces)


def body(
    inputs,
    seq_table,
    mix_gain,
    mix_bias,
    in_proj,
    short_conv,
    long_filter,
    cond_weight,
    out_proj,
    glu_gain,
    glu_bias,
    glu_in,
    glu_out,
    cotangent,
):
    slots = inputs.shape[1]
    block_len = slots // 4
    table_row = seq_table[0]
    segment = segment_ids(table_row, slots)
    core_fixed = partial(
        mixer_core,
        segment=segment,
        pair_mask=pair_masks(table_row, block_len, 4),
        tables=dft_tables(block_len),
        members=member_table(segment, 4),
    )
    model_width = in_proj.shape[3]
    layers = in_proj.shape[0]
    contract_last = (((1,), (1,)), ((), ()))
    contract_first = (((0,), (0,)), ((), ()))
    residual = inputs.astype(jnp.float32).T
    kept_values = []
    for layer_no in range(layers):
        normed, mix_kept = norm_forward(
            residual, mix_gain[layer_no], mix_bias[layer_no], model_width
        )
        full_normed = gather_channels(normed)
        project = jnp.einsum(
            "sd,ekd->ske", full_normed, in_proj[layer_no], preferred_element_type=jnp.float32
        )
        gated_out, core_back = jax.vjp(
            core_fixed, project, short_conv[layer_no], long_filter[layer_no], cond_weight[layer_no]
        )
        full_gated = gather_channels(gated_out.astype(jnp.bfloat16))
        residual = residual + lax.dot_general(
            full_gated, out_proj[layer_no], contract_last, preferred_element_type=jnp.float32
        )
        normed_glu, glu_kept = norm_forward(
            residual, glu_gain[layer_no], glu_bias[layer_no], model_width
        )
        full_glu = gather_channels(normed_glu)
        gate_up = jnp.einsum(
            "sd,dke->ske", full_glu, glu_in[layer_no], preferred_element_type=jnp.float32
        )
        glu_values, glu_back = jax.vjp(glu_units, gate_up)
        glu_low = glu_values.astype(jnp.bfloat16)
        summand = lax.dot_general(
            glu_low, glu_out[layer_no], contract_last, preferred_element_type=jnp.float32
        )
        branch = lax.psum_scatter(
            summand.astype(jnp.bfloat16), "chan", scatter_dimension=1, tiled=True
        ).astype(jnp.float32)
        residual = residual + branch
        kept_values.append(
            (mix_kept, full_normed, core_back, full_gated, glu_kept, full_glu, glu_back, glu_low)
        )
    grad_state = cotangent.astype(jnp.float32).T
    layer_grads = [None] * layers
    for layer_no in reversed(range(layers)):
        mix_kept, full_normed, core_back, full_gated, glu_kept, full_glu, glu_back, glu_low = (
            kept_values[layer_no]
        )
        branch_low = grad_state.astype(jnp.bfloat16)
        full_branch = lax.all_gather(branch_low, "chan", axis=1, tiled=True)
        unit_grad = jnp.dot(full_branch, glu_out[layer_no], preferred_element_type=jnp.float32)
        down_grad = lax.dot_general(
            full_branch, glu_low, contract_first, preferred_element_type=jnp.float32
        )
        (gate_up_grad,) = glu_back(unit_grad)
        gate_low = gate_up_grad.astype(jnp.bfloat16)
        glu_in_grad = jnp.einsum(
            "sd,ske->dke", full_glu, gate_low, preferred_element_type=jnp.float32
        )
        norm_grad = sum_channels(
            jnp.einsum(
                "ske,dke->sd", gate_low, glu_in[layer_no], preferred_element_type=jnp.float32
            )
        )
        input_part, glu_gain_grad, glu_bias_grad = norm_backward(
            norm_grad, glu_kept, glu_gain[layer_no], model_width
        )
        grad_state = grad_state + input_part
        mixer_low = grad_state.astype(jnp.bfloat16)
        out_proj_grad = lax.dot_general(
            mixer_low, full_gated, contract_first, preferred_element_type=jnp.float32
        )
        gated_grad = sum_channels(
            jnp.dot(mixer_low, out_proj[layer_no], preferred_element_type=jnp.float32)
        )
        project_grad, short_grad, filter_grad, cond_grad = core_back(gated_grad)
        project_low = project_grad.astype(jnp.bfloat16)
        in_proj_grad = jnp.einsum(
            "ske,sd->ekd", project_low, full_normed, preferred_element_type=jnp.float32
        )
        norm_grad = sum_channels(
            jnp.einsum(
                "ske,ekd->sd", project_low, in_proj[layer_no], preferred_element_type=jnp.float32
            )
        )
        input_part, mix_gain_grad, mix_bias_grad = norm_backward(
            norm_grad, mix_kept, mix_gain[layer_no], model_width
        )
        grad_state = grad_state + input_part
        large_grads = (in_proj_grad, out_proj_grad, filter_grad, glu_in_grad, down_grad)
        small_grads = (
            mix_gain_grad,
            mix_bias_grad,
            short_grad,
            glu_gain_grad,
            glu_bias_grad,
            cond_grad,
        )
        layer_grads[layer_no] = (large_grads, small_grads)
    large_all = jax.tree.map(stack_layers, *[entry[0] for entry in layer_grads])
    small_all = jax.tree.map(stack_layers, *[entry[1] for entry in layer_grads])
    large_all = (
        lax.psum_scatter(large_all[0], "dp", scatter_dimension=1, tiled=True),
        lax.psum_scatter(large_all[1], "dp", scatter_dimension=1, tiled=True),
        lax.psum_scatter(large_all[2], "dp", scatter_dimension=1, tiled=True),
        lax.psum_scatter(large_all[3], "dp", scatter_dimension=1, tiled=True),
        lax.psum_scatter(large_all[4], "dp", scatter_dimension=1, tiled=True),
    )
    small_all = lax.psum(
        (small_all[0], small_all[1], small_all[2], small_all[3], small_all[4], small_all[5]), "dp"
    )
    return (
        residual.T,
        grad_state.T,
        small_all[0],
        small_all[1],
        large_all[0],
        small_all[2],
        large_all[2],
        small_all[5],
        large_all[1],
        small_all[3],
        small_all[4],
        large_all[3],
        large_all[4],
    )


def solution(mesh):
    in_specs = (
        P("chan", "dp"),
        P("dp", None),
        P(None, "chan"),
        P(None, "chan"),
        P(None, "chan", None, None),
        P(None, None, None, "chan"),
        P(None, "chan", None),
        P(None, "chan"),
        P(None, "chan", None),
        P(None, "chan"),
        P(None, "chan"),
        P(None, None, None, "chan"),
        P(None, None, "chan"),
        P("chan", "dp"),
    )
    out_specs = (
        P("chan", "dp"),
        P("chan", "dp"),
        P(None, "chan"),
        P(None, "chan"),
        P(None, ("chan", "dp"), None, None),
        P(None, None, None, "chan"),
        P(None, ("chan", "dp"), None),
        P(None, "chan"),
        P(None, ("chan", "dp"), None),
        P(None, "chan"),
        P(None, "chan"),
        P(None, "dp", None, "chan"),
        P(None, "dp", "chan"),
    )
    return jax.shard_map(body, mesh=mesh, in_specs=in_specs, out_specs=out_specs, check_vma=False)
```

profile of v0, /device:TPU:0, one launch (start us, length us, event | category | flops | bytes accessed | tf_op | source)
XLA Modules:
  0.0 1479.8 jit_solution(10568791141424042345)
XLA Ops:
  12.5 12.7 all-reduce.107
  48.8 8.9 sine_negate_fusion
  58.8 15.3 %fusion.356 = f32[4,513,192]{1,2,0:T(8,128)S(1)} fusion(f32[1,1024,192]{1,2,0:T(8,128)S(1)} %get-tuple-element.282, f32[1,1024,192]{1,2,0:T(8,128)S(1)} %get-tuple-element.281, f32[1,1024,192]{1,2,0:T(8,128)S(1)} %get-tuple-element.280, f32[1,1024,192]{1,2,0:T(8,128)S(1)} %get-tuple-element.308), kind=kOutput, calls=%fused_computation.511 | convolution fusion | flops 4850989056 | bytes 4721664 | tf_op jit(solution)/shard_map/jvp(fm,kmc->kfc)/dot_general | solution.py:83
  75.3 15.2 %fusion.362 = f32[4,513,192]{1,2,0:T(8,128)S(1)} fusion(f32[1,1024,192]{1,2,0:T(8,128)S(1)} %get-tuple-element.282, f32[1,1024,192]{1,2,0:T(8,128)S(1)} %get-tuple-element.281, f32[1,1024,192]{1,2,0:T(8,128)S(1)} %get-tuple-element.280, f32[1,1024,192]{1,2,0:T(8,128)S(1)} %get-tuple-element.308), kind=kOutput, calls=%fused_computation.513 | convolution fusion | flops 4851514368 | bytes 4721664 | tf_op jit(solution)/shard_map/jvp(fm,kmc->kfc)/dot_general | solution.py:84
  123.9 9.1 fusion.133
  146.9 27.7 %all-gather.11.cloned.1.call-done = bf16[2048,768]{0,1:T(8,128)(2,1)} async-done(((bf16[2048,192]{0,1:T(8,128)(2,1)}), bf16[2048,768]{0,1:T(8,128)(2,1)}) %all-gather.11.cloned.1.call-update) | async-done | bytes 3145744 | tf_op jit(solution)/shard_map/all_gather | solution.py:125
  177.4 10.2 all-reduce.106
  197.4 21.9 %all-gather.13.cloned.1.call-done = bf16[2048,768]{0,1:T(8,128)(2,1)} async-done(((bf16[2048,192]{0,1:T(8,128)(2,1)}), bf16[2048,768]{0,1:T(8,128)(2,1)}) %all-gather.13.cloned.1.call-update) | async-done | bytes 3145744 | tf_op jit(solution)/shard_map/all_gather | solution.py:125
  231.9 17.3 %convolution_convert_fusion.1 = bf16[2048,768]{0,1:T(8,128)(2,1)} fusion(f32[2048,2,768]{2,0,1:T(8,128)S(1)} %fusion.75, bf16[2,768,768]{2,1,0:T(8,128)(2,1)S(1)} %copy-done.229), kind=kOutput, calls=%fused_computation.145 | convolution fusion | flops 2521300992 | bytes 16908288 | tf_op jit(solution)/shard_map/dot_general | solution.py:216
  249.3 38.1 %reduce-scatter.14.cloned.1.call-done = bf16[2048,192]{0,1:T(8,128)(2,1)} async-done(((bf16[2048,768]{0,1:T(8,128)(2,1)}), bf16[2048,192]{0,1:T(8,128)(2,1)}) %reduce-scatter.14.cloned.1.call-update) | async-done | bytes 786448 | tf_op jit(solution)/shard_map/reduce_scatter | solution.py:219
  289.4 11.0 all-reduce.105
  303.6 15.1 %fusion.359 = f32[4,513,192]{1,2,0:T(8,128)S(1)} fusion(f32[1,1024,192]{1,2,0:T(8,128)S(1)} %get-tuple-element.279, f32[1,1024,192]{1,2,0:T(8,128)S(1)} %get-tuple-element.278, f32[1,1024,192]{1,2,0:T(8,128)S(1)} %get-tuple-element.277, f32[1,1024,192]{1,2,0:T(8,128)S(1)} %copy-done.129), kind=kOutput, calls=%fused_computation.512 | convolution fusion | flops 4850989056 | bytes 4721664 | tf_op jit(solution)/shard_map/jvp(fm,kmc->kfc)/dot_general | solution.py:83
  320.0 15.2 %fusion.365 = f32[4,513,192]{1,2,0:T(8,128)S(1)} fusion(f32[1,1024,192]{1,2,0:T(8,128)S(1)} %get-tuple-element.279, f32[1,1024,192]{1,2,0:T(8,128)S(1)} %get-tuple-element.278, f32[1,1024,192]{1,2,0:T(8,128)S(1)} %get-tuple-element.277, f32[1,1024,192]{1,2,0:T(8,128)S(1)} %copy-done.129), kind=kOutput, calls=%fused_computation.514 | convolution fusion | flops 4851514368 | bytes 4721664 | tf_op jit(solution)/shard_map/jvp(fm,kmc->kfc)/dot_general | solution.py:84
  375.3 9.1 add_bitcast_fusion.5
  390.3 29.0 %all-gather.17.cloned.1.call-done = bf16[2048,768]{0,1:T(8,128)(2,1)} async-done(((bf16[2048,192]{0,1:T(8,128)(2,1)}), bf16[2048,768]{0,1:T(8,128)(2,1)}) %all-gather.17.cloned.1.call-update) | async-done | bytes 3145744 | tf_op jit(solution)/shard_map/all_gather | solution.py:125
  422.1 10.7 all-reduce.104
  434.1 15.4 %all-gather.21.cloned.1.call-done = bf16[2048,768]{0,1:T(8,128)(2,1)} async-done(((bf16[2048,192]{0,1:T(8,128)(2,1)}), bf16[2048,768]{0,1:T(8,128)(2,1)}) %all-gather.21.cloned.1.call-update) | async-done | bytes 3145744 | tf_op jit(solution)/shard_map/all_gather | solution.py:233
  457.0 22.7 %all-gather.19.cloned.1.call-done = bf16[2048,768]{0,1:T(8,128)(2,1)} async-done(((bf16[2048,192]{0,1:T(8,128)(2,1)}), bf16[2048,768]{0,1:T(8,128)(2,1)}) %all-gather.19.cloned.1.call-update) | async-done | bytes 3145744 | tf_op jit(solution)/shard_map/all_gather | solution.py:125
  487.6 15.0 %multiply_bitcast_fusion.1 = (f32[2048,1,768]{2,0,1:T(8,128)}, f32[2048,768]{1,0:T(8,128)S(1)}) fusion(f32[2048,768]{1,0:T(8,128)S(1)} %copy-done.33, f32[2048,2,768]{2,0,1:T(8,128)S(1)} %fusion.69), kind=kLoop, calls=%fused_computation.65 | loop fusion | flops 102236160 | bytes 25165824 | tf_op jit(solution)/shard_map/transpose(jvp())/broadcast_in_dim | solution.py:117
  511.2 11.1 bitcast_convert_fusion.3
  522.4 19.3 %convolution_convert_fusion = bf16[2048,768]{0,1:T(8,128)(2,1)} fusion(f32[2048,2,768]{2,0,1:T(8,128)} %copy-done.21, bf16[2,768,768]{2,1,0:T(8,128)(2,1)} %param.26), kind=kOutput, calls=%fused_computation.143 | convolution fusion | flops 2521300992 | bytes 16908288 | tf_op jit(solution)/shard_map/dot_general | solution.py:216
  541.7 18.7 %reduce-scatter.18.cloned.1.call-done = bf16[2048,192]{0,1:T(8,128)(2,1)} async-done(((bf16[2048,768]{0,1:T(8,128)(2,1)}), bf16[2048,192]{0,1:T(8,128)(2,1)}) %reduce-scatter.18.cloned.1.call-update) | async-done | bytes 786448 | tf_op jit(solution)/shard_map/reduce_scatter | solution.py:129
  563.0 10.1 all-reduce.103
  573.1 27.7 %reduce-scatter.16.cloned.1.call-done = bf16[2048,192]{0,1:T(8,128)(2,1)} async-done(((bf16[2048,768]{0,1:T(8,128)(2,1)}), bf16[2048,192]{0,1:T(8,128)(2,1)}) %reduce-scatter.16.cloned.1.call-update) | async-done | bytes 786448 | tf_op jit(solution)/shard_map/reduce_scatter | solution.py:219
  607.5 37.6 %reduce-scatter.20.cloned.1.call-done = bf16[2048,192]{0,1:T(8,128)(2,1)} async-done(((bf16[2048,768]{0,1:T(8,128)(2,1)}), bf16[2048,192]{0,1:T(8,128)(2,1)}) %reduce-scatter.20.cloned.1.call-update) | async-done | bytes 786448 | tf_op jit(solution)/shard_map/reduce_scatter | solution.py:129
  716.3 38.1 %reduce-scatter.22.cloned.1.call-done = bf16[2048,192]{0,1:T(8,128)(2,1)} async-done(((bf16[2048,768]{0,1:T(8,128)(2,1)}), bf16[2048,192]{0,1:T(8,128)(2,1)}) %reduce-scatter.22.cloned.1.call-update) | async-done | bytes 786448 | tf_op jit(solution)/shard_map/reduce_scatter | solution.py:129
  756.8 10.1 all-reduce.102
  769.6 29.7 %all-gather.23.cloned.1.call-done = bf16[2048,768]{0,1:T(8,128)(2,1)} async-done(((bf16[2048,192]{0,1:T(8,128)(2,1)}), bf16[2048,768]{0,1:T(8,128)(2,1)}) %all-gather.23.cloned.1.call-update) | async-done | bytes 3145744 | tf_op jit(solution)/shard_map/all_gather | solution.py:233
  804.4 17.1 %multiply_bitcast_fusion = (f32[2048,1,768]{2,0,1:T(8,128)}, f32[2048,768]{1,0:T(8,128)S(1)}) fusion(f32[2048,768]{1,0:T(8,128)S(1)} %fusion.453, f32[2048,2,768]{2,0,1:T(8,128)} %copy-done.20), kind=kLoop, calls=%fused_computation.53 | loop fusion | flops 102236160 | bytes 25165824 | tf_op jit(solution)/shard_map/transpose(jvp())/broadcast_in_dim | solution.py:117
  830.2 11.1 bitcast_convert_fusion.1
  841.3 38.1 %reduce-scatter.24.cloned.1.call-done = bf16[2048,192]{0,1:T(8,128)(2,1)} async-done(((bf16[2048,768]{0,1:T(8,128)(2,1)}), bf16[2048,192]{0,1:T(8,128)(2,1)}) %reduce-scatter.24.cloned.1.call-update) | async-done | bytes 786448 | tf_op jit(solution)/shard_map/reduce_scatter | solution.py:129
  882.4 10.1 all-reduce.101
  899.5 9.3 fusion.85
  922.2 16.4 %reduce-scatter.26.cloned.1.call-done = bf16[2048,192]{0,1:T(8,128)(2,1)} async-done(((bf16[2048,768]{0,1:T(8,128)(2,1)}), bf16[2048,192]{0,1:T(8,128)(2,1)}) %reduce-scatter.26.cloned.1.call-update) | async-done | bytes 786448 | tf_op jit(solution)/shard_map/reduce_scatter | solution.py:129
  959.4 15.0 %fusion.220 = (f32[513,192]{0,1:T(8,128)}, f32[513,192]{0,1:T(8,128)}, f32[513,192]{0,1:T(8,128)}, f32[513,192]{0,1:T(8,128)}, f32[513,192]{0,1:T(8,128)}, /*ind...) fusion(f32[4,513,192]{1,2,0:T(8,128)S(1)} %copy-done.7, ...), kind=kLoop, calls=%fused_computation.358 | loop fusion | flops 19699200 | bytes 34670656 | tf_op jit(solution)/shard_map/transpose(jvp())/reduce_sum | solution.py:96
  1028.7 10.2 fusion.345
  1038.9 9.5 fusion.342
  1052.3 17.5 %fusion.108 = f32[4,192,1024]{2,1,0:T(8,128)S(1)} fusion(f32[1,513,192]{1,2,0:T(8,128)S(1)} %bitcast.906, f32[1,513,192]{1,2,0:T(8,128)S(1)} %bitcast.905, f32[1,513,192]{1,2,0:T(8,128)} %bitcast.908, f32[1,513,192]{1,2,0:T(8,128)S(1)} %bitcast.907, f32[1,513,192]{1,2,0:T(8,128)} %bitcast.910, f32[1,513,192]{1,2,0:T(8,128)} %bitcast.909, ...), kind=kOutput, calls=%fused_computation.252 | convolution fusion | flops 4851912704 | bytes 6297600 | tf_op jit(solution)/shard_map/transpose(jvp(fm,kmc->kfc))/dot_general | solution.py:84
  1069.9 15.8 %add_bitcast_fusion.1 = f32[4,1024,192]{1,2,0:T(8,128)S(1)} fusion(f32[4,192,1024]{2,1,0:T(8,128)S(1)} %fusion.108, f32[1,513,192]{1,2,0:T(8,128)S(1)} %bitcast.898, f32[1,513,192]{1,2,0:T(8,128)S(1)} %bitcast.897, f32[1,513,192]{1,2,0:T(8,128)S(1)} %bitcast.900, f32[1,513,192]{1,2,0:T(8,128)S(1)} %bitcast.899, f32[1,513,192]{1,2,0:T(8,128)S(1)} %bitcast.902, ...), kind=kOutput, calls=%fused_computation.173 | convolution fusion | flops 4852173824 | bytes 9443328 | tf_op jit(solution)/shard_map/transpose(jvp(fm,kmc->kfc))/dot_general | solution.py:83
  1088.4 15.5 %fusion.106 = f32[4,192,1024]{2,1,0:T(8,128)S(1)} fusion(f32[1,513,192]{1,2,0:T(8,128)S(1)} %bitcast.895, f32[1,513,192]{1,2,0:T(8,128)S(1)} %bitcast.896, f32[1,513,192]{1,2,0:T(8,128)S(1)} %bitcast.890, f32[1,513,192]{1,2,0:T(8,128)S(1)} %bitcast.889, f32[1,513,192]{1,2,0:T(8,128)S(1)} %bitcast.892, f32[1,513,192]{1,2,0:T(8,128)S(1)} %bitcast.891, ...), kind=kOutput, calls=%fused_computation.250 | convolution fusion | flops 4851912704 | bytes 6297600 | tf_op jit(solution)/shard_map/transpose(jvp(fm,kmc->kfc))/dot_general | solution.py:84
  1104.0 15.7 %add_bitcast_fusion = f32[4,1024,192]{1,2,0:T(8,128)S(1)} fusion(f32[4,192,1024]{2,1,0:T(8,128)S(1)} %fusion.106, f32[1,513,192]{1,2,0:T(8,128)S(1)} %bitcast.893, f32[1,513,192]{1,2,0:T(8,128)S(1)} %bitcast.894, f32[1,513,192]{1,2,0:T(8,128)S(1)} %bitcast.884, f32[1,513,192]{1,2,0:T(8,128)S(1)} %bitcast.883, f32[1,513,192]{1,2,0:T(8,128)S(1)} %bitcast.886, ...), kind=kOutput, calls=%fused_computation.172 | convolution fusion | flops 4852173824 | bytes 9443328 | tf_op jit(solution)/shard_map/transpose(jvp(fm,kmc->kfc))/dot_general | solution.py:83
  1135.2 10.4 reduce-scatter.28.cloned.1.call-done
  1147.7 38.1 %all-reduce.99 = (f32[2,192]{1,0:T(2,128)}, f32[2,192]{1,0:T(2,128)}, f32[2,3,3,192]{3,2,1,0:T(4,128)S(1)}, f32[2,192]{1,0:T(2,128)}, f32[2,192]{1,0:T(2,128)}, /*index=5*/f32[2,192]{1,0:T(2,128)}) all-reduce(f32[2,192]{1,0:T(2,128)S(1)} %pad_maximum_fusion.20, ...), channel_id=1, replica_groups=mesh['dp'=8,'chan'=4] {'dp'}, use_global_device_ids=true, to_apply=%region_43.44 | all-reduce | flops 5376 | bytes 43008 | tf_op jit(solution)/shard_map/psum | solution.py:292
  1186.4 10.2 all-reduce.100
  1198.3 15.3 %reduce-scatter.34.cloned.1.call-done = f32[2,24,768]{2,1,0:T(8,128)} async-done(((f32[2,192,768]{2,1,0:T(8,128)}), f32[2,24,768]{2,1,0:T(8,128)}) %reduce-scatter.34.cloned.1.call-update) | async-done | bytes 147472 | tf_op jit(solution)/shard_map/reduce_scatter | solution.py:287
  1213.6 98.5 %reduce-scatter.38.cloned.1.call-done = f32[2,96,768]{2,1,0:T(8,128)} async-done(((f32[2,768,768]{2,1,0:T(8,128)}), f32[2,96,768]{2,1,0:T(8,128)}) %reduce-scatter.38.cloned.1.call-update) | async-done | bytes 589840 | tf_op jit(solution)/shard_map/reduce_scatter | solution.py:290
  1312.1 78.0 %reduce-scatter.32.cloned.1.call-done = f32[2,24,2048]{2,1,0:T(8,128)} async-done(((f32[2,192,2048]{2,1,0:T(8,128)}), f32[2,24,2048]{2,1,0:T(8,128)}) %reduce-scatter.32.cloned.1.call-update) | async-done | bytes 393232 | tf_op jit(solution)/shard_map/reduce_scatter | solution.py:288
  1390.1 82.5 %reduce-scatter.30.cloned.1.call-done = f32[2,24,3,768]{3,1,2,0:T(8,128)} async-done(((f32[2,192,3,768]{3,1,2,0:T(8,128)}), f32[2,24,3,768]{3,1,2,0:T(8,128)}) %reduce-scatter.30.cloned.1.call-update) | async-done | bytes 442384 | tf_op jit(solution)/shard_map/reduce_scatter | solution.py:286
  (698 shorter events, 403.5 us)
Async XLA Ops:
  7.2 84.5 %all-gather.9.cloned.1.call-start = ((), (), s32[]{:S(2)}) async-start(), calls=%async_computation.13 | async-start | bytes 3932160 | tf_op jit(solution)/shard_map/all_gather | solution.py:125
  27.1 147.5 %all-gather.11.cloned.1.call-start = ((), (), s32[]{:S(2)}) async-start(), calls=%async_computation.14 | async-start | bytes 3932160 | tf_op jit(solution)/shard_map/all_gather | solution.py:125
  31.1 101.9 %copy-start.190 = (f32[4]{0:T(128)}, f32[4]{0:T(128)S(1)}, u32[]{:S(2)}) copy-start(f32[4]{0:T(128)S(1)} %get-tuple-element.323) | copy-start | bytes 52
  31.1 65.0 %copy-start.177 = (f32[1,1,3,192]{3,2,0,1:T(4,128)}, f32[1,1,3,192]{3,2,0,1:T(4,128)S(1)}, u32[]{:S(2)}) copy-start(f32[1,1,3,192]{3,2,0,1:T(4,128)S(1)} %copy.121) | copy-start | bytes 6916
  33.3 632.6 %copy-start.127 = (s32[2048]{0:T(1024)}, s32[2048]{0:T(1024)S(1)}, u32[]{:S(2)}) copy-start(s32[2048]{0:T(1024)S(1)} %fusion.587) | copy-start | bytes 24580
  34.1 62.0 %copy-start.161 = (f32[2048]{0:T(1024)}, f32[2048]{0:T(1024)S(1)}, u32[]{:S(2)}) copy-start(f32[2048]{0:T(1024)S(1)} %get-tuple-element.319) | copy-start | bytes 24580
  34.1 62.0 %copy-start.164 = (f32[2048]{0:T(1024)}, f32[2048]{0:T(1024)S(1)}, u32[]{:S(2)}) copy-start(f32[2048]{0:T(1024)S(1)} %get-tuple-element.320) | copy-start | bytes 24580
  39.1 93.9 %copy-start.16 = (f32[1024,513]{0,1:T(8,128)}, f32[1024,513]{0,1:T(8,128)S(1)}, u32[]{:S(2)}) copy-start(f32[1024,513]{0,1:T(8,128)S(1)} %fusion.105) | copy-start | bytes 6303748
  48.8 47.3 %copy-start.179 = (f32[3,192]{1,0:T(4,128)}, f32[3,192]{1,0:T(4,128)S(1)}, u32[]{:S(2)}) copy-start(f32[3,192]{1,0:T(4,128)S(1)} %get-tuple-element.328) | copy-start | bytes 6916
  48.8 47.3 %copy-start.181 = (f32[3,192]{1,0:T(4,128)}, f32[3,192]{1,0:T(4,128)S(1)}, u32[]{:S(2)}) copy-start(f32[3,192]{1,0:T(4,128)S(1)} %get-tuple-element.327) | copy-start | bytes 6916
  75.3 57.7 %copy-start.65 = (f32[513,192]{0,1:T(8,128)}, f32[513,192]{0,1:T(8,128)S(1)}, u32[]{:S(2)}) copy-start(f32[513,192]{0,1:T(8,128)S(1)} %get-tuple-element.255) | copy-start | bytes 1181956
  91.7 41.3 %copy-start.67 = (f32[513,192]{0,1:T(8,128)}, f32[513,192]{0,1:T(8,128)S(1)}, u32[]{:S(2)}) copy-start(f32[513,192]{0,1:T(8,128)S(1)} %get-tuple-element.259) | copy-start | bytes 1181956
  145.7 73.6 %all-gather.13.cloned.1.call-start = ((), (), s32[]{:S(2)}) async-start(), calls=%async_computation.15 | async-start | bytes 3932160 | tf_op jit(solution)/shard_map/all_gather | solution.py:125
  146.3 41.4 %copy-start.197 = (f32[1,192]{1,0:T(1,128)}, f32[1,192]{1,0:T(1,128)S(1)}, u32[]{:S(2)}) copy-start(f32[1,192]{1,0:T(1,128)S(1)} %get-tuple-element.298) | copy-start | bytes 2308
  177.4 109.9 %copy-start.24 = (f32[2048,192]{0,1:T(8,128)}, f32[2048,192]{0,1:T(8,128)S(1)}, u32[]{:S(2)}) copy-start(f32[2048,192]{0,1:T(8,128)S(1)} %get-tuple-element.312) | copy-start | bytes 4718596
  189.6 97.8 %reduce-scatter.14.cloned.1.call-start = ((), (), s32[]{:S(2)}) async-start(), calls=%async_computation.16 | async-start | bytes 3932160 | tf_op jit(solution)/shard_map/reduce_scatter | solution.py:219
  249.2 87.3 %all-gather.15.cloned.1.call-start = ((), (), s32[]{:S(2)}) async-start(), calls=%async_computation.17 | async-start | bytes 3932160 | tf_op jit(solution)/shard_map/all_gather | solution.py:125
  289.4 129.8 %copy-start.10 = (f32[2048,192]{0,1:T(8,128)}, f32[2048,192]{0,1:T(8,128)S(1)}, u32[]{:S(2)}) copy-start(f32[2048,192]{0,1:T(8,128)S(1)} %get-tuple-element.170) | copy-start | bytes 4718596
  302.4 116.8 %all-gather.17.cloned.1.call-start = ((), (), s32[]{:S(2)}) async-start(), calls=%async_computation.18 | async-start | bytes 3932160 | tf_op jit(solution)/shard_map/all_gather | solution.py:125
  302.5 38.3 %copy-start.183 = (f32[1,1,3,192]{3,2,0,1:T(4,128)}, f32[1,1,3,192]{3,2,0,1:T(4,128)S(1)}, u32[]{:S(2)}) copy-start(f32[1,1,3,192]{3,2,0,1:T(4,128)S(1)} %copy.120) | copy-start | bytes 6916
  389.4 60.1 %all-gather.21.cloned.1.call-start = ((), (), s32[]{:S(2)}) async-start(), calls=%async_computation.21 | async-start | bytes 3932160 | tf_op jit(solution)/shard_map/all_gather | solution.py:233
  390.2 42.6 %copy-start.204 = (f32[1,192]{1,0:T(1,128)S(1)}, f32[1,192]{1,0:T(1,128)}, u32[]{:S(2)}) copy-start(f32[1,192]{1,0:T(1,128)} %get-tuple-element.297) | copy-start | bytes 2308
  390.2 42.6 %copy-start.221 = (f32[1,192]{1,0:T(1,128)S(1)}, f32[1,192]{1,0:T(1,128)}, u32[]{:S(2)}) copy-start(f32[1,192]{1,0:T(1,128)} %get-tuple-element.299) | copy-start | bytes 2308
  390.2 89.5 %all-gather.19.cloned.1.call-start = ((), (), s32[]{:S(2)}) async-start(), calls=%async_computation.19 | async-start | bytes 3932160 | tf_op jit(solution)/shard_map/all_gather | solution.py:125
  422.1 138.4 %copy-start.32 = (f32[2048,192]{0,1:T(8,128)}, f32[2048,192]{0,1:T(8,128)S(1)}, u32[]{:S(2)}) copy-start(f32[2048,192]{0,1:T(8,128)S(1)} %get-tuple-element.314) | copy-start | bytes 4718596
  434.1 126.4 %reduce-scatter.18.cloned.1.call-start = ((), (), s32[]{:S(2)}) async-start(), calls=%async_computation.22 | async-start | bytes 3932160 | tf_op jit(solution)/shard_map/reduce_scatter | solution.py:129
  522.3 78.5 %reduce-scatter.16.cloned.1.call-start = ((), (), s32[]{:S(2)}) async-start(), calls=%async_computation.20 | async-start | bytes 3932160 | tf_op jit(solution)/shard_map/reduce_scatter | solution.py:219
  541.6 59.2 %copy-start.113 = (bf16[192,2048]{1,0:T(8,128)(2,1)S(1)}, bf16[192,2048]{1,0:T(8,128)(2,1)}, u32[]{:S(2)}) copy-start(bf16[192,2048]{1,0:T(8,128)(2,1)} %param.27) | copy-start | bytes 2359300
  541.6 103.5 %reduce-scatter.20.cloned.1.call-start = ((), (), s32[]{:S(2)}) async-start(), calls=%async_computation.23 | async-start | bytes 3932160 | tf_op jit(solution)/shard_map/reduce_scatter | solution.py:129
  560.5 40.4 %copy-start.112 = (bf16[2048,192]{0,1:T(8,128)(2,1)S(1)}, bf16[2048,192]{0,1:T(8,128)(2,1)}, u32[]{:S(2)}) copy-start(bf16[2048,192]{0,1:T(8,128)(2,1)} %reduce-scatter.18.cloned.1.call-done) | copy-start | bytes 2359300
  604.4 288.2 %copy-start.14 = (f32[2048,192]{0,1:T(8,128)}, f32[2048,192]{0,1:T(8,128)S(1)}, u32[]{:S(2)}) copy-start(f32[2048,192]{0,1:T(8,128)S(1)} %get-tuple-element.263) | copy-start | bytes 4718596
  607.1 147.3 %reduce-scatter.22.cloned.1.call-start = ((), (), s32[]{:S(2)}) async-start(), calls=%async_computation.24 | async-start | bytes 3932160 | tf_op jit(solution)/shard_map/reduce_scatter | solution.py:129
  716.2 38.2 %copy-start.11 = (f32[2048,192]{0,1:T(8,128)S(1)}, f32[2048,192]{0,1:T(8,128)}, u32[]{:S(2)}) copy-start(f32[2048,192]{0,1:T(8,128)} %copy-done.10) | copy-start | bytes 4718596
  716.2 38.2 %copy-start.158 = (f32[2048]{0:T(1024)S(1)}, f32[2048]{0:T(1024)}, u32[]{:S(2)}) copy-start(f32[2048]{0:T(1024)} %copy-done.157) | copy-start | bytes 24580
  716.2 38.2 %copy-start.160 = (f32[2048]{0:T(1024)S(1)}, f32[2048]{0:T(1024)}, u32[]{:S(2)}) copy-start(f32[2048]{0:T(1024)} %copy-done.159) | copy-start | bytes 24580
  716.2 38.2 %copy-start.189 = (f32[1,192]{1,0:T(1,128)S(1)}, f32[1,192]{1,0:T(1,128)}, u32[]{:S(2)}) copy-start(f32[1,192]{1,0:T(1,128)} %get-tuple-element.303) | copy-start | bytes 2308
  716.2 83.1 %all-gather.23.cloned.1.call-start = ((), (), s32[]{:S(2)}) async-start(), calls=%async_computation.25 | async-start | bytes 3932160 | tf_op jit(solution)/shard_map/all_gather | solution.py:233
  769.6 109.8 %reduce-scatter.24.cloned.1.call-start = ((), (), s32[]{:S(2)}) async-start(), calls=%async_computation.26 | async-start | bytes 3932160 | tf_op jit(solution)/shard_map/reduce_scatter | solution.py:129
  841.2 38.2 %copy-start.174 = (f32[2048]{0:T(1024)S(1)}, f32[2048]{0:T(1024)}, u32[]{:S(2)}) copy-start(f32[2048]{0:T(1024)} %copy-done.173) | copy-start | bytes 24580
  841.2 38.2 %copy-start.198 = (f32[1,192]{1,0:T(1,128)S(1)}, f32[1,192]{1,0:T(1,128)}, u32[]{:S(2)}) copy-start(f32[1,192]{1,0:T(1,128)} %copy-done.197) | copy-start | bytes 2308
  841.3 97.3 %reduce-scatter.26.cloned.1.call-start = ((), (), s32[]{:S(2)}) async-start(), calls=%async_computation.27 | async-start | bytes 3932160 | tf_op jit(solution)/shard_map/reduce_scatter | solution.py:129
  899.5 232.5 %reduce-scatter.36.cloned.1.call-start = ((), (), s32[]{:S(2)}) async-start(), calls=%async_computation.32 | async-start | bytes 10616832 | tf_op jit(solution)/shard_map/reduce_scatter | solution.py:289
  921.7 223.8 %reduce-scatter.28.cloned.1.call-start = ((), (), s32[]{:S(2)}) async-start(), calls=%async_computation.28 | async-start | bytes 3932160 | tf_op jit(solution)/shard_map/reduce_scatter | solution.py:129
  1021.6 192.0 %reduce-scatter.34.cloned.1.call-start = ((), (), s32[]{:S(2)}) async-start(), calls=%async_computation.31 | async-start | bytes 1327104 | tf_op jit(solution)/shard_map/reduce_scatter | solution.py:287
  1028.6 283.5 %reduce-scatter.38.cloned.1.call-start = ((), (), s32[]{:S(2)}) async-start(), calls=%async_computation.33 | async-start | bytes 5308416 | tf_op jit(solution)/shard_map/reduce_scatter | solution.py:290
  1051.0 339.1 %reduce-scatter.32.cloned.1.call-start = ((), (), s32[]{:S(2)}) async-start(), calls=%async_computation.30 | async-start | bytes 3538944 | tf_op jit(solution)/shard_map/reduce_scatter | solution.py:288
  1122.1 350.4 %reduce-scatter.30.cloned.1.call-start = ((), (), s32[]{:S(2)}) async-start(), calls=%async_computation.29 | async-start | bytes 3981312 | tf_op jit(solution)/shard_map/reduce_scatter | solution.py:286
  1145.6 51.0 %copy-start.114 = (bf16[2048,192]{0,1:T(8,128)(2,1)S(1)}, bf16[2048,192]{0,1:T(8,128)(2,1)}, u32[]{:S(2)}) copy-start(bf16[2048,192]{0,1:T(8,128)(2,1)} %reduce-scatter.28.cloned.1.call-done) | copy-start | bytes 2359300
  (216 other events, 1695.7 us)
Sparse Core Ops, SparseCore 0:
  27.2 28.8 all-gather.8
  145.8 28.7 all-gather.10
  189.7 29.5 all-gather.12
  249.3 37.9 reduce-scatter.13
  302.5 29.6 all-gather.14
  389.6 29.6 all-gather.16
  420.9 28.6 all-gather.20
  451.2 28.5 all-gather.18
  522.4 37.9 reduce-scatter.17
  562.8 37.9 reduce-scatter.15
  607.2 37.9 reduce-scatter.19
  716.3 37.9 reduce-scatter.21
  769.7 29.5 all-gather.22
  841.4 37.9 reduce-scatter.23
  899.6 38.9 reduce-scatter.25
  942.5 163.4 reduce-scatter.35
  1108.5 37.0 reduce-scatter.27
  1149.4 64.1 reduce-scatter.33
  1217.8 94.2 reduce-scatter.37
  1316.1 73.9 reduce-scatter.31
  1394.3 78.2 reduce-scatter.29
where the time goes:
time: 1490 us; the launch traced here: 1480 us
  waiting for transfers between devices  647 us (43%)
  matrix products  413 us (28%)
  other arithmetic  189 us (13%)
  blocking collectives  123 us (8%)
  local copies, waits for them, and re-layouts  86 us (6%)
  between operations  19.7 us (1%)
    reduce_scatter x6, waiting for transfers between devices, sum_channels(): lax.psum_scatter(summand.astype(jnp.bfloat16), 'chan', scatter_dimension=...  159 us
    all_gather x6, waiting for transfers between devices, gather_channels(): return lax.all_gather(values, 'chan', axis=1, tiled=True)  101 us
    reduce_scatter x1, waiting for transfers between devices, body(): lax.psum_scatter(large_all[4], 'dp', scatter_dimension=1, tiled=True)  98.5 us
    psum x8, blocking collectives, channel_sums(): return lax.psum((first_sum, second_sum), 'chan')  85.2 us
    reduce_scatter x1, waiting for transfers between devices, body(): lax.psum_scatter(large_all[0], 'dp', scatter_dimension=1, tiled=True)  82.5 us
    reduce_scatter x1, waiting for transfers between devices, body(): lax.psum_scatter(large_all[2], 'dp', scatter_dimension=1, tiled=True)  78 us
    reduce_scatter x2, waiting for transfers between devices, body(): lax.psum_scatter(summand.astype(jnp.bfloat16), 'chan', scatter_dimension=...  65.8 us
    dot_general x4, matrix products, block_conv(): kernel_imag = jnp.einsum('fm,kmc->kfc', sine_neg, lagged, precision=PRECISE)  63.4 us
  transfers between devices with their start and end apart: 21, of which 18 were waited for; matrix products, arithmetic and copies ran while one was open for 23% of the time, Pallas kernels for 0%

commit v1 on v0

v1 whole, which is shorter than its diff:
```python
import math

import jax
import jax.numpy as jnp
import numpy as np
from jax import lax
from jax.experimental import pallas as pl
from jax.experimental.pallas import tpu as pltpu
from jax.sharding import PartitionSpec as P

EPSILON = 1e-05
F32 = jnp.float32
BF16 = jnp.bfloat16
VMEM_LIMIT = 63 * 2**20
LOADS = 4


def dft_table(block_len):
    period = 2 * block_len
    position = np.arange(block_len)[:, None]
    phase = ((2 * np.arange(block_len)[None, :] + 1) * position) % (2 * period)
    phase = phase * (math.pi / period)
    return np.concatenate([np.cos(phase), -np.sin(phase)], axis=1)


class Facts:
    def __init__(self, table_ref, blocks, block_len):
        length, count = table_ref[0, 0], table_ref[0, 1]
        used = length * count
        pair = jnp.where(length >= 2 * block_len, 1.0, 0.0)
        four = jnp.where(length >= 4 * block_len, 1.0, 0.0)
        active = [jnp.where(i * block_len < used, 1.0, 0.0) for i in range(blocks)]
        self.same = [[None] * blocks for _ in range(blocks)]
        for i in range(blocks):
            for j in range(blocks):
                if i == j:
                    self.same[i][j] = active[i]
                else:
                    joined = pair if i // 2 == j // 2 else four
                    self.same[i][j] = active[i] * active[j] * joined
        shortest = 1.0 / block_len
        self.inverse = shortest * (1.0 - 0.5 * pair - 0.25 * four)


class Io:
    def __init__(self, source, loads, stores):
        self.source, self.loads, self.stores, self.pending = source, loads, stores, []

    def ready(self, *numbers, cuts=None):
        for number in numbers:
            for copy in self.loads[number] if cuts is None else self.loads[number][cuts]:
                copy.wait()

    def flush(self, number, part=0, at=None):
        source, target, sems = self.stores[number]
        if at is not None:
            source, target = source.at[at], target.at[at]
        copy = pltpu.make_async_copy(source, target, sems.at[part])
        copy.start()
        self.pending.append(copy)

    def finish(self):
        for copy in self.pending:
            copy.wait()


def fused_call(kernel, operands, outs, scratch, collective, name, parts, scalars=-1, order=(),
               cuts=None, manual=()):
    arrays, layers = [], []
    for operand in operands:
        array, layer = operand if isinstance(operand, tuple) else (operand, None)
        arrays.append(array)
        layers.append(layer)
    cuts = cuts or {}
    inputs, results = len(arrays), len(outs)
    buffers, sems = [], []
    for number, (array, layer) in enumerate(zip(arrays, layers)):
        if number != scalars:
            buffers.append(pltpu.VMEM(array.shape if layer is None else array.shape[1:], array.dtype))
            sems.append(pltpu.SemaphoreType.DMA((len(cuts.get(number, (0,))),)))
    for (shape, dtype), count in zip(outs, parts):
        buffers.append(pltpu.VMEM(shape, dtype))
        sems.append(pltpu.SemaphoreType.DMA((count,)))

    def body(*refs):
        extra = list(refs[inputs + results + len(scratch) :])
        places, marks = extra[: len(buffers)], extra[len(buffers) :]
        sources, loads, stores, views, n = {}, {}, {}, [], 0
        for number in range(inputs):
            if number == scalars:
                views.append(refs[number])
                continue
            source = refs[number]
            if layers[number] is not None:
                source = source.at[layers[number]]
            sources[number] = source
            views.append(places[n])
            if number not in manual:
                pairs = [(source, places[n])]
                if number in cuts:
                    rows = [pl.ds(*one) for one in cuts[number]]
                    pairs = [(source.at[one], places[n].at[one]) for one in rows]
                loads[number] = [
                    pltpu.make_async_copy(*pair, marks[n].at[i]) for i, pair in enumerate(pairs)
                ]
            n += 1
        for number in range(results):
            stores[number] = (places[n], refs[inputs + number], marks[n])
            views.append(places[n])
            n += 1
        started = set()
        for one in list(order) + list(loads):
            number, chosen = one if isinstance(one, tuple) else (one, None)
            for i, copy in enumerate(loads[number]):
                if (chosen is None or i == chosen) and (number, i) not in started:
                    started.add((number, i))
                    copy.start()
        io = Io(sources, loads, stores)
        kernel(io, *views, *refs[inputs + results : inputs + results + len(scratch)])
        io.finish()

    anywhere = pl.BlockSpec(memory_space=pl.ANY)
    scalar_spec = pl.BlockSpec(memory_space=pltpu.SMEM)
    params = {}
    if collective is not None:
        params = dict(collective_id=collective, has_side_effects=True)
    return pl.pallas_call(
        body,
        out_shape=tuple(jax.ShapeDtypeStruct(*out) for out in outs),
        in_specs=[scalar_spec if n == scalars else anywhere for n in range(inputs)],
        out_specs=tuple([anywhere] * results),
        scratch_shapes=list(scratch) + buffers + sems,
        compiler_params=pltpu.CompilerParams(vmem_limit_bytes=VMEM_LIMIT, **params),
        name=name,
    )(*arrays)


def ring_position(index, count):
    odd = index % 2
    return (1 - odd) * (index // 2) + odd * (count - 1 - index // 2)


def ring_member(position, count):
    late = position // (count // 2)
    return (1 - late) * 2 * position + late * (2 * (count - 1 - position) + 1)


def chan_peers():
    me = lax.axis_index("chan")
    mate = me + 1 - 2 * (me % 2)
    across = (me + 2) % 4
    return me, mate, across, (mate + 2) % 4


def greet(peers, members=()):
    barrier = pltpu.get_barrier_semaphore()
    for peer in peers:
        pl.semaphore_signal(barrier, inc=1, device_id={"chan": peer})
    for member in members:
        pl.semaphore_signal(barrier, inc=1, device_id={"dp": member})
    pl.semaphore_wait(barrier, len(peers) + len(members))


def send_to(peer, source, target, send, recv):
    return pltpu.make_async_remote_copy(source, target, send, recv, device_id={"chan": peer})


def span(index, size, unit=None):
    if isinstance(index, int):
        return pl.ds(index * size, size)
    return pl.ds(pl.multiple_of(index * size, unit or size), size)


def gather_copy(place, peers, sems, kind, part):
    me, mate, across, _ = peers
    block = place(across if kind == 2 else me, part)
    send, recv = sems
    return send_to(
        across if kind == 0 else mate, block, block, send.at[kind, part], recv.at[kind, part]
    )


def norm_columns(values):
    mean = jnp.mean(values, axis=0, keepdims=True)
    center = values - mean
    inverse = lax.rsqrt(jnp.mean(center * center, axis=0, keepdims=True) + EPSILON)
    return center * inverse, inverse


def norm_pullback(grad, values, gain):
    normal, inverse = norm_columns(values)
    product = grad * normal
    scaled = grad * gain
    first = jnp.mean(scaled, axis=0, keepdims=True)
    second = jnp.mean(product * gain, axis=0, keepdims=True)
    return inverse * (scaled - first - normal * second), product


def lane_sums(values):
    return jnp.sum(values, axis=1, keepdims=True)


def matmul(left, right):
    return jnp.dot(left, right, preferred_element_type=F32)


def matmul_nt(left, right):
    return lax.dot_general(
        left, right, (((1,), (1,)), ((), ())), preferred_element_type=F32
    )


def transpose_into(target, source, tile):
    for n in range(source.shape[0] // tile):
        target[:, n * tile : (n + 1) * tile] = source[n * tile : (n + 1) * tile].T


def transpose_columns(target, source, tile):
    for n in range(source.shape[1] // tile):
        target[n * tile : (n + 1) * tile, :] = source[:, n * tile : (n + 1) * tile].T


def exchange(peers, source, target, send, recv):
    copies = []
    for n, peer in enumerate((peers[2], peers[3], peers[1])):
        copy = send_to(peer, source(peer), target(), send.at[n], recv.at[n])
        copy.start()
        copies.append(copy)
    return copies


def to_channels(peers, low, landing, send, recv):
    shard, tokens = landing.shape[0], low.shape[1]
    me = peers[0]
    mine = span(me, tokens)
    copies = exchange(
        peers, lambda peer: low.at[span(peer, shard, 32), :], lambda: landing.at[:, mine], send, recv
    )
    return copies


def to_tokens(peers, low, landing, send, recv):
    shard, half = low.shape[0], landing.shape[1] // 2
    mine = span(peers[0], shard, 32)
    copies = [
        exchange(
            peers, lambda peer: low.at[:, span(peer * 2 + part, half)],
            lambda: landing.at[mine, pl.ds(part * half, half)], send.at[part], recv.at[part],
        )
        for part in range(2)
    ]
    landing[mine, :] = low[:, span(peers[0], 2 * half)]
    return copies


class Track:
    def __init__(self, own, first, last, carry=None):
        self.own, self.first, self.last, self.carry = own, first, last, carry
        self.count, self.rows, self.lanes = own.shape

    def out(self):
        if self.last == self.count - 1:
            return ((self.rows, self.lanes), F32)
        return ((2, self.rows, self.lanes // 2), BF16)


def ring_operands(tracks):
    return [one.own for one in tracks] + [one.carry for one in tracks if one.first]


def ring_scratch(tracks):
    slots = [
        pltpu.VMEM((one.last - one.first, 2, one.rows, one.lanes // 2), BF16) for one in tracks
    ]
    if not tracks:
        return []
    longest = max(one.last - one.first for one in tracks)
    return slots + [pltpu.SemaphoreType.DMA((longest, len(tracks), 2))] * 2


class Ring:
    def __init__(self, tracks, operands, outs, scratch, sources):
        self.tracks, self.outs = tracks, outs
        self.count = tracks[0].count
        self.owns = operands[: len(tracks)]
        self.sources = sources[: len(tracks)]
        carries = list(sources[len(tracks) :])
        self.carries = [carries.pop(0) if one.first else None for one in tracks]
        *self.slots, self.send, self.recv = scratch
        self.here = lax.axis_index("dp")
        self.place = ring_position(self.here, self.count)
        after = ring_member((self.place + 1) % self.count, self.count)
        before = ring_member((self.place + self.count - 1) % self.count, self.count)
        self.toward = (after, before)
        self.rounds = max(one.last - one.first for one in tracks) - 1

    def copy(self, track, direction, turn, source):
        return pltpu.make_async_remote_copy(
            source,
            self.slots[track].at[turn, direction],
            self.send.at[turn, track, direction],
            self.recv.at[turn, track, direction],
            device_id={"dp": self.toward[direction]},
        )

    def owner(self, direction, step):
        move = step + 1
        if direction == 0:
            move = self.count - move
        return ring_member((self.place + move) % self.count, self.count)

    def own(self, track, direction, owner, owns=None):
        own = (owns or self.owns)[track]
        half = own.shape[2] // 2
        return own.at[owner, :, pl.ds(direction * half, half)]

    def held(self, track, direction, turn):
        return self.slots[track].at[turn, direction]

    def start(self):
        for track, carry in enumerate(self.carries):
            for direction in range(2):
                if carry is None:
                    source = self.own(track, direction, self.owner(direction, 0), self.sources)
                else:
                    source = carry.at[direction]
                self.copy(track, direction, 0, source).start()

    def round(self, turn, extra):
        for track, info in enumerate(self.tracks):
            def one(track=track, info=info):
                for direction in range(2):
                    held = self.held(track, direction, turn - 1)
                    self.copy(track, direction, turn - 1, held).wait_recv()
                    own = self.own(track, direction, self.owner(direction, info.first + turn))
                    held[...] = (held[...].astype(F32) + own[...].astype(F32)).astype(BF16)
                    self.copy(track, direction, turn, held).start()

            if info.last - info.first - 1 == self.rounds:
                one()
            else:
                pl.when(turn < info.last - info.first)(one)
        return extra

    def advance(self, point, points):
        first, last = self.rounds * point // points, self.rounds * (point + 1) // points
        if isinstance(point, int) and last == first:
            return
        if isinstance(point, int) and last == first + 1:
            self.round(last, 0)
            return
        lax.fori_loop(1 + first, 1 + last, self.round, 0)

    def loop(self, body, steps, point, pieces, points):
        for n in range(pieces):
            lax.fori_loop(steps * n // pieces, steps * (n + 1) // pieces, body, 0)
            self.advance(point + n, points)

    def finish(self):
        for track, (info, out) in enumerate(zip(self.tracks, self.outs)):
            turns = info.last - info.first
            half = info.lanes // 2
            whole = info.last == self.count - 1
            for direction in range(2):
                held = self.held(track, direction, turns - 1)
                self.copy(track, direction, turns - 1, held).wait_recv()
                owner = self.here if whole else self.owner(direction, info.last)
                own = self.own(track, direction, owner)
                total = held[...].astype(F32) + own[...].astype(F32)
                if whole:
                    out[:, pl.ds(direction * half, half)] = total
                else:
                    out[direction] = total.astype(BF16)

        def settle(turn, extra):
            for track, info in enumerate(self.tracks):
                def one(track=track):
                    for direction in range(2):
                        held = self.held(track, direction, turn)
                        self.copy(track, direction, turn, held).wait_send()

                if info.last - info.first == self.rounds + 1:
                    one()
                else:
                    pl.when(turn < info.last - info.first)(one)
            return extra

        lax.fori_loop(0, self.rounds + 1, settle, 0)


def ring_rows(rows):
    return -(-rows // 16) * 16


def split_rows(target, source, unit, joined):
    rows, kinds, lanes = source.shape

    def one(n, carry):
        here = span(n, unit)
        for kind in range(kinds):
            values = source[here, kind, :]
            if joined:
                target[here, kind * lanes : (kind + 1) * lanes] = values
            else:
                target[pl.ds(pl.multiple_of(kind * rows + n * unit, unit), unit), :] = values
        return carry

    return one


def first_project_kernel(
    io, inputs_ref, mix_gain, mix_bias, glu_gain, glu_bias, weight_in, short_in, cond_in, up_in,
    seq_ref, x_ref, gains_ref, full, project_ref, weight_ref, up_ref, columns_ref, keep_ref,
    raw, gains_low, gains_land, turn, send, recv, gains_send, gains_recv,
):
    peers = chan_peers()
    me = peers[0]
    shard, slots = inputs_ref.shape
    parts, width, half = raw.shape
    layers = mix_gain.shape[0]
    greet(peers[1:])
    io.ready(0, 1, 2, 3, 4)

    def gather(kind, part):
        return gather_copy(
            lambda owner, part: raw.at[part, span(owner, shard, 32), :],
            peers, (send, recv), kind, part,
        )

    for layer in range(layers):
        for kind, one in enumerate((mix_gain, mix_bias, glu_gain, glu_bias)):
            row = 4 * layer + kind
            gains_low[row : row + 1, :] = one[layer : layer + 1, :]
    gains_land[me] = gains_low[...]
    copies = exchange(
        peers, lambda peer: gains_low, lambda: gains_land.at[me], gains_send, gains_recv
    )
    for part in range(parts):
        raw[part, span(me, shard, 32), :] = inputs_ref[:, part * half : (part + 1) * half]
        for kind in range(2):
            gather(kind, part).start()
    io.ready(5, 6, 7)
    for layer in range(layers):
        lax.fori_loop(0, shard // 48, split_rows(weight_ref.at[layer], weight_in.at[layer], 48, False), 0)
        turn[...] = jnp.zeros_like(turn)
        for tap in range(3):
            turn[3 * tap : 3 * tap + 3, :shard] = short_in[layer, tap]
        turn[9:10, :shard] = cond_in[layer : layer + 1, :]
        columns_ref[layer] = turn[...].T[:shard]
    slot = lax.broadcasted_iota(jnp.int32, keep_ref.shape, 1)
    row = lax.broadcasted_iota(jnp.int32, keep_ref.shape, 0)
    within = slot & (seq_ref[0, 0] - 1)
    keep_ref[...] = jnp.where(within > row, 1.0, 0.0)
    io.flush(4)
    io.flush(6)
    io.flush(7)
    for copy in copies:
        copy.wait()
    turn[...] = jnp.zeros_like(turn)
    for owner in range(4):
        turn[: 4 * layers, :shard] = gains_land[owner]
        gains_ref[owner * shard : (owner + 1) * shard, :] = turn[...].T[:shard]
    io.flush(1)
    io.ready(8)
    gather(0, 0).wait_recv()
    gather(2, 0).start()
    for part in range(parts):
        if part + 1 < parts:
            gather(0, part + 1).wait_recv()
            gather(2, part + 1).start()
        gather(1, part).wait_recv()
        gather(2, part).wait_recv()
        values = raw[part].astype(F32)

        @pl.when(me == part // 2)
        def _():
            x_ref[:, (part % 2) * half : (part % 2 + 1) * half] = values

        normal, _ = norm_columns(values)
        full[part] = (normal * gains_ref[:, 0:1] + gains_ref[:, 1:2]).astype(BF16)
        io.flush(2, part, part)
        columns = slice(part * half, (part + 1) * half)
        project_ref[:, columns] = matmul(weight_ref[0], full[part])
        io.flush(3, part, (slice(None), pl.ds(part * half, half)))
        cuts = width // 64
        lax.fori_loop(
            cuts * part // parts, cuts * (part + 1) // parts, split_rows(up_ref, up_in, 64, True), 0
        )
    io.flush(0)
    io.flush(5)
    for part in range(parts):
        for kind in range(3):
            gather(kind, part).wait_send()


def first_project(inputs, gain_arrays, in_proj, short_conv, cond_weight, glu_in, seq_table,
                  collective):
    shard, slots = inputs.shape
    layers, _, streams, width = in_proj.shape
    hidden = glu_in[0].shape[3]
    tokens = slots // 4
    return fused_call(
        first_project_kernel,
        [inputs, *gain_arrays, in_proj, short_conv, cond_weight, glu_in, seq_table],
        [
            ((width, tokens), F32),
            ((width, 128), F32),
            ((8, width, tokens // 2), BF16),
            ((streams * shard, slots), F32),
            ((layers, streams * shard, width), BF16),
            ((width, 2 * hidden), BF16),
            ((layers, shard, 128), F32),
            ((8, slots), F32),
        ],
        [
            pltpu.VMEM((8, width, tokens // 2), BF16),
            pltpu.VMEM((4 * layers, shard), F32),
            pltpu.VMEM((4, 4 * layers, shard), F32),
            pltpu.VMEM((128, 256), F32),
        ]
        + [pltpu.SemaphoreType.DMA((3, 8))] * 2
        + [pltpu.SemaphoreType.DMA((3,))] * 2,
        collective,
        "first_project",
        (1, 1, 8, 8, 1, 1, 1, 1),
        9,
    )


def scatter_copy(peers, buffers, sems, kind, part):
    _, mate, across, _ = peers
    send, recv = sems
    return send_to(
        across if kind == 2 else mate,
        buffers[2 * kind].at[part],
        buffers[2 * kind + 1].at[part],
        send.at[kind, part],
        recv.at[kind, part],
    )


def scatter_buffers(width, half):
    return [pltpu.VMEM((2, width, half), BF16)] * 6


def block_place(full):
    return lambda owner, part: full.at[owner * 2 + part]


def block_at(step, peers, gathers):
    me, mate, across, diag = peers
    if gathers:
        mine = 1 - (step + 6) // 8
        kind = (step + 1) % 3
        part = mine * step + (1 - mine) * ((step - 2) // 3)
        kind = kind - mine * 4
    else:
        near = step // 4
        mine = step // 6
        part = (1 - near) * (step // 2) + near * (step % 2)
        kind = (1 - near) * (1 + step % 2) - mine
    far = kind * (2 - kind) * (across - mate) + kind * (kind - 1) // 2 * (diag - mate)
    return kind, part, ((1 - mine) * (mate + far) + mine * me) * 2 + part, mine


def run_blocks(peers, full, gather_sems, scatter_sems, buffers, partial, kept, own, ring=None):
    me, mate, across, diag = peers
    gathers = gather_sems is not None

    def gather(kind, part):
        return gather_copy(block_place(full), peers, gather_sems, kind, part)

    def step_body(step, carry):
        kind, part, block, mine = block_at(step, peers, gathers)

        if gathers:
            @pl.when(kind == 0)
            def _():
                gather(1, part).wait_recv()

            @pl.when(kind == 1)
            def _():
                gather(0, part).wait_recv()
                gather(2, part).start()

            @pl.when(kind == 2)
            def _():
                gather(2, part).wait_recv()

        share = partial(block, step)

        def scatter(kind):
            return scatter_copy(peers, buffers, scatter_sems, kind, part)

        @pl.when(mine == 1)
        def _():
            own[part] = share

        @pl.when(kind == 0)
        def _():
            buffers[2][part] = share.astype(BF16)
            scatter(1).start()

        @pl.when(kind == 1)
        def _():
            kept[...] = share

        @pl.when(kind == 2)
        def _():
            buffers[0][part] = share.astype(BF16)
            scatter(0).start()
            scatter(0).wait_recv()
            buffers[4][part] = (kept[...] + buffers[1][part].astype(F32)).astype(BF16)
            scatter(2).start()

        if ring is not None:
            ring.advance(step, 8)
        return carry

    lax.fori_loop(0, 8, step_body, 0)


def scattered(peers, scatter_sems, buffers, own, part):
    for kind in (1, 2):
        scatter_copy(peers, buffers, scatter_sems, kind, part).wait_recv()
    return own[part] + buffers[3][part].astype(F32) + buffers[5][part].astype(F32)


def drain_gather(peers, full, gather_sems):
    for part in range(2):
        for kind in range(3):
            gather_copy(block_place(full), peers, gather_sems, kind, part).wait_send()


def drain_scatter(peers, scatter_sems, buffers):
    for part in range(2):
        for kind in range(3):
            scatter_copy(peers, buffers, scatter_sems, kind, part).wait_send()


def feed_kernel(gain_at, follows, io, gated_ref, x_ref, gains_ref, out_weight, up_columns,
                down_weight, *refs):
    refs = list(refs)
    weight_ref, up_in = (refs.pop(0), refs.pop(0)) if follows else (None, None)
    token_gated, mid_ref, full, next_ref, units, gelus, slopes = refs[:7]
    refs = refs[7:]
    if follows:
        next_full, project_ref, next_up = refs[:3]
        *refs, next_send, next_recv = refs[3:]
    up_weight, kept, own, *rest = refs
    buffers, sems = rest[:6], rest[6:]
    send, recv, gather_send, gather_recv, scatter_send, scatter_recv = sems
    gather_sems, scatter_sems = (gather_send, gather_recv), (scatter_send, scatter_recv)
    peers = chan_peers()
    me = peers[0]
    width, tokens = x_ref.shape
    half = tokens // 2
    hidden = down_weight.shape[1]
    greet(peers[1:])
    io.ready(0)
    copies = to_tokens(peers, gated_ref, token_gated, send, recv)
    io.ready(1, 2, 3, 4, 5)
    transpose_columns(up_weight, up_columns, 256)
    for part in range(2):
        for copy in copies[part]:
            copy.wait()
        columns = slice(part * half, (part + 1) * half)
        mid = x_ref[:, columns] + matmul(out_weight[...], token_gated[:, columns])
        mid_ref[:, columns] = mid
        normal, _ = norm_columns(mid)
        gain = gains_ref[:, gain_at : gain_at + 1]
        bias = gains_ref[:, gain_at + 1 : gain_at + 2]
        full[me * 2 + part] = (normal * gain + bias).astype(BF16)
        for kind in range(2):
            gather_copy(block_place(full), peers, gather_sems, kind, part).start()
    io.flush(0)
    io.flush(1)

    def partial(block, step):
        normed = full[block]
        tile = 256
        for n in range(hidden // tile):
            gate = matmul(up_weight[n * tile : (n + 1) * tile], normed)
            up = matmul(up_weight[hidden + n * tile : hidden + (n + 1) * tile], normed)
            rows = slice(n * tile, (n + 1) * tile)
            cdf = 0.5 * (1.0 + lax.erf(gate * math.sqrt(0.5)))
            density = jnp.exp(-0.5 * gate * gate) * (1.0 / math.sqrt(2.0 * math.pi))
            gelu = gate * cdf
            units[block, rows] = (gelu * up).astype(BF16)
            gelus[block, rows] = gelu.astype(BF16)
            slopes[block, rows] = (up * (cdf + gate * density)).astype(BF16)
        return matmul(down_weight[...], units[block])

    run_blocks(peers, full, gather_sems, scatter_sems, buffers, partial, kept, own)
    for number in (2, 4, 5, 6):
        io.flush(number)
    if follows:
        io.ready(6, 7)
    place = block_place(next_full) if follows else None
    for part in range(2):
        if follows:
            cuts = width // 64
            lax.fori_loop(
                cuts * part // 2, cuts * (part + 1) // 2, split_rows(next_up, up_in, 64, True), 0
            )
        columns = slice(part * half, (part + 1) * half)
        value = mid_ref[:, columns] + scattered(peers, scatter_sems, buffers, own, part)
        next_ref[:, columns] = value.astype(next_ref.dtype)
        if follows:
            normal, _ = norm_columns(value)
            gain = gains_ref[:, gain_at + 2 : gain_at + 3]
            bias = gains_ref[:, gain_at + 3 : gain_at + 4]
            next_full[me * 2 + part] = (normal * gain + bias).astype(BF16)
            for kind in range(2):
                gather_copy(place, peers, (next_send, next_recv), kind, part).start()
    io.flush(3)
    if follows:
        io.flush(9)
    drain_gather(peers, full, gather_sems)
    drain_scatter(peers, scatter_sems, buffers)
    if follows:
        project_blocks(io, peers, next_full, (next_send, next_recv), weight_ref, project_ref, 7, 8)


def project_blocks(io, peers, full, sems, weight_ref, project_ref, full_out, project_out):
    me, mate, across, diag = peers
    half = full.shape[2]

    def gather(kind, part):
        return gather_copy(block_place(full), peers, sems, kind, part)

    order = [(me, 0), (me, 1), (mate, 0), (mate, 1)]
    order += [(across, 0), (diag, 0), (across, 1), (diag, 1)]
    for step, (owner, part) in enumerate(order):
        if 2 <= step < 4:
            gather(1, part).wait_recv()
        elif step >= 4 and step % 2 == 0:
            gather(0, part).wait_recv()
            gather(2, part).start()
        elif step >= 4:
            gather(2, part).wait_recv()
        block = owner * 2 + part
        io.flush(full_out, step, block)
        columns = span(block, half)
        project_ref[:, columns] = matmul(weight_ref[...], full[block])
        io.flush(project_out, step, (slice(None), columns))
    for kind in range(3):
        for part in range(2):
            gather(kind, part).wait_send()


def feed_forward(gated, values, gains, out_weight, up_columns, down_weight, following, gain_at,
                 collective):
    width, tokens = values.shape
    half = tokens // 2
    follows = list(following)
    block = ((8, width, half), BF16)
    outs = [((width, tokens), BF16), ((width, tokens), F32), block]
    outs.append(((width, tokens), F32 if follows else BF16))
    hidden = down_weight[0].shape[2]
    outs += [((8, hidden, half), BF16)] * 3
    parts = [1] * 7
    extra = []
    if follows:
        outs += [block, ((follows[0][0].shape[1], 4 * tokens), F32)]
        outs.append(((width, 2 * hidden), BF16))
        parts += [8, 8, 1]
        extra = [pltpu.SemaphoreType.DMA((3, 2))] * 2
    return fused_call(
        lambda *refs: feed_kernel(gain_at, bool(follows), *refs),
        [gated, values, gains, out_weight, up_columns, down_weight] + follows,
        outs,
        [
            pltpu.VMEM((2 * hidden, width), BF16),
            pltpu.VMEM((width, half), F32),
            pltpu.VMEM((2, width, half), F32),
        ]
        + scatter_buffers(width, half)
        + [pltpu.SemaphoreType.DMA((2, 3))] * 2
        + [pltpu.SemaphoreType.DMA((3, 2))] * 4
        + extra,
        collective,
        "feed_forward",
        parts,
    )


def weight_grad(store, rows, columns, left, right, blocks, row_tile, column_tile):
    across = columns // column_tile

    def one(n, carry):
        row, column = span(n // across, row_tile), span(n % across, column_tile)
        total = matmul_nt(left(0, row), right(0, column))
        for block in range(1, blocks):
            total = total + matmul_nt(left(block, row), right(block, column))
        store(n // across, column, total)
        return carry

    lax.fori_loop(0, rows // row_tile * across, one, 0)


def feed_back_kernel(gain_at, gathered, tracks, io, grad_ref, down_weight, gelus, slopes, up_columns,
                     out_weight, mid_ref, gains_ref, token_gated, units, normed, *refs):
    refs = list(refs)
    rings = len(tracks)
    inputs = len(ring_operands(tracks))
    ring_in, refs = refs[:inputs], refs[inputs:]
    state_ref, gated_ref, feed_grads, out_grad, sums_ref = refs[:5]
    large, refs = refs[5 : 5 + rings], refs[5 + rings :]
    ring = None
    if rings:
        sources = [io.source[11 + n] for n in range(inputs)]
        ring = Ring(tracks, ring_in, large, refs[-rings - 2 :], sources)
        refs = refs[: -rings - 2]
    full = grad_ref if gathered else refs.pop(0)
    gates, mixer_low, kept, own, turned, *rest, load_sems = refs
    gated_low = full
    buffers, sems = rest[:6], rest[6:]
    send, recv, gather_send, gather_recv, scatter_send, scatter_recv = sems
    gather_sems, scatter_sems = (gather_send, gather_recv), (scatter_send, scatter_recv)
    if gathered:
        gather_sems = None
    peers = chan_peers()
    me, mate, across, diag = peers
    width, tokens = mid_ref.shape
    half = tokens // 2
    shard = gated_ref.shape[0]
    hidden = down_weight.shape[1]
    tile = 256
    saved = ((io.source[2], gelus), (io.source[3], slopes))
    if gathered:
        saved += ((io.source[0], full),)

    def loads(step, block):
        return [
            pltpu.make_async_copy(source.at[block], target.at[block], load_sems.at[n, step])
            for n, (source, target) in enumerate(saved)
        ]

    for step in range(8):
        for copy in loads(step, block_at(step, peers, not gathered)[2]):
            copy.start()
    greet(peers[1:], ring.toward if rings else ())
    if not gathered:
        io.ready(0)
        for part in range(2):
            full[me * 2 + part] = grad_ref[:, part * half : (part + 1) * half].astype(BF16)
            for kind in range(2):
                gather_copy(block_place(full), peers, gather_sems, kind, part).start()
    if rings:
        ring.start()
    io.ready(1)
    down_rows, out_rows = turned.at[:hidden], turned.at[:width]
    transpose_into(down_rows, down_weight, tile)
    io.ready(4)
    if rings:
        io.ready(*range(11, 11 + rings))

    def partial(block, step):
        for copy in loads(step, block):
            copy.wait()
        grad = full[block]
        for n in range(hidden // tile):
            rows = slice(n * tile, (n + 1) * tile)
            later = slice(hidden + n * tile, hidden + (n + 1) * tile)
            unit_grad = matmul(down_rows[rows], grad)
            gates[block, rows] = (unit_grad * slopes[block, rows].astype(F32)).astype(BF16)
            gates[block, later] = (unit_grad * gelus[block, rows].astype(F32)).astype(BF16)
        return matmul(up_columns[...], gates[block])

    run_blocks(peers, full, gather_sems, scatter_sems, buffers, partial, kept, own, ring)
    io.ready(5, 6, 7, 8, 9, 10)
    transpose_into(out_rows, out_weight, tile)
    if not gathered:
        drain_gather(peers, full, gather_sems)

    def a2a(part, n):
        peer = (across, diag, mate)[n]
        return send_to(
            peer,
            gated_low.at[part, span(peer, shard, 32), :],
            gated_ref.at[:, span(me * 2 + part, half)],
            send.at[part, n],
            recv.at[part, n],
        )

    chunk_rows = feed_grads.shape[1] // 3
    row_tile = 384

    def store_grad(kind):
        def store(index, column, total):
            chunks = row_tile // chunk_rows
            for n in range(chunks):
                feed_grads[
                    index * chunks + n, kind * chunk_rows : (kind + 1) * chunk_rows, column
                ] = total[n * chunk_rows : (n + 1) * chunk_rows].astype(BF16)

        return store

    def store_out(index, column, total):
        out_grad[span(index, tile), column] = total.astype(BF16)

    gain = gains_ref[:, gain_at : gain_at + 1]
    for part in range(2):
        for kind in (0,) if part == 0 else (1, 2):
            if kind == 0:
                left, right = lambda b, r: full[b, r], lambda b, c: units[b, c]
            else:
                first = (kind - 1) * hidden
                left = lambda b, r: normed[b, r]
                right = lambda b, c, first=first: gates[
                    b, pl.ds(pl.multiple_of(c.start + first, tile), tile)
                ]
            weight_grad(store_grad(kind), width, hidden, left, right, 8, row_tile, tile)
        columns = slice(part * half, (part + 1) * half)
        grad = scattered(peers, scatter_sems, buffers, own, part)
        change, product = norm_pullback(grad, mid_ref[:, columns], gain)
        before = full[me * 2 + part].astype(F32) if gathered else grad_ref[:, columns]
        state = before + change
        state_ref[:, columns] = state
        mixer_low[:, columns] = state.astype(BF16)
        gated_low[part] = matmul(out_rows[...], mixer_low[:, columns]).astype(BF16)
        for n in range(3):
            a2a(part, n).start()
        if part == 0:
            sums_ref[:, 0:1] = lane_sums(product)
            sums_ref[:, 1:2] = lane_sums(grad)
        else:
            sums_ref[:, 0:1] = sums_ref[:, 0:1] + lane_sums(product)
            sums_ref[:, 1:2] = sums_ref[:, 1:2] + lane_sums(grad)
    io.flush(0)
    io.flush(2)
    io.flush(4)
    for part in range(2):
        gated_ref[:, span(me * 2 + part, half)] = gated_low[part, span(me, shard, 32), :]
    weight_grad(
        store_out, width, width,
        lambda b, r: mixer_low[r, :], lambda b, c: token_gated[c, :], 1, tile, tile,
    )
    io.flush(3)
    if rings:
        ring.finish()
        for n in range(rings):
            io.flush(5 + n)
    for part in range(2):
        for n in range(3):
            a2a(part, n).wait()
    io.flush(1)
    drain_scatter(peers, scatter_sems, buffers)


def feed_back(grad, mid, gains, normed, up_columns, down_weight, out_weight, token_gated, saved,
              tracks, gain_at, count, collective):
    width, tokens = mid.shape
    half = tokens // 2
    hidden = down_weight[0].shape[2]
    gathered = grad.ndim == 3
    units, gelus, slopes = saved
    own_loads = tuple(range(11, 11 + len(tracks)))
    carries = tuple(range(11 + len(tracks), 11 + len(ring_operands(tracks))))
    manual = (2, 3) + ((0,) if gathered else ()) + carries
    return fused_call(
        lambda *refs: feed_back_kernel(gain_at, gathered, tracks, *refs),
        [grad, down_weight, gelus, slopes, up_columns, out_weight, mid, gains, token_gated, units]
        + [normed]
        + ring_operands(tracks),
        [
            ((width, tokens), F32),
            ((width // 4, 4 * tokens), BF16),
            ((count, 3 * width // count, hidden), BF16),
            ((width, width), BF16),
            ((width, 8), F32),
        ]
        + [one.out() for one in tracks],
        [pltpu.VMEM((8, width, half), BF16)] * (not gathered)
        + [
            pltpu.VMEM((8, 2 * hidden, half), BF16),
            pltpu.VMEM((width, tokens), BF16),
            pltpu.VMEM((width, half), F32),
            pltpu.VMEM((2, width, half), F32),
            pltpu.VMEM((max(hidden, width), width), BF16),
        ]
        + scatter_buffers(width, half)
        + [pltpu.SemaphoreType.DMA((2, 3))] * 2
        + [pltpu.SemaphoreType.DMA((3, 2))] * 4
        + [pltpu.SemaphoreType.DMA((3, 8))]
        + ring_scratch(tracks),
        collective,
        "feed_back",
        [1] * (5 + len(tracks)),
        manual=manual,
        order=((0,) if not gathered else ()) + (1, 4) + own_loads,
    )


def project_back_kernel(gain_at, each, tracks, io, project_grad, weight_ref, square_ref, normed,
                        state_ref, x_ref, gains_ref, *refs):
    inputs = len(ring_operands(tracks))
    ring_in, refs = refs[:inputs], refs[inputs:]
    next_ref, in_grad, sums_ref = refs[:3]
    large, refs = refs[3 : 3 + len(tracks)], refs[3 + len(tracks) :]
    kept, own, weight_rows, in_full, *rest = refs
    buffers, (scatter_send, scatter_recv, *ring_rest) = rest[:6], rest[6:]
    scatter_sems = (scatter_send, scatter_recv)
    peers = chan_peers()
    me, mate, across, diag = peers
    sources = [io.source[7 + n] for n in range(inputs)]
    ring = Ring(tracks, ring_in, large, ring_rest, sources)
    width, tokens = x_ref.shape
    half = tokens // 2
    rows = weight_ref.shape[0]
    shard = rows // 3
    greet((mate, across), ring.toward)
    ring.start()
    io.ready(1)
    for first, size in ((0, 512), (512, rows - 512)):
        weight_rows[:, first : first + size] = weight_ref[first : first + size].T
    io.ready(0)

    def share(owner, part):
        return matmul(weight_rows[...], project_grad[:, span(owner * 2 + part, half)])

    for part in range(2):
        buffers[0][part] = share(diag, part).astype(BF16)
        scatter_copy(peers, buffers, scatter_sems, 0, part).start()
        kept[...] = share(across, part)
        scatter_copy(peers, buffers, scatter_sems, 0, part).wait_recv()
        buffers[4][part] = (kept[...] + buffers[1][part].astype(F32)).astype(BF16)
        scatter_copy(peers, buffers, scatter_sems, 2, part).start()
    for part in range(2):
        buffers[2][part] = share(mate, part).astype(BF16)
        scatter_copy(peers, buffers, scatter_sems, 1, part).start()
        own[part] = share(me, part)
    io.ready(*range(7, 7 + len(tracks)))
    ring.advance(0, 3)
    io.ready(2, 3)
    if in_full.shape[1] > 4 * each:
        in_full[...] = jnp.zeros_like(in_full)
    for chunk in range(shard // each):
        in_full[chunk, 3 * each : 4 * each] = square_ref[chunk * each : (chunk + 1) * each]
    tile = 256
    for stream in range(3):
        def column_tile(n, carry):
            column = span(n, tile)
            total = None
            for block in range(8):
                left = project_grad[
                    stream * shard : (stream + 1) * shard, block * half : (block + 1) * half
                ]
                value = matmul_nt(left, normed[block, column])
                total = value if total is None else total + value
            for chunk in range(shard // each):
                in_full[chunk, stream * each : (stream + 1) * each, column] = total[
                    chunk * each : (chunk + 1) * each
                ]
            return carry

        lax.fori_loop(0, width // tile, column_tile, 0)
    ring.advance(1, 3)
    in_grad[...] = in_full[...].astype(BF16)
    io.flush(1)
    io.ready(4, 5, 6)
    gain = gains_ref[:, gain_at : gain_at + 1]
    for part in range(2):
        columns = slice(part * half, (part + 1) * half)
        grad = scattered(peers, scatter_sems, buffers, own, part)
        change, product = norm_pullback(grad, x_ref[:, columns], gain)
        next_ref[:, columns] = state_ref[:, columns] + change
        if part == 0:
            sums_ref[:, 0:1] = lane_sums(product)
            sums_ref[:, 1:2] = lane_sums(grad)
            ring.advance(2, 3)
        else:
            sums_ref[:, 0:1] = sums_ref[:, 0:1] + lane_sums(product)
            sums_ref[:, 1:2] = sums_ref[:, 1:2] + lane_sums(grad)
    io.flush(0)
    io.flush(2)
    ring.finish()
    for n in range(len(tracks)):
        io.flush(3 + n)
    drain_scatter(peers, scatter_sems, buffers)


def project_back(project_grad, state, values, gains, normed, weight, square, tracks, gain_at,
                 collective):
    width, tokens = values.shape
    half = tokens // 2
    rows = project_grad.shape[0]
    count = tracks[0].count
    each = rows // 3 // count
    packed = (count, ring_rows(4 * each), width)
    return fused_call(
        lambda *refs: project_back_kernel(gain_at, each, tracks, *refs),
        [project_grad, weight, square, normed, state, values, gains] + ring_operands(tracks),
        [((width, tokens), F32), (packed, BF16), ((width, 8), F32)]
        + [one.out() for one in tracks],
        [
            pltpu.VMEM((width, half), F32),
            pltpu.VMEM((2, width, half), F32),
            pltpu.VMEM((width, rows), BF16),
            pltpu.VMEM(packed, F32),
        ]
        + scatter_buffers(width, half)
        + [pltpu.SemaphoreType.DMA((3, 2))] * 2
        + ring_scratch(tracks),
        collective,
        "project_back",
        [1] * (3 + len(tracks)),
        manual=tuple(range(7 + len(tracks), 7 + len(ring_operands(tracks)))),
        order=(1, 0) + tuple(range(7, 7 + len(tracks))),
    )


def mask_heads(values, keep, blocks):
    length = values.shape[1] // blocks
    pieces = []
    for j in range(blocks):
        start = j * length
        pieces.append(values[:, start : start + 128] * keep[:, start : start + 128])
        pieces.append(values[:, start + 128 : start + length])
    return jnp.concatenate(pieces, axis=1)


def eight(rows):
    return pl.ds(pl.multiple_of(rows, 8), 8)


def sixteen(rows):
    return pl.ds(pl.multiple_of(rows, 16), 16)


def stream_rows(project_ref, columns_ref, keep_ref, rows, shard, stream, blocks):
    values = project_ref[eight(stream * shard + rows), :]
    total = values * columns_ref[eight(rows), stream : stream + 1]
    for offset in (1, 2):
        moved = mask_heads(pltpu.roll(values, offset, 1), keep_ref[offset - 1 : offset, :], blocks)
        column = 3 * offset + stream
        total = total + moved * columns_ref[eight(rows), column : column + 1]
    return total


def sequence_factor(power, cond, facts, blocks):
    energy = []
    for i in range(blocks):
        total = 0.0
        for j in range(blocks):
            total = total + power[j] * facts.same[i][j]
        energy.append(total * facts.inverse)
    logs = [jnp.log(1.0 + value) for value in energy]
    factor = [
        (1.0 + cond * value) * facts.same[i][i] for i, value in enumerate(logs)
    ]
    return energy, logs, factor


def block_sums(values, blocks):
    length = values.shape[1] // blocks
    return [lane_sums(values[:, i * length : (i + 1) * length]) for i in range(blocks)]


def spread_blocks(columns, length):
    return jnp.concatenate(
        [jnp.broadcast_to(column, (column.shape[0], length)) for column in columns], axis=1
    )


def plain_bins(spectrum_ref, rows, shard, blocks):
    half = spectrum_ref.shape[1] // 2
    bins = []
    for k in range(blocks):
        here = spectrum_ref[eight(k * shard + rows), :]
        bins.append((here[:, :half], here[:, half:]))
    return bins


def filter_bins(spectrum_ref, sign, rows, shard, blocks):
    plain = plain_bins(spectrum_ref, rows, shard, blocks)
    bins = [plain[0]]
    for k in range(1, blocks):
        (real, imag), (before_real, before_imag) = plain[k], plain[k - 1]
        bins.append((real - sign * before_imag, imag + sign * before_real))
    return bins


def store_blocks(target, values, rows, shard, blocks):
    length = values.shape[1] // blocks
    for j in range(blocks):
        target[sixteen(j * shard + rows), :] = values[:, j * length : (j + 1) * length]


def join(halves):
    return jnp.concatenate(halves, axis=0).astype(BF16)


def channel_cuts(shard, streams):
    size = shard // LOADS
    return [(s * shard + n * size, size) for n in range(LOADS) for s in range(streams)]


def channel_order(numbers, streams=3):
    order = []
    for n in range(LOADS):
        for number in numbers:
            each = streams if number == 1 else 1
            order += [(number, n * each + i) for i in range(each)]
    return tuple(order)


def conv_forward_kernel(blocks, carries, io, filter_ref, project_ref, columns_ref, keep_ref,
                        sign_ref, table_ref, seq_ref, carried_in, back_ref, gated_ref, conv_ref, carried,
                        signal_low, filter_low, signal_bins, filter_spectrum, out_low, convolved,
                        factor_ref, *sems):
    shard, slots = gated_ref.shape
    length = slots // blocks
    scale = 1.0 / length
    steps = shard // 16
    peers = chan_peers()
    me = peers[0]
    parts = carried.shape[0]
    facts = Facts(seq_ref, blocks, length)
    greet(peers[1:])

    def gather(kind, part):
        return gather_copy(
            lambda owner, part: carried.at[part, span(owner, shard, 32), :],
            peers, sems, kind, part,
        )

    def forward(first, last):
        for part in range(parts * first // 8, parts * last // 8):
            gather(0, part).wait_recv()
            gather(2, part).start()

    io.ready(7)
    for part in range(parts):
        if carries == 1:
            carried[part, span(me, shard, 32), :] = carried_in[part]
        else:
            lanes = carried.shape[2]
            carried[part, span(me, shard, 32), :] = carried_in[:, part * lanes : (part + 1) * lanes]
        for kind in range(2):
            gather(kind, part).start()
    io.ready(2, 3, 4)

    def prepare(n, carry):
        rows = n * 16
        signals = []
        for part in range(2):
            here = rows + 8 * part
            one, two = (
                stream_rows(project_ref, columns_ref, keep_ref, here, shard, stream, blocks)
                for stream in (1, 2)
            )
            signals.append(one * two)
            cond = columns_ref[eight(here), 9:10]
            _, _, factor = sequence_factor(block_sums(two * two, blocks), cond, facts, blocks)
            for j in range(blocks):
                factor_ref[eight(here), j : j + 1] = factor[j]
        store_blocks(signal_low, join(signals), rows, shard, blocks)
        kernel = filter_ref[sixteen(rows), :].astype(BF16)
        store_blocks(filter_low, kernel, rows, shard, blocks)
        return carry

    for n in range(LOADS):
        io.ready(0, cuts=slice(n, n + 1))
        io.ready(1, cuts=slice(3 * n, 3 * n + 3))
        lax.fori_loop(steps * n // LOADS, steps * (n + 1) // LOADS, prepare, 0)
    io.ready(5)
    signal_bins[...] = matmul(signal_low[...], table_ref[...])
    forward(0, 2)
    filter_spectrum[...] = matmul(filter_low[...], table_ref[...])
    forward(2, 3)

    def combine(n, carry):
        rows = n * 16
        joined = [[] for _ in range(blocks)]
        for part in range(2):
            here = rows + 8 * part
            window = filter_bins(filter_spectrum, sign_ref[0:1, :], here, shard, blocks)
            signal = plain_bins(signal_bins, here, shard, blocks)
            for i in range(blocks):
                real = imag = None
                for j in range(i, -1, -1):
                    fr, fi = window[i - j]
                    sr, si = signal[j]
                    more_real, more_imag = fr * sr - fi * si, fr * si + fi * sr
                    if j == i:
                        real, imag = more_real, more_imag
                    else:
                        factor = facts.same[i][j]
                        real, imag = real + more_real * factor, imag + more_imag * factor
                joined[i].append(jnp.concatenate([real, imag], axis=1))
        for i in range(blocks):
            out_low[sixteen(i * shard + rows), :] = join(joined[i])
        return carry

    lax.fori_loop(0, steps, combine, 0)
    forward(3, 5)
    io.ready(8)
    convolved[...] = matmul(out_low[...], back_ref[...]) * scale
    forward(5, 6)

    def finish(n, carry):
        rows = n * 16
        gated = []
        for part in range(2):
            here = rows + 8 * part
            zero = stream_rows(project_ref, columns_ref, keep_ref, here, shard, 0, blocks)
            pieces = []
            for j in range(blocks):
                source = convolved[eight(j * shard + here), :]
                columns = slice(j * length, (j + 1) * length)
                conv_ref[eight(here), columns] = source
                pieces.append(zero[:, columns] * (source * factor_ref[eight(here), j : j + 1]))
            gated.append(jnp.concatenate(pieces, axis=1))
        gated_ref[sixteen(rows), :] = join(gated)
        return carry

    lax.fori_loop(0, steps // 2, finish, 0)
    forward(6, 7)
    top, rest = pl.ds(0, shard // 2), pl.ds(shard // 2, shard // 2)
    io.flush(0, 0, top)
    io.flush(1, 0, top)
    lax.fori_loop(steps // 2, steps, finish, 0)
    io.flush(0, 1, rest)
    io.flush(1, 1, rest)
    forward(7, 8)
    for part in range(parts):
        for kind in (1, 2):
            gather(kind, part).wait_recv()
        io.flush(2, part, part)
    for part in range(parts):
        for kind in range(3):
            gather(kind, part).wait_send()


def conv_forward(project, filter_rows, columns, keep, sign, table, seq_table, back, carried,
                 carries, blocks, collective):
    shard, slots = filter_rows[0].shape[1:]
    width = 4 * shard
    length = slots // blocks
    low = pltpu.VMEM((blocks * shard, length), BF16)
    bins = pltpu.VMEM((blocks * shard, 2 * length), F32)
    if carries == 1:
        out = ((carried.shape[0], width, width), BF16)
    else:
        out = ((8, width, slots // 8), BF16)
    return fused_call(
        lambda *refs: conv_forward_kernel(blocks, carries, *refs),
        [filter_rows, project, columns, keep, sign, table, seq_table, carried, back],
        [((shard, slots), BF16), ((shard, slots), F32), out],
        [
            low,
            low,
            bins,
            bins,
            pltpu.VMEM((blocks * shard, 2 * length), BF16),
            pltpu.VMEM((blocks * shard, length), F32),
            pltpu.VMEM((shard, 128), F32),
        ]
        + [pltpu.SemaphoreType.DMA((3, out[0][0]))] * 2,
        collective,
        "conv_forward",
        [2, 2, out[0][0]],
        6,
        (7, 2, 3, 4) + channel_order((1, 0)) + (5, 8),
        {0: channel_cuts(shard, 1), 1: channel_cuts(shard, 3)},
    )


def conv_backward_kernel(blocks, tracks, with_outputs, io, grad_ref, project_ref, conv_ref,
                         filter_ref, columns_ref, keep_ref, sign_ref, table_ref, seq_ref,
                         square_ref, *refs):
    refs = list(refs)
    back_ref = refs.pop(len(ring_operands(tracks)) + with_outputs)
    rings = len(tracks)
    inputs = len(ring_operands(tracks))
    ring_in, refs = refs[:inputs], refs[inputs:]
    if with_outputs:
        residual_ref = refs.pop(0)
    project_grad, filter_pack, square_sum, sums_ref = refs[:4]
    large, refs = refs[4 : 4 + rings], refs[4 + rings :]
    if with_outputs:
        outputs_ref = refs.pop(0)
        *refs, out_land, out_send, out_recv = refs
    sources = [io.source[10 + n] for n in range(inputs)]
    ring = Ring(tracks, ring_in, large, refs[-rings - 2 :], sources)
    refs = refs[: -rings - 2]
    signal_low, filter_low, grad_low, signal_bins, filter_spectrum, grad_bins, *refs = refs
    signal_out, filter_out, mixed, energy_ref, square_land, square_send, square_recv = refs
    signal_grad = filter_spectrum.at[:, : filter_spectrum.shape[1] // 2]
    peers = chan_peers()
    greet(peers[1:], ring.toward)
    ring.start()
    copies = exchange(
        peers, lambda peer: io.source[9].at[peer], lambda: square_land.at[peers[0]],
        square_send, square_recv,
    )
    if with_outputs:
        copies += to_channels(
            peers, io.source[10 + inputs], out_land, out_send, out_recv
        )
    io.ready(4, 5, 6)
    shard, slots = grad_ref.shape
    length = slots // blocks
    scale = 1.0 / length
    steps = shard // 16
    facts = Facts(seq_ref, blocks, length)

    def prepare(n, carry):
        rows = n * 16
        signals, scaled = [], []
        grads = grad_ref[sixteen(rows), :].astype(F32)
        for part in range(2):
            here = rows + 8 * part
            zero, one, two = (
                stream_rows(project_ref, columns_ref, keep_ref, here, shard, stream, blocks)
                for stream in range(3)
            )
            mixed[0, eight(here), :] = one
            mixed[1, eight(here), :] = two
            signals.append(one * two)
            cond = columns_ref[eight(here), 9:10]
            power = block_sums(two * two, blocks)
            energy, logs, factor = sequence_factor(power, cond, facts, blocks)
            conv_grad = grads[8 * part : 8 * part + 8] * zero
            factor_grad = block_sums(conv_grad * conv_ref[eight(here), :], blocks)
            cond_grad = 0.0
            for j in range(blocks):
                cond_grad = cond_grad + factor_grad[j] * logs[j]
            sums_ref[eight(here), 9:10] = cond_grad
            for i in range(blocks):
                total = 0.0
                for j in range(blocks):
                    total = total + factor_grad[j] * facts.same[i][j]
                energy_ref[eight(here), i : i + 1] = (
                    total * cond / (1.0 + energy[i]) * (2.0 * facts.inverse)
                )
                energy_ref[eight(here), blocks + i : blocks + i + 1] = factor[i]
            scaled.append(conv_grad * spread_blocks([one * scale for one in factor], length))
        store_blocks(signal_low, join(signals), rows, shard, blocks)
        store_blocks(grad_low, join(scaled), rows, shard, blocks)
        kernel = filter_ref[sixteen(rows), :].astype(BF16)
        store_blocks(filter_low, kernel, rows, shard, blocks)
        return carry

    for n in range(LOADS):
        for number, each in ((0, 1), (1, 3), (2, 1), (3, 1)):
            io.ready(number, cuts=slice(n * each, (n + 1) * each))
        lax.fori_loop(steps * n // LOADS, steps * (n + 1) // LOADS, prepare, 0)
    io.ready(7)
    io.ready(*range(10, 10 + rings))
    grad_bins[...] = matmul(grad_low[...], table_ref[...])
    signal_bins[...] = matmul(signal_low[...], table_ref[...])
    filter_spectrum[...] = matmul(filter_low[...], table_ref[...])
    ring.advance(0, 3)

    def combine(n, carry):
        rows = n * 16
        sign = sign_ref[0:1, :]
        joined = [[] for _ in range(blocks)]
        windows = [[] for _ in range(blocks)]
        for part in range(2):
            here = rows + 8 * part
            window = filter_bins(filter_spectrum, sign, here, shard, blocks)
            signal = plain_bins(signal_bins, here, shard, blocks)
            grads = plain_bins(grad_bins, here, shard, blocks)
            for j in range(blocks):
                for i in range(j, blocks):
                    fr, fi = window[i - j]
                    gr, gi = grads[i]
                    more_real, more_imag = fr * gr + fi * gi, fr * gi - fi * gr
                    if i == j:
                        real, imag = more_real, more_imag
                    else:
                        factor = facts.same[i][j]
                        real, imag = real + more_real * factor, imag + more_imag * factor
                joined[j].append(jnp.concatenate([real, imag], axis=1))
            after = None
            for k in reversed(range(blocks)):
                real = imag = None
                for j in range(blocks - k):
                    sr, si = signal[j]
                    gr, gi = grads[j + k]
                    more_real, more_imag = sr * gr + si * gi, sr * gi - si * gr
                    if k:
                        factor = facts.same[j + k][j]
                        more_real, more_imag = more_real * factor, more_imag * factor
                    real = more_real if real is None else real + more_real
                    imag = more_imag if imag is None else imag + more_imag
                if after is None:
                    whole = (real, imag)
                else:
                    whole = (real + sign * after[1], imag - sign * after[0])
                windows[k].append(jnp.concatenate(whole, axis=1))
                after = (real, imag)
        for j in range(blocks):
            signal_out[sixteen(j * shard + rows), :] = join(joined[j])
            filter_out[sixteen(j * shard + rows), :] = join(windows[j])
        return carry

    lax.fori_loop(0, steps, combine, 0)
    io.ready(10 + inputs + with_outputs)
    signal_grad[...] = matmul(signal_out[...], back_ref[...])
    ring.advance(1, 3)
    filter_rows = matmul(filter_out[...], back_ref[...])
    count, pack_rows, lanes = filter_pack.shape
    each = shard // count
    stack = slots // lanes
    if pack_rows > stack * each:
        filter_pack[...] = jnp.zeros_like(filter_pack)
    for chunk in range(count):
        lags = [
            filter_rows[j * shard + chunk * each : j * shard + (chunk + 1) * each]
            for j in range(blocks)
        ]
        layers = [
            jnp.concatenate(lags[n * blocks // stack : (n + 1) * blocks // stack], axis=1)
            for n in range(stack)
        ]
        value = layers[0] if stack == 1 else jnp.concatenate(layers, axis=0)
        filter_pack[chunk, : stack * each] = value.astype(BF16)
    io.flush(1)

    def finish(n, carry):
        rows = n * 16
        totals = [[] for _ in range(3)]
        outer = grad_ref[sixteen(rows), :].astype(F32)
        for part in range(2):
            here = rows + 8 * part
            local = eight(here)
            factor = [energy_ref[local, blocks + i : blocks + i + 1] for i in range(blocks)]
            energy = [energy_ref[local, i : i + 1] for i in range(blocks)]
            signal = jnp.concatenate(
                [signal_grad[eight(j * shard + here), :] for j in range(blocks)], axis=1
            )
            for stream in range(3):
                if stream == 0:
                    value = outer[8 * part : 8 * part + 8] * (
                        conv_ref[local, :] * spread_blocks(factor, length)
                    )
                elif stream == 1:
                    value = signal * mixed[1, local, :]
                else:
                    value = signal * mixed[0, local, :] + (
                        spread_blocks(energy, length) * mixed[1, local, :]
                    )
                plain = project_ref[eight(stream * shard + here), :]
                total = value * columns_ref[local, stream : stream + 1]
                sums_ref[local, stream : stream + 1] = lane_sums(value * plain)
                for offset in (1, 2):
                    column = 3 * offset + stream
                    moved = pltpu.roll(
                        mask_heads(value, keep_ref[offset - 1 : offset, :], blocks),
                        slots - offset, 1,
                    )
                    sums_ref[local, column : column + 1] = lane_sums(moved * plain)
                    total = total + moved * columns_ref[local, column : column + 1]
                totals[stream].append(total)
        for stream in range(3):
            project_grad[sixteen(stream * shard + rows), :] = join(totals[stream])
        return carry

    lax.fori_loop(0, steps // 2, finish, 0)
    ring.advance(2, 3)
    lax.fori_loop(steps // 2, steps, finish, 0)
    for stream in range(3):
        io.flush(0, stream, pl.ds(stream * shard, shard))
    for copy in copies:
        copy.wait()
    io.ready(9)
    total = square_ref[peers[0]].astype(F32)
    for peer in peers[1:]:
        total = total + square_land[peer].astype(F32)
    square_sum[...] = total
    io.flush(2)
    if with_outputs:
        io.ready(10 + inputs)
        tokens = residual_ref.shape[1]
        out_land[:, span(peers[0], tokens)] = residual_ref[span(peers[0], shard, 32), :]
        outputs_ref[...] = out_land[...].astype(F32)
        io.flush(4 + rings)
    io.flush(3)
    ring.finish()
    for n in range(rings):
        io.flush(4 + n)


def filter_layout(shard, slots, count):
    each = shard // count
    stack = 2 if each % 8 == 0 else 1
    return count, ring_rows(stack * each), slots // stack


def conv_backward(grad, project, conv, filter_rows, columns, keep, sign, table, seq_table, back, square,
                  tracks, residual, blocks, collective):
    shard, slots = filter_rows[0].shape[1:]
    length = slots // blocks
    low = pltpu.VMEM((blocks * shard, length), BF16)
    bins = pltpu.VMEM((blocks * shard, 2 * length), F32)
    out = pltpu.VMEM((blocks * shard, 2 * length), BF16)
    outs, extra = [], []
    if residual:
        outs = [((shard, slots), F32)]
        extra = [pltpu.VMEM((shard, slots), BF16)] + [pltpu.SemaphoreType.DMA((3,))] * 2
    return fused_call(
        lambda *refs: conv_backward_kernel(blocks, tracks, bool(residual), *refs),
        [grad, project, conv, filter_rows, columns, keep, sign, table, seq_table, square]
        + ring_operands(tracks)
        + list(residual)
        + [back],
        [
            ((3 * shard, slots), BF16),
            (filter_layout(shard, slots, tracks[0].count), BF16),
            ((shard, 4 * shard), F32),
            ((shard, 128), F32),
        ]
        + [one.out() for one in tracks]
        + outs,
        [low, low, low, bins, bins, bins, out, out]
        + [pltpu.VMEM((2, shard, slots), F32), pltpu.VMEM((shard, 128), F32)]
        + [pltpu.VMEM(square.shape, BF16)]
        + [pltpu.SemaphoreType.DMA((3,))] * 2
        + ring_scratch(tracks)
        + extra,
        collective,
        "conv_backward",
        [3, 1, 1, 1] + [1] * (len(tracks) + len(outs)),
        8,
        (4, 5, 6) + channel_order((0, 1, 2, 3)) + (7,),
        {0: channel_cuts(shard, 1), 1: channel_cuts(shard, 3), 2: channel_cuts(shard, 1)}
        | {3: channel_cuts(shard, 1)},
        tuple(range(10 + len(tracks), 10 + len(ring_operands(tracks)))),
    )


def last_kernel(layers, tracks, io, state_ref, *refs):
    refs = list(refs)
    gain_sums, refs = refs[: 2 * layers], refs[2 * layers :]
    row_sums, refs = refs[:layers], refs[layers:]
    rings, inputs = len(tracks), len(ring_operands(tracks))
    ring_in, refs = refs[:inputs], refs[inputs:]
    input_grad, small_out = refs[:2]
    large, refs = refs[2 : 2 + rings], refs[2 + rings :]
    state_low, landing, sums, turn, gains, gains_land, small_own, small_land, *refs = refs
    chan_send, chan_recv, small_send, small_recv, state_send, state_recv, *refs = refs
    peers = chan_peers()
    me = peers[0]
    dp = lax.axis_index("dp")
    first = 1 + 3 * layers
    ring = Ring(tracks, ring_in, large, refs, [io.source[first + n] for n in range(inputs)])
    count = ring.count
    shard = landing.shape[0]
    greet(peers[1:], [(dp + offset) % count for offset in range(1, count)])
    ring.start()
    io.ready(*range(0, first))
    for layer in range(layers):
        sums[:, 4 * layer : 4 * layer + 2] = gain_sums[2 * layer][:, 0:2]
        sums[:, 4 * layer + 2 : 4 * layer + 4] = gain_sums[2 * layer + 1][:, 0:2]
    turn[...] = jnp.zeros_like(turn)
    for owner in range(4):
        turn[:shard, : 4 * layers] = sums[owner * shard : (owner + 1) * shard, : 4 * layers]
        gains[owner] = turn[...].T[: 4 * layers]
    copies = exchange(
        peers, lambda peer: gains.at[peer], lambda: gains_land.at[me], chan_send, chan_recv
    )
    state_low[...] = state_ref[...].astype(BF16)
    state_copies = to_channels(peers, state_low, landing, state_send, state_recv)
    landing[:, span(me, state_low.shape[1])] = state_low[span(me, shard, 32), :]
    io.ready(*range(first, first + rings))
    ring.advance(0, 6)
    for layer in range(layers):
        turn[:shard, 10 * layer : 10 * layer + 10] = row_sums[layer][:, 0:10]
    small_own[4 * layers :, :] = turn[...].T[: small_own.shape[0] - 4 * layers]
    for copy in copies:
        copy.wait()
    total = gains[me]
    for peer in peers[1:]:
        total = total + gains_land[peer]
    small_own[: 4 * layers, :] = total
    small_copies = []
    for offset in range(1, count):
        copy = pltpu.make_async_remote_copy(
            small_own,
            small_land.at[offset - 1],
            small_send.at[offset - 1],
            small_recv.at[offset - 1],
            device_id={"dp": (dp + offset) % count},
        )
        copy.start()
        small_copies.append(copy)
    for point in range(1, 4):
        ring.advance(point, 6)
    small = small_own[...]
    for copy in small_copies:
        copy.wait()
    for n in range(count - 1):
        small = small + small_land[n]
    small_out[...] = small
    io.flush(1)
    ring.advance(4, 6)
    for copy in state_copies:
        copy.wait()
    input_grad[...] = landing[...].astype(F32)
    io.flush(0)
    ring.advance(5, 6)
    ring.finish()
    for n in range(rings):
        io.flush(2 + n)


def last_sums(state, gain_sums, row_sums, tracks, collective):
    width, tokens = state.shape
    shard = width // 4
    layers = len(row_sums)
    count = tracks[0].count
    small = (-(-14 * layers // 8) * 8, 256)
    return fused_call(
        lambda *refs: last_kernel(layers, tracks, *refs),
        [state] + gain_sums + row_sums + ring_operands(tracks),
        [((shard, 4 * tokens), F32), (small, F32)] + [one.out() for one in tracks],
        [
            pltpu.VMEM((width, tokens), BF16),
            pltpu.VMEM((shard, 4 * tokens), BF16),
            pltpu.VMEM((width, 128), F32),
            pltpu.VMEM((256, 128), F32),
            pltpu.VMEM((4, 4 * layers, 256), F32),
            pltpu.VMEM((4, 4 * layers, 256), F32),
            pltpu.VMEM(small, F32),
            pltpu.VMEM((count - 1,) + small, F32),
            pltpu.SemaphoreType.DMA((3,)),
            pltpu.SemaphoreType.DMA((3,)),
            pltpu.SemaphoreType.DMA((count - 1,)),
            pltpu.SemaphoreType.DMA((count - 1,)),
            pltpu.SemaphoreType.DMA((3,)),
            pltpu.SemaphoreType.DMA((3,)),
        ]
        + ring_scratch(tracks),
        collective,
        "last_sums",
        [1] * (2 + len(tracks)),
        order=tuple(range(1, 1 + 3 * layers)) + (0,),
        manual=tuple(
            range(1 + 3 * layers + len(tracks), 1 + 3 * layers + len(ring_operands(tracks)))
        ),
    )


def collect_kernel(layers, *refs):
    refs = list(refs)
    outputs_in, input_in, small = refs[:3]
    refs = refs[3:]
    feeds, refs = refs[:layers], refs[layers:]
    filters, refs = refs[:layers], refs[layers:]
    packs, refs = refs[:layers], refs[layers:]
    (outputs, input_grad, mix_gain, mix_bias, in_grad, short, filter_grad, cond, out_grad, glu_gain,
     glu_bias, up_grad, down_grad, held, sems) = refs
    pairs = ((outputs_in, outputs), (input_in, input_grad))
    loads = [
        pltpu.make_async_copy(source, held.at[n], sems.at[n]) for n, (source, _) in enumerate(pairs)
    ]
    copies = [
        pltpu.make_async_copy(held.at[n], target, sems.at[2 + n])
        for n, (_, target) in enumerate(pairs)
    ]
    for copy in loads:
        copy.start()
    each = in_grad.shape[1]
    shard = cond.shape[1]
    lanes = filters[0].shape[1]
    for layer in range(layers):
        for kind, out in enumerate((mix_gain, mix_bias, glu_gain, glu_bias)):
            row = 4 * layer + kind
            out[layer : layer + 1, :] = small[row : row + 1, :shard]
        row = 4 * layers + 10 * layer
        for tap in range(3):
            short[layer, tap] = small[row + 3 * tap : row + 3 * tap + 3, :shard]
        cond[layer : layer + 1, :] = small[row + 9 : row + 10, :shard]
        for stream in range(3):
            in_grad[layer, :, stream, :] = packs[layer][stream * each : (stream + 1) * each]
        out_grad[layer] = packs[layer][3 * each : 4 * each]
        for n in range(filter_grad.shape[2] // lanes):
            filter_grad[layer, :, n * lanes : (n + 1) * lanes] = filters[layer][
                n * each : (n + 1) * each
            ]
        rows = down_grad.shape[1]
        down_grad[layer] = feeds[layer][:rows]
        for kind in range(2):
            up_grad[layer, :, kind, :] = feeds[layer][(kind + 1) * rows : (kind + 2) * rows]
        loads[layer].wait()
        copies[layer].start()
    for copy in copies:
        copy.wait()


def collect(outputs, input_grad, small, feeds, filters, packs, each):
    layers = len(feeds)
    shard, slots = outputs.shape
    width = 4 * shard
    rows, hidden = feeds[0].shape[0] // 3, feeds[0].shape[1]
    anywhere = pl.BlockSpec(memory_space=pl.ANY)
    local = pl.BlockSpec(memory_space=pltpu.VMEM)
    operands = [outputs, input_grad, small, *feeds, *filters, *packs]
    small_shape = (layers, shard)
    shapes = [
        (shard, slots), (shard, slots), small_shape, small_shape, (layers, each, 3, width),
        (layers, 3, 3, shard), (layers, each, slots), small_shape, (layers, each, width),
        small_shape, small_shape, (layers, rows, 2, hidden), (layers, rows, hidden),
    ]
    return pl.pallas_call(
        lambda *refs: collect_kernel(layers, *refs),
        out_shape=tuple(jax.ShapeDtypeStruct(shape, F32) for shape in shapes),
        in_specs=[anywhere] * 2 + [local] * (len(operands) - 2),
        out_specs=tuple([anywhere] * 2 + [local] * (len(shapes) - 2)),
        scratch_shapes=[pltpu.VMEM((2, shard, slots), F32), pltpu.SemaphoreType.DMA((4,))],
        compiler_params=pltpu.CompilerParams(vmem_limit_bytes=VMEM_LIMIT),
        name="collect",
    )(*operands)


def body(
    inputs,
    seq_table,
    mix_gain,
    mix_bias,
    in_proj,
    short_conv,
    long_filter,
    cond_weight,
    out_proj,
    glu_gain,
    glu_bias,
    glu_in,
    glu_out,
    cotangent,
):
    shard, slots = inputs.shape
    layers, width = in_proj.shape[0], in_proj.shape[3]
    hidden = glu_out.shape[2]
    blocks = 4
    count = lax.axis_size("dp")
    each = shard // count
    turns = count // 2
    table = jnp.asarray(dft_table(slots // blocks), BF16)
    sign = jnp.asarray(np.tile(1.0 - 2.0 * (np.arange(slots // blocks) % 2), (8, 1)), F32)
    residual, gains, normed, project, in_rows, up_columns, columns, keep = first_project(
        inputs, (mix_gain, mix_bias, glu_gain, glu_bias), in_proj, short_conv, cond_weight,
        (glu_in, 0), seq_table, 1,
    )
    constants = (keep, sign, table, seq_table, jnp.asarray(dft_table(slots // blocks).T, BF16))
    kept, state = [], None
    for l in range(layers):
        gated, conv, carried = conv_forward(
            project, (long_filter, l), (columns, l), *constants, cotangent if l else out_proj,
            2 if l else 1, blocks, 10 + l,
        )
        if l:
            state = carried
        else:
            full_out = carried
        token_gated, middle, normed_glu, after, *rest = feed_forward(
            gated, residual, gains, (full_out, l), up_columns, (glu_out, l),
            ((in_rows, l + 1), (glu_in, l + 1)) if l + 1 < layers else (), 4 * l + 2, 20 + l,
        )
        saved, follow = [up_columns] + rest[:3], rest[3:]
        kept.append((residual, normed, project, conv, token_gated, middle, normed_glu, saved))
        residual = after
        if follow:
            normed, project, up_columns = follow
    feeds, filters, packs, gain_sums, row_sums = ([None] * layers for _ in range(5))
    waiting = []
    for l in reversed(range(layers)):
        before, normed, project, conv, token_gated, middle, normed_glu, saved = kept[l]
        top = l == layers - 1
        state, gated_grad, feed_grads, out_grad, glu_sums, *large = feed_back(
            state, middle, gains, normed_glu, saved[0], (glu_out, l), (full_out, l), token_gated,
            saved[1:], waiting, 4 * l + 2, count, 30 + l,
        )
        if waiting:
            filters[l + 1], packs[l + 1] = large
        project_low, filter_pack, square, row_sums[l], held, *rest = conv_backward(
            gated_grad, project, conv, (long_filter, l), (columns, l), *constants,
            out_grad.reshape(4, shard, width), [Track(feed_grads, 0, turns)],
            (residual,) if top else (), blocks, 40 + l,
        )
        if top:
            outputs = rest[0]
        feed_track = Track(feed_grads, turns, count - 1, held)
        state, in_pack, mix_sums, feeds[l], held = project_back(
            project_low, state, before, gains, normed, (in_rows, l), square,
            [feed_track, Track(filter_pack, 0, turns)], 4 * l, 50 + l,
        )
        waiting = [Track(filter_pack, turns, count - 1, held), Track(in_pack, 0, count - 1)]
        gain_sums[l] = [mix_sums, glu_sums]
    input_grad, small, filters[0], packs[0] = last_sums(
        state, [one for pair in gain_sums for one in pair], row_sums, waiting, 60
    )
    return collect(outputs, input_grad, small, feeds, filters, packs, each)


def solution(mesh):
    in_specs = (
        P("chan", "dp"),
        P("dp", None),
        P(None, "chan"),
        P(None, "chan"),
        P(None, "chan", None, None),
        P(None, None, None, "chan"),
        P(None, "chan", None),
        P(None, "chan"),
        P(None, "chan", None),
        P(None, "chan"),
        P(None, "chan"),
        P(None, None, None, "chan"),
        P(None, None, "chan"),
        P("chan", "dp"),
    )
    out_specs = (
        P("chan", "dp"),
        P("chan", "dp"),
        P(None, "chan"),
        P(None, "chan"),
        P(None, ("chan", "dp"), None, None),
        P(None, None, None, "chan"),
        P(None, ("chan", "dp"), None),
        P(None, "chan"),
        P(None, ("chan", "dp"), None),
        P(None, "chan"),
        P(None, "chan"),
        P(None, "dp", None, "chan"),
        P(None, "dp", "chan"),
    )
    return jax.shard_map(body, mesh=mesh, in_specs=in_specs, out_specs=out_specs, check_vma=False)
```

time: 1490 us -> 471 us (0.32)
  waiting for transfers between devices: 647 us -> 0 us
  Pallas kernels: 0 us -> 452 us
  matrix products: 413 us -> 0 us
  other arithmetic: 189 us -> 0 us
  blocking collectives: 123 us -> 0 us
  local copies, waits for them, and re-layouts: 86 us -> 9.04 us
  between operations: 19.7 us -> 1.19 us
    reduce_scatter x13 -> x0, waiting for transfers between devices: 499 us -> none  [the longest x6 159 us: sum_channels(): lax.psum_scatter(summand.astype(jnp.bfloat16), 'chan', scatter_dimension=...]
    pallas_call x0 -> x13, Pallas kernels: none -> 452 us  [the longest x12 446 us: fused_call(): pl.pallas_call(body, out_shape=tuple((jax.ShapeDtypeStruct(*out) for out...]
    dot_general x54 -> x0, matrix products: 406 us -> none  [the longest x4 63.4 us: block_conv(): kernel_imag = jnp.einsum('fm,kmc->kfc', sine_neg, lagged, precision=PRECISE)]
    all_gather x8 -> x0, waiting for transfers between devices: 146 us -> none  [the longest x6 101 us: gather_channels(): return lax.all_gather(values, 'chan', axis=1, tiled=True)]
    psum x9 -> x0, blocking collectives: 123 us -> none  [the longest x8 85.2 us: channel_sums(): return lax.psum((first_sum, second_sum), 'chan')]
    broadcast_in_dim x6 -> x0, other arithmetic: 56.5 us -> none  [the longest x4 49.2 us: glu_units(): return jax.nn.gelu(gate_up[:, 0], approximate=False) * gate_up[:, 1]]
    reduce_sum x12 -> x0, other arithmetic: 48.9 us -> none  [the longest x1 15 us: block_conv(): kernel_real[shift_by] * source_imag + kernel_imag[shift_by] * source_real]
    unnamed x492 -> x2, local copies, waits for them, and re-layouts: 47.6 us -> 5.77 us
  transfers between devices with their start and end apart: 21 -> 0, of which waited for: 18 -> 0; matrix products, arithmetic and copies ran while one was open for 23% -> 0% of each run, Pallas kernels for 0% -> 0%
where the time goes in v1:
time: 471 us; the launch traced here: 463 us
  Pallas kernels  452 us (96%)
  local copies, waits for them, and re-layouts  9.04 us (2%)
    pallas_call x12, Pallas kernels, fused_call(): pl.pallas_call(body, out_shape=tuple((jax.ShapeDtypeStruct(*out) for out...  446 us

profile of v1, /device:TPU:0, one launch (start us, length us, event | category | flops | bytes accessed | tf_op | source)
XLA Modules:
  0.0 462.7 jit_solution(15761377439004412311)
XLA Ops:
  0.6 1.3 copy.31.refs_6_
  2.0 4.4 copy.30.refs_5_
  6.4 29.0 %first_project.1 = (f32[768,512]{1,0:T(8,128)}, f32[768,128]{1,0:T(8,128)}, bf16[8,768,256]{2,1,0:T(8,128)(2,1)}, f32[576,2048]{1,0:T(8,128)}, bf16[2,576,768]{2...) custom-call(bf16[192,2048]{1,0:T(8,128)(2,1)} %refs_0_.3, ...), custom_call_target="tpu_custom_call" | custom-call | tf_op jit(solution)/shard_map/first_project/pallas_call | solution.py:127
  35.4 19.6 %conv_forward.2 = (bf16[192,2048]{1,0:T(8,128)(2,1)}, f32[192,2048]{1,0:T(8,128)}, bf16[2,768,768]{2,1,0:T(8,128)(2,1)}) custom-call(f32[2,192,2048]{2,1,0:T(8,128)} %refs_3_.5, f32[576,2048]{1,0:T(8,128)} %get-tuple-element.81.refs_1_, f32[2,192,128]{2,1,0:T(8,128)} %get-tuple-element.82.refs_2_.refs_4_, f32[8,2048]{1,0:T(8,128)} %get-tuple-element.83.refs_3_.refs_5_, ...), custom_call_target="tpu_custom_call" | custom-call | tf_op jit(solution)/shard_map/conv_forward/pallas_call | solution.py:127
  55.0 66.6 %feed_forward.2 = (bf16[768,512]{1,0:T(8,128)(2,1)}, f32[768,512]{1,0:T(8,128)}, bf16[8,768,256]{2,1,0:T(8,128)(2,1)}, f32[768,512]{1,0:T(8,128)}, bf16[8,768,25...) custom-call(bf16[192,2048]{1,0:T(8,128)(2,1)} %get-tuple-element.84., ...), custom_call_target="tpu_custom_call" | custom-call | tf_op jit(solution)/shard_map/feed_forward/pallas_call | solution.py:127
  121.7 25.1 %conv_forward.3 = (bf16[192,2048]{1,0:T(8,128)(2,1)}, f32[192,2048]{1,0:T(8,128)}, bf16[8,768,256]{2,1,0:T(8,128)(2,1)}) custom-call(f32[2,192,2048]{2,1,0:T(8,128)} %refs_3_.5, f32[576,2048]{1,0:T(8,128)} %get-tuple-element.90.refs_1_, f32[2,192,128]{2,1,0:T(8,128)} %get-tuple-element.82.refs_2_.refs_4_, f32[8,2048]{1,0:T(8,128)} %get-tuple-element.83.refs_3_.refs_5_, ...), custom_call_target="tpu_custom_call" | custom-call | tf_op jit(solution)/shard_map/conv_forward/pallas_call | solution.py:127
  146.7 47.0 %feed_forward.3 = (bf16[768,512]{1,0:T(8,128)(2,1)}, f32[768,512]{1,0:T(8,128)}, bf16[8,768,256]{2,1,0:T(8,128)(2,1)}, bf16[768,512]{1,0:T(8,128)(2,1)}, bf16[8,...) custom-call(bf16[192,2048]{1,0:T(8,128)(2,1)} %get-tuple-element.92.refs_0_, ...), custom_call_target="tpu_custom_call" | custom-call | tf_op jit(solution)/shard_map/feed_forward/pallas_call | solution.py:127
  193.8 40.7 %feed_back.2 = (f32[768,512]{1,0:T(8,128)}, bf16[192,2048]{1,0:T(8,128)(2,1)}, bf16[8,288,768]{2,1,0:T(8,128)(2,1)}, bf16[768,768]{1,0:T(8,128)(2,1)}, f32[768,8]{1,0:T(8,128)}) custom-call(bf16[8,768,256]{2,1,0:T(8,128)(2,1)} %get-tuple-element.91.refs_0_, bf16[2,768,768]{2,1,0:T(8,128)(2,1)} %refs_1_.5, bf16[8,768,256]{2,1,0:T(8,128)(2,1)} %get-tuple-element.95.refs_2_, ...), custom_call_target="tpu_custom_call" | custom-call | tf_op jit(solution)/shard_map/feed_back/pallas_call | solution.py:127
  234.4 39.4 %conv_backward.2 = (bf16[576,2048]{1,0:T(8,128)(2,1)}, bf16[8,48,1024]{2,1,0:T(8,128)(2,1)}, f32[192,768]{1,0:T(8,128)}, f32[192,128]{1,0:T(8,128)}, bf16[2,288,384]{2,1,0:T(8,128)(2,1)}, /*index=5*/f32[192,2048]{1,0:T(8,128)}) custom-call(bf16[192,2048]{1,0:T(8,128)(2,1)} %get-tuple-element.101.refs_0_, f32[576,2048]{1,0:T(8,128)} %get-tuple-element.90.refs_1_, ...), custom_call_target="tpu_custom_call" | custom-call | tf_op jit(solution)/shard_map/conv_backward/pallas_call | solution.py:127
  273.9 29.3 %project_back.2 = (f32[768,512]{1,0:T(8,128)}, bf16[8,96,768]{2,1,0:T(8,128)(2,1)}, f32[768,8]{1,0:T(8,128)}, f32[288,768]{1,0:T(8,128)}, bf16[2,48,512]{2,1,0:T(8,128)(2,1)}) custom-call(bf16[576,2048]{1,0:T(8,128)(2,1)} %get-tuple-element.107.refs_0_, bf16[2,576,768]{2,1,0:T(8,128)(2,1)} %get-tuple-element.89.refs_6_.refs_1_, ...), custom_call_target="tpu_custom_call" | custom-call | tf_op jit(solution)/shard_map/project_back/pallas_call | solution.py:127
  303.1 49.6 %feed_back.3 = (f32[768,512]{1,0:T(8,128)}, bf16[192,2048]{1,0:T(8,128)(2,1)}, bf16[8,288,768]{2,1,0:T(8,128)(2,1)}, bf16[768,768]{1,0:T(8,128)(2,1)}, f32[768,8...) custom-call(f32[768,512]{1,0:T(8,128)} %get-tuple-element.113.refs_0_, bf16[2,768,768]{2,1,0:T(8,128)(2,1)} %refs_1_.5, ...), custom_call_target="tpu_custom_call" | custom-call | tf_op jit(solution)/shard_map/feed_back/pallas_call | solution.py:127
  352.8 37.7 %conv_backward.3 = (bf16[576,2048]{1,0:T(8,128)(2,1)}, bf16[8,48,1024]{2,1,0:T(8,128)(2,1)}, f32[192,768]{1,0:T(8,128)}, f32[192,128]{1,0:T(8,128)}, bf16[2,288,384]{2,1,0:T(8,128)(2,1)}) custom-call(bf16[192,2048]{1,0:T(8,128)(2,1)} %get-tuple-element.122.refs_0_, f32[576,2048]{1,0:T(8,128)} %get-tuple-element.81.refs_1_, ...), custom_call_target="tpu_custom_call" | custom-call | tf_op jit(solution)/shard_map/conv_backward/pallas_call | solution.py:127
  390.5 28.0 %project_back.3 = (f32[768,512]{1,0:T(8,128)}, bf16[8,96,768]{2,1,0:T(8,128)(2,1)}, f32[768,8]{1,0:T(8,128)}, f32[288,768]{1,0:T(8,128)}, bf16[2,48,512]{2,1,0:T(8,128)(2,1)}) custom-call(bf16[576,2048]{1,0:T(8,128)(2,1)} %get-tuple-element.126.refs_0_, bf16[2,576,768]{2,1,0:T(8,128)(2,1)} %get-tuple-element.89.refs_6_.refs_1_, ...), custom_call_target="tpu_custom_call" | custom-call | tf_op jit(solution)/shard_map/project_back/pallas_call | solution.py:127
  418.5 34.0 %last_sums.1 = (f32[192,2048]{1,0:T(8,128)}, f32[32,256]{1,0:T(8,128)}, f32[48,1024]{1,0:T(8,128)}, f32[96,768]{1,0:T(8,128)}) custom-call(f32[768,512]{1,0:T(8,128)} %get-tuple-element.132.refs_0_, f32[768,8]{1,0:T(8,128)} %get-tuple-element.133.refs_1_, f32[768,8]{1,0:T(8,128)} %get-tuple-element.134.refs_2_, f32[768,8]{1,0:T(8,128)} %get-tuple-element.135.refs_3_, ...), custom_call_target="tpu_custom_call" | custom-call | tf_op jit(solution)/shard_map/last_sums/pallas_call | solution.py:127
  452.5 6.5 %collect.1 = (f32[192,2048]{1,0:T(8,128)}, f32[192,2048]{1,0:T(8,128)}, f32[2,192]{1,0:T(2,128)}, f32[2,192]{1,0:T(2,128)}, f32[2,24,3,768]{3,2,1,0:T(4,128)}, /...) custom-call(f32[192,2048]{1,0:T(8,128)} %get-tuple-element.106.refs_, ...), custom_call_target="tpu_custom_call" | custom-call | tf_op jit(solution)/shard_map/collect/pallas_call | solution.py:1810
  459.0 1.4 copy.33
  460.3 1.9 copy.32

commit v2 on v1

--- a/solution.py
+++ b/solution.py
@@ -409,8 +409,8 @@
 
 
 def first_project_kernel(
-    io, inputs_ref, mix_gain, mix_bias, glu_gain, glu_bias, weight_in, short_in, cond_in, up_in,
-    seq_ref, x_ref, gains_ref, full, project_ref, weight_ref, up_ref, columns_ref, keep_ref,
+    io, inputs_ref, mix_gain, mix_bias, glu_gain, glu_bias, weight_in, short_in, cond_in,
+    seq_ref, x_ref, gains_ref, full, project_ref, weight_ref, columns_ref, keep_ref,
     raw, gains_low, gains_land, turn, send, recv, gains_send, gains_recv,
 ):
     peers = chan_peers()
@@ -451,9 +451,8 @@
     row = lax.broadcasted_iota(jnp.int32, keep_ref.shape, 0)
     within = slot & (seq_ref[0, 0] - 1)
     keep_ref[...] = jnp.where(within > row, 1.0, 0.0)
-    io.flush(4)
-    io.flush(6)
-    io.flush(7)
+    for number in (4, 5, 6):
+        io.flush(number)
     for copy in copies:
         copy.wait()
     turn[...] = jnp.zeros_like(turn)
@@ -461,7 +460,6 @@
         turn[: 4 * layers, :shard] = gains_land[owner]
         gains_ref[owner * shard : (owner + 1) * shard, :] = turn[...].T[:shard]
     io.flush(1)
-    io.ready(8)
     gather(0, 0).wait_recv()
     gather(2, 0).start()
     for part in range(parts):
@@ -482,33 +480,25 @@
         columns = slice(part * half, (part + 1) * half)
         project_ref[:, columns] = matmul(weight_ref[0], full[part])
         io.flush(3, part, (slice(None), pl.ds(part * half, half)))
-        cuts = width // 64
-        lax.fori_loop(
-            cuts * part // parts, cuts * (part + 1) // parts, split_rows(up_ref, up_in, 64, True), 0
-        )
     io.flush(0)
-    io.flush(5)
     for part in range(parts):
         for kind in range(3):
             gather(kind, part).wait_send()
 
 
-def first_project(inputs, gain_arrays, in_proj, short_conv, cond_weight, glu_in, seq_table,
-                  collective):
+def first_project(inputs, gain_arrays, in_proj, short_conv, cond_weight, seq_table, collective):
     shard, slots = inputs.shape
     layers, _, streams, width = in_proj.shape
-    hidden = glu_in[0].shape[3]
     tokens = slots // 4
     return fused_call(
         first_project_kernel,
-        [inputs, *gain_arrays, in_proj, short_conv, cond_weight, glu_in, seq_table],
+        [inputs, *gain_arrays, in_proj, short_conv, cond_weight, seq_table],
         [
             ((width, tokens), F32),
             ((width, 128), F32),
             ((8, width, tokens // 2), BF16),
             ((streams * shard, slots), F32),
             ((layers, streams * shard, width), BF16),
-            ((width, 2 * hidden), BF16),
             ((layers, shard, 128), F32),
             ((8, slots), F32),
         ],
@@ -522,8 +512,8 @@
         + [pltpu.SemaphoreType.DMA((3,))] * 2,
         collective,
         "first_project",
-        (1, 1, 8, 8, 1, 1, 1, 1),
-        9,
+        (1, 1, 8, 8, 1, 1, 1),
+        8,
     )
 
 
@@ -638,7 +628,7 @@
             scatter_copy(peers, buffers, scatter_sems, kind, part).wait_send()
 
 
-def feed_kernel(gain_at, follows, io, gated_ref, x_ref, gains_ref, out_weight, up_columns,
+def feed_kernel(gain_at, raw, follows, io, gated_ref, x_ref, gains_ref, out_weight, up_columns,
                 down_weight, *refs):
     refs = list(refs)
     weight_ref, up_in = (refs.pop(0), refs.pop(0)) if follows else (None, None)
@@ -647,6 +637,7 @@
     if follows:
         next_full, project_ref, next_up = refs[:3]
         *refs, next_send, next_recv = refs[3:]
+    up_raw, up_columns = (up_columns, refs.pop(0)) if raw else (None, up_columns)
     up_weight, kept, own, *rest = refs
     buffers, sems = rest[:6], rest[6:]
     send, recv, gather_send, gather_recv, scatter_send, scatter_recv = sems
@@ -659,8 +650,12 @@
     greet(peers[1:])
     io.ready(0)
     copies = to_tokens(peers, gated_ref, token_gated, send, recv)
-    io.ready(1, 2, 3, 4, 5)
+    io.ready(4)
+    if raw:
+        lax.fori_loop(0, width // 64, split_rows(up_columns, up_raw, 64, True), 0)
+        io.flush(7 + 3 * follows)
     transpose_columns(up_weight, up_columns, 256)
+    io.ready(1, 2, 3, 5)
     for part in range(2):
         for copy in copies[part]:
             copy.wait()
@@ -766,8 +761,12 @@
         outs.append(((width, 2 * hidden), BF16))
         parts += [8, 8, 1]
         extra = [pltpu.SemaphoreType.DMA((3, 2))] * 2
+    raw = up_columns[0].ndim == 4 if isinstance(up_columns, tuple) else False
+    if raw:
+        outs.append(((width, 2 * hidden), BF16))
+        parts.append(1)
     return fused_call(
-        lambda *refs: feed_kernel(gain_at, bool(follows), *refs),
+        lambda *refs: feed_kernel(gain_at, raw, bool(follows), *refs),
         [gated, values, gains, out_weight, up_columns, down_weight] + follows,
         outs,
         [
@@ -782,6 +781,7 @@
         collective,
         "feed_forward",
         parts,
+        order=(0, 4),
     )
 
 
@@ -813,7 +813,7 @@
         ring = Ring(tracks, ring_in, large, refs[-rings - 2 :], sources)
         refs = refs[: -rings - 2]
     full = grad_ref if gathered else refs.pop(0)
-    gates, mixer_low, kept, own, turned, *rest, load_sems = refs
+    mixer_low, kept, own, turned, *rest, load_sems = refs
     gated_low = full
     buffers, sems = rest[:6], rest[6:]
     send, recv, gather_send, gather_recv, scatter_send, scatter_recv = sems
@@ -862,11 +862,12 @@
         grad = full[block]
         for n in range(hidden // tile):
             rows = slice(n * tile, (n + 1) * tile)
-            later = slice(hidden + n * tile, hidden + (n + 1) * tile)
             unit_grad = matmul(down_rows[rows], grad)
-            gates[block, rows] = (unit_grad * slopes[block, rows].astype(F32)).astype(BF16)
-            gates[block, later] = (unit_grad * gelus[block, rows].astype(F32)).astype(BF16)
-        return matmul(up_columns[...], gates[block])
+            slopes[block, rows] = (unit_grad * slopes[block, rows].astype(F32)).astype(BF16)
+            gelus[block, rows] = (unit_grad * gelus[block, rows].astype(F32)).astype(BF16)
+        return matmul(up_columns[:, :hidden], slopes[block]) + matmul(
+            up_columns[:, hidden:], gelus[block]
+        )
 
     run_blocks(peers, full, gather_sems, scatter_sems, buffers, partial, kept, own, ring)
     io.ready(5, 6, 7, 8, 9, 10)
@@ -897,21 +898,24 @@
 
         return store
 
+    def feed_grad(kind):
+        if kind == 0:
+            left, right = lambda b, r: full[b, r], lambda b, c: units[b, c]
+        else:
+            def left(b, r):
+                return normed[b, r]
+
+            def right(b, c):
+                return (slopes, gelus)[kind - 1][b, c]
+
+        weight_grad(store_grad(kind), width, hidden, left, right, 8, row_tile, tile)
+
     def store_out(index, column, total):
         out_grad[span(index, tile), column] = total.astype(BF16)
 
     gain = gains_ref[:, gain_at : gain_at + 1]
     for part in range(2):
-        for kind in (0,) if part == 0 else (1, 2):
-            if kind == 0:
-                left, right = lambda b, r: full[b, r], lambda b, c: units[b, c]
-            else:
-                first = (kind - 1) * hidden
-                left = lambda b, r: normed[b, r]
-                right = lambda b, c, first=first: gates[
-                    b, pl.ds(pl.multiple_of(c.start + first, tile), tile)
-                ]
-            weight_grad(store_grad(kind), width, hidden, left, right, 8, row_tile, tile)
+        feed_grad(part)
         columns = slice(part * half, (part + 1) * half)
         grad = scattered(peers, scatter_sems, buffers, own, part)
         change, product = norm_pullback(grad, mid_ref[:, columns], gain)
@@ -929,6 +933,7 @@
             sums_ref[:, 0:1] = sums_ref[:, 0:1] + lane_sums(product)
             sums_ref[:, 1:2] = sums_ref[:, 1:2] + lane_sums(grad)
     io.flush(0)
+    feed_grad(2)
     io.flush(2)
     io.flush(4)
     for part in range(2):
@@ -974,7 +979,6 @@
         + [one.out() for one in tracks],
         [pltpu.VMEM((8, width, half), BF16)] * (not gathered)
         + [
-            pltpu.VMEM((8, 2 * hidden, half), BF16),
             pltpu.VMEM((width, tokens), BF16),
             pltpu.VMEM((width, half), F32),
             pltpu.VMEM((2, width, half), F32),
@@ -993,14 +997,17 @@
     )
 
 
-def project_back_kernel(gain_at, each, tracks, io, project_grad, weight_ref, square_ref, normed,
+def project_back_kernel(gain_at, each, tracks, in_track, io, project_grad, weight_ref, square_ref, normed,
                         state_ref, x_ref, gains_ref, *refs):
     inputs = len(ring_operands(tracks))
     ring_in, refs = refs[:inputs], refs[inputs:]
     next_ref, in_grad, sums_ref = refs[:3]
     large, refs = refs[3 : 3 + len(tracks)], refs[3 + len(tracks) :]
+    in_held, *refs = refs
     kept, own, weight_rows, in_full, *rest = refs
     buffers, (scatter_send, scatter_recv, *ring_rest) = rest[:6], rest[6:]
+    *ring_rest, in_slots, in_send, in_recv = ring_rest
+    in_ring = Ring([in_track], [in_grad], [in_held], [in_slots, in_send, in_recv], [in_grad])
     scatter_sems = (scatter_send, scatter_recv)
     peers = chan_peers()
     me, mate, across, diag = peers
@@ -1031,8 +1038,6 @@
         buffers[2][part] = share(mate, part).astype(BF16)
         scatter_copy(peers, buffers, scatter_sems, 1, part).start()
         own[part] = share(me, part)
-    io.ready(*range(7, 7 + len(tracks)))
-    ring.advance(0, 3)
     io.ready(2, 3)
     if in_full.shape[1] > 4 * each:
         in_full[...] = jnp.zeros_like(in_full)
@@ -1056,9 +1061,11 @@
             return carry
 
         lax.fori_loop(0, width // tile, column_tile, 0)
-    ring.advance(1, 3)
     in_grad[...] = in_full[...].astype(BF16)
+    in_ring.start()
     io.flush(1)
+    io.ready(*range(7, 7 + len(tracks)))
+    ring.advance(0, 2)
     io.ready(4, 5, 6)
     gain = gains_ref[:, gain_at : gain_at + 1]
     for part in range(2):
@@ -1069,7 +1076,8 @@
         if part == 0:
             sums_ref[:, 0:1] = lane_sums(product)
             sums_ref[:, 1:2] = lane_sums(grad)
-            ring.advance(2, 3)
+            ring.advance(1, 2)
+            in_ring.advance(0, 1)
         else:
             sums_ref[:, 0:1] = sums_ref[:, 0:1] + lane_sums(product)
             sums_ref[:, 1:2] = sums_ref[:, 1:2] + lane_sums(grad)
@@ -1078,6 +1086,8 @@
     ring.finish()
     for n in range(len(tracks)):
         io.flush(3 + n)
+    in_ring.finish()
+    io.flush(3 + len(tracks))
     drain_scatter(peers, scatter_sems, buffers)
 
 
@@ -1089,11 +1099,12 @@
     count = tracks[0].count
     each = rows // 3 // count
     packed = (count, ring_rows(4 * each), width)
+    in_track = Track(jax.ShapeDtypeStruct(packed, BF16), 0, count // 4)
     return fused_call(
-        lambda *refs: project_back_kernel(gain_at, each, tracks, *refs),
+        lambda *refs: project_back_kernel(gain_at, each, tracks, in_track, *refs),
         [project_grad, weight, square, normed, state, values, gains] + ring_operands(tracks),
         [((width, tokens), F32), (packed, BF16), ((width, 8), F32)]
-        + [one.out() for one in tracks],
+        + [one.out() for one in tracks + [in_track]],
         [
             pltpu.VMEM((width, half), F32),
             pltpu.VMEM((2, width, half), F32),
@@ -1102,10 +1113,11 @@
         ]
         + scatter_buffers(width, half)
         + [pltpu.SemaphoreType.DMA((3, 2))] * 2
-        + ring_scratch(tracks),
+        + ring_scratch(tracks)
+        + ring_scratch([in_track]),
         collective,
         "project_back",
-        [1] * (3 + len(tracks)),
+        [1] * (4 + len(tracks)),
         manual=tuple(range(7 + len(tracks), 7 + len(ring_operands(tracks)))),
         order=(1, 0) + tuple(range(7, 7 + len(tracks))),
     )
@@ -1840,13 +1852,13 @@
     blocks = 4
     count = lax.axis_size("dp")
     each = shard // count
-    turns = count // 2
     table = jnp.asarray(dft_table(slots // blocks), BF16)
     sign = jnp.asarray(np.tile(1.0 - 2.0 * (np.arange(slots // blocks) % 2), (8, 1)), F32)
-    residual, gains, normed, project, in_rows, up_columns, columns, keep = first_project(
+    residual, gains, normed, project, in_rows, columns, keep = first_project(
         inputs, (mix_gain, mix_bias, glu_gain, glu_bias), in_proj, short_conv, cond_weight,
-        (glu_in, 0), seq_table, 1,
+        seq_table, 1,
     )
+    up_columns = (glu_in, 0)
     constants = (keep, sign, table, seq_table, jnp.asarray(dft_table(slots // blocks).T, BF16))
     kept, state = [], None
     for l in range(layers):
@@ -1862,7 +1874,9 @@
             gated, residual, gains, (full_out, l), up_columns, (glu_out, l),
             ((in_rows, l + 1), (glu_in, l + 1)) if l + 1 < layers else (), 4 * l + 2, 20 + l,
         )
-        saved, follow = [up_columns] + rest[:3], rest[3:]
+        saved, follow = rest[:3], rest[3:]
+        up_columns = follow.pop() if l == 0 else up_columns
+        saved = [up_columns] + saved
         kept.append((residual, normed, project, conv, token_gated, middle, normed_glu, saved))
         residual = after
         if follow:
@@ -1877,22 +1891,27 @@
             saved[1:], waiting, 4 * l + 2, count, 30 + l,
         )
         if waiting:
-            filters[l + 1], packs[l + 1] = large
+            feeds[l + 1], filters[l + 1], packs[l + 1] = large
+        one, two = (count // 4, count // 2) if l else (3 * count // 8, 5 * count // 8)
         project_low, filter_pack, square, row_sums[l], held, *rest = conv_backward(
             gated_grad, project, conv, (long_filter, l), (columns, l), *constants,
-            out_grad.reshape(4, shard, width), [Track(feed_grads, 0, turns)],
+            out_grad.reshape(4, shard, width), [Track(feed_grads, 0, one)],
             (residual,) if top else (), blocks, 40 + l,
         )
         if top:
             outputs = rest[0]
-        feed_track = Track(feed_grads, turns, count - 1, held)
-        state, in_pack, mix_sums, feeds[l], held = project_back(
+        tracks = [Track(feed_grads, one, two, held), Track(filter_pack, 0, two - one)]
+        state, in_pack, mix_sums, feed_held, held, in_held = project_back(
             project_low, state, before, gains, normed, (in_rows, l), square,
-            [feed_track, Track(filter_pack, 0, turns)], 4 * l, 50 + l,
+            tracks, 4 * l, 50 + l,
         )
-        waiting = [Track(filter_pack, turns, count - 1, held), Track(in_pack, 0, count - 1)]
+        waiting = [
+            Track(feed_grads, two, count - 1, feed_held),
+            Track(filter_pack, two - one, count - 1, held),
+            Track(in_pack, count // 4, count - 1, in_held),
+        ]
         gain_sums[l] = [mix_sums, glu_sums]
-    input_grad, small, filters[0], packs[0] = last_sums(
+    input_grad, small, feeds[0], filters[0], packs[0] = last_sums(
         state, [one for pair in gain_sums for one in pair], row_sums, waiting, 60
     )
     return collect(outputs, input_grad, small, feeds, filters, packs, each)

time: 471 us -> 463 us (0.983)
  Pallas kernels: 452 us -> 446 us
    pallas_call x12, Pallas kernels: 446 us -> 439 us  [fused_call(): pl.pallas_call(body, out_shape=tuple((jax.ShapeDtypeStruct(*out) for out...]
where the time goes in v2:
time: 463 us; the launch traced here: 456 us
  Pallas kernels  446 us (96%)
  local copies, waits for them, and re-layouts  9.04 us (2%)
    pallas_call x12, Pallas kernels, fused_call(): pl.pallas_call(body, out_shape=tuple((jax.ShapeDtypeStruct(*out) for out...  439 us

profile of v2, /device:TPU:0, one launch (start us, length us, event | category | flops | bytes accessed | tf_op | source)
XLA Modules:
  0.0 456.0 jit_solution(1299020675352825923)
XLA Ops:
  0.6 1.3 copy.31.refs_6_
  2.0 4.4 copy.30.refs_5_
  6.4 26.4 %first_project.1 = (f32[768,512]{1,0:T(8,128)}, f32[768,128]{1,0:T(8,128)}, bf16[8,768,256]{2,1,0:T(8,128)(2,1)}, f32[576,2048]{1,0:T(8,128)}, bf16[2,576,768]{2...) custom-call(bf16[192,2048]{1,0:T(8,128)(2,1)} %refs_0_.3, f32[2,192]{1,0:T(2,128)} %refs_1_.3, ...), custom_call_target="tpu_custom_call" | custom-call | tf_op jit(solution)/shard_map/first_project/pallas_call | solution.py:127
  32.8 20.8 %conv_forward.2 = (bf16[192,2048]{1,0:T(8,128)(2,1)}, f32[192,2048]{1,0:T(8,128)}, bf16[2,768,768]{2,1,0:T(8,128)(2,1)}) custom-call(f32[2,192,2048]{2,1,0:T(8,128)} %refs_3_.5, f32[576,2048]{1,0:T(8,128)} %get-tuple-element.85.refs_1_, f32[2,192,128]{2,1,0:T(8,128)} %get-tuple-element.86.refs_2_.refs_4_, f32[8,2048]{1,0:T(8,128)} %get-tuple-element.87.refs_3_.refs_5_, ...), custom_call_target="tpu_custom_call" | custom-call | tf_op jit(solution)/shard_map/conv_forward/pallas_call | solution.py:127
  53.6 66.7 %feed_forward.2 = (bf16[768,512]{1,0:T(8,128)(2,1)}, f32[768,512]{1,0:T(8,128)}, bf16[8,768,256]{2,1,0:T(8,128)(2,1)}, f32[768,512]{1,0:T(8,128)}, bf16[8,768,25...) custom-call(bf16[192,2048]{1,0:T(8,128)(2,1)} %get-tuple-element.88., ...), custom_call_target="tpu_custom_call" | custom-call | tf_op jit(solution)/shard_map/feed_forward/pallas_call | solution.py:127
  120.3 25.2 %conv_forward.3 = (bf16[192,2048]{1,0:T(8,128)(2,1)}, f32[192,2048]{1,0:T(8,128)}, bf16[8,768,256]{2,1,0:T(8,128)(2,1)}) custom-call(f32[2,192,2048]{2,1,0:T(8,128)} %refs_3_.5, f32[576,2048]{1,0:T(8,128)} %get-tuple-element.93.refs_1_, f32[2,192,128]{2,1,0:T(8,128)} %get-tuple-element.86.refs_2_.refs_4_, f32[8,2048]{1,0:T(8,128)} %get-tuple-element.87.refs_3_.refs_5_, ...), custom_call_target="tpu_custom_call" | custom-call | tf_op jit(solution)/shard_map/conv_forward/pallas_call | solution.py:127
  145.5 46.9 %feed_forward.3 = (bf16[768,512]{1,0:T(8,128)(2,1)}, f32[768,512]{1,0:T(8,128)}, bf16[8,768,256]{2,1,0:T(8,128)(2,1)}, bf16[768,512]{1,0:T(8,128)(2,1)}, bf16[8,...) custom-call(bf16[192,2048]{1,0:T(8,128)(2,1)} %get-tuple-element.95.refs_0_, ...), custom_call_target="tpu_custom_call" | custom-call | tf_op jit(solution)/shard_map/feed_forward/pallas_call | solution.py:127
  192.4 38.6 %feed_back.2 = (f32[768,512]{1,0:T(8,128)}, bf16[192,2048]{1,0:T(8,128)(2,1)}, bf16[8,288,768]{2,1,0:T(8,128)(2,1)}, bf16[768,768]{1,0:T(8,128)(2,1)}, f32[768,8]{1,0:T(8,128)}) custom-call(bf16[8,768,256]{2,1,0:T(8,128)(2,1)} %get-tuple-element.94.refs_0_, bf16[2,768,768]{2,1,0:T(8,128)(2,1)} %refs_1_.5, bf16[8,768,256]{2,1,0:T(8,128)(2,1)} %get-tuple-element.98.refs_2_, ...), custom_call_target="tpu_custom_call" | custom-call | tf_op jit(solution)/shard_map/feed_back/pallas_call | solution.py:127
  231.0 35.0 %conv_backward.2 = (bf16[576,2048]{1,0:T(8,128)(2,1)}, bf16[8,48,1024]{2,1,0:T(8,128)(2,1)}, f32[192,768]{1,0:T(8,128)}, f32[192,128]{1,0:T(8,128)}, bf16[2,288,384]{2,1,0:T(8,128)(2,1)}, /*index=5*/f32[192,2048]{1,0:T(8,128)}) custom-call(bf16[192,2048]{1,0:T(8,128)(2,1)} %get-tuple-element.104.refs_0_, f32[576,2048]{1,0:T(8,128)} %get-tuple-element.93.refs_1_, ...), custom_call_target="tpu_custom_call" | custom-call | tf_op jit(solution)/shard_map/conv_backward/pallas_call | solution.py:127
  266.0 27.0 %project_back.2 = (f32[768,512]{1,0:T(8,128)}, bf16[8,96,768]{2,1,0:T(8,128)(2,1)}, f32[768,8]{1,0:T(8,128)}, bf16[2,288,384]{2,1,0:T(8,128)(2,1)}, bf16[2,48,51...) custom-call(bf16[576,2048]{1,0:T(8,128)(2,1)} %get-tuple-element.110.refs_0_, ...), custom_call_target="tpu_custom_call" | custom-call | tf_op jit(solution)/shard_map/project_back/pallas_call | solution.py:127
  292.9 53.0 %feed_back.3 = (f32[768,512]{1,0:T(8,128)}, bf16[192,2048]{1,0:T(8,128)(2,1)}, bf16[8,288,768]{2,1,0:T(8,128)(2,1)}, bf16[768,768]{1,0:T(8,128)(2,1)}, f32[768,8...) custom-call(f32[768,512]{1,0:T(8,128)} %get-tuple-element.116.refs_0_, ...), custom_call_target="tpu_custom_call" | custom-call | tf_op jit(solution)/shard_map/feed_back/pallas_call | solution.py:127
  346.0 34.8 %conv_backward.3 = (bf16[576,2048]{1,0:T(8,128)(2,1)}, bf16[8,48,1024]{2,1,0:T(8,128)(2,1)}, f32[192,768]{1,0:T(8,128)}, f32[192,128]{1,0:T(8,128)}, bf16[2,288,384]{2,1,0:T(8,128)(2,1)}) custom-call(bf16[192,2048]{1,0:T(8,128)(2,1)} %get-tuple-element.128.refs_0_, f32[576,2048]{1,0:T(8,128)} %get-tuple-element.85.refs_1_, ...), custom_call_target="tpu_custom_call" | custom-call | tf_op jit(solution)/shard_map/conv_backward/pallas_call | solution.py:127
  380.8 27.1 %project_back.3 = (f32[768,512]{1,0:T(8,128)}, bf16[8,96,768]{2,1,0:T(8,128)(2,1)}, f32[768,8]{1,0:T(8,128)}, bf16[2,288,384]{2,1,0:T(8,128)(2,1)}, bf16[2,48,51...) custom-call(bf16[576,2048]{1,0:T(8,128)(2,1)} %get-tuple-element.132.refs_0_, ...), custom_call_target="tpu_custom_call" | custom-call | tf_op jit(solution)/shard_map/project_back/pallas_call | solution.py:127
  407.9 37.8 %last_sums.1 = (f32[192,2048]{1,0:T(8,128)}, f32[32,256]{1,0:T(8,128)}, f32[288,768]{1,0:T(8,128)}, f32[48,1024]{1,0:T(8,128)}, f32[96,768]{1,0:T(8,128)}) custom-call(f32[768,512]{1,0:T(8,128)} %get-tuple-element.138.refs_0_, f32[768,8]{1,0:T(8,128)} %get-tuple-element.139.refs_1_, f32[768,8]{1,0:T(8,128)} %get-tuple-element.140.refs_2_, ...), custom_call_target="tpu_custom_call" | custom-call | tf_op jit(solution)/shard_map/last_sums/pallas_call | solution.py:127
  445.8 6.5 %collect.1 = (f32[192,2048]{1,0:T(8,128)}, f32[192,2048]{1,0:T(8,128)}, f32[2,192]{1,0:T(2,128)}, f32[2,192]{1,0:T(2,128)}, f32[2,24,3,768]{3,2,1,0:T(4,128)}, /...) custom-call(f32[192,2048]{1,0:T(8,128)} %get-tuple-element.109.refs_, ...), custom_call_target="tpu_custom_call" | custom-call | tf_op jit(solution)/shard_map/collect/pallas_call | solution.py:1822
  452.3 1.4 copy.33
  453.6 1.9 copy.32

commit v3 on v2

--- a/solution.py
+++ b/solution.py
@@ -239,20 +239,6 @@
     return copies
 
 
-def to_tokens(peers, low, landing, send, recv):
-    shard, half = low.shape[0], landing.shape[1] // 2
-    mine = span(peers[0], shard, 32)
-    copies = [
-        exchange(
-            peers, lambda peer: low.at[:, span(peer * 2 + part, half)],
-            lambda: landing.at[mine, pl.ds(part * half, half)], send.at[part], recv.at[part],
-        )
-        for part in range(2)
-    ]
-    landing[mine, :] = low[:, span(peers[0], 2 * half)]
-    return copies
-
-
 class Track:
     def __init__(self, own, first, last, carry=None):
         self.own, self.first, self.last, self.carry = own, first, last, carry
@@ -409,8 +395,8 @@
 
 
 def first_project_kernel(
-    io, inputs_ref, mix_gain, mix_bias, glu_gain, glu_bias, weight_in, short_in, cond_in,
-    seq_ref, x_ref, gains_ref, full, project_ref, weight_ref, columns_ref, keep_ref,
+    io, inputs_ref, mix_gain, mix_bias, glu_gain, glu_bias, weight_in, short_in, cond_in, up_in,
+    seq_ref, x_ref, gains_ref, full, project_ref, weight_ref, up_ref, columns_ref, keep_ref,
     raw, gains_low, gains_land, turn, send, recv, gains_send, gains_recv,
 ):
     peers = chan_peers()
@@ -451,8 +437,9 @@
     row = lax.broadcasted_iota(jnp.int32, keep_ref.shape, 0)
     within = slot & (seq_ref[0, 0] - 1)
     keep_ref[...] = jnp.where(within > row, 1.0, 0.0)
-    for number in (4, 5, 6):
-        io.flush(number)
+    io.flush(4)
+    io.flush(6)
+    io.flush(7)
     for copy in copies:
         copy.wait()
     turn[...] = jnp.zeros_like(turn)
@@ -460,6 +447,7 @@
         turn[: 4 * layers, :shard] = gains_land[owner]
         gains_ref[owner * shard : (owner + 1) * shard, :] = turn[...].T[:shard]
     io.flush(1)
+    io.ready(8)
     gather(0, 0).wait_recv()
     gather(2, 0).start()
     for part in range(parts):
@@ -480,25 +468,33 @@
         columns = slice(part * half, (part + 1) * half)
         project_ref[:, columns] = matmul(weight_ref[0], full[part])
         io.flush(3, part, (slice(None), pl.ds(part * half, half)))
+        cuts = width // 64
+        lax.fori_loop(
+            cuts * part // parts, cuts * (part + 1) // parts, split_rows(up_ref, up_in, 64, True), 0
+        )
     io.flush(0)
+    io.flush(5)
     for part in range(parts):
         for kind in range(3):
             gather(kind, part).wait_send()
 
 
-def first_project(inputs, gain_arrays, in_proj, short_conv, cond_weight, seq_table, collective):
+def first_project(inputs, gain_arrays, in_proj, short_conv, cond_weight, glu_in, seq_table,
+                  collective):
     shard, slots = inputs.shape
     layers, _, streams, width = in_proj.shape
+    hidden = glu_in[0].shape[3]
     tokens = slots // 4
     return fused_call(
         first_project_kernel,
-        [inputs, *gain_arrays, in_proj, short_conv, cond_weight, seq_table],
+        [inputs, *gain_arrays, in_proj, short_conv, cond_weight, glu_in, seq_table],
         [
             ((width, tokens), F32),
             ((width, 128), F32),
             ((8, width, tokens // 2), BF16),
             ((streams * shard, slots), F32),
             ((layers, streams * shard, width), BF16),
+            ((width, 2 * hidden), BF16),
             ((layers, shard, 128), F32),
             ((8, slots), F32),
         ],
@@ -512,8 +508,8 @@
         + [pltpu.SemaphoreType.DMA((3,))] * 2,
         collective,
         "first_project",
-        (1, 1, 8, 8, 1, 1, 1),
-        8,
+        (1, 1, 8, 8, 1, 1, 1, 1),
+        9,
     )
 
 
@@ -604,7 +600,7 @@
             scatter(2).start()
 
         if ring is not None:
-            ring.advance(step, 8)
+            pl.when(step % 3 == 2)(lambda: ring.advance(step // 3, 4))
         return carry
 
     lax.fori_loop(0, 8, step_body, 0)
@@ -628,37 +624,27 @@
             scatter_copy(peers, buffers, scatter_sems, kind, part).wait_send()
 
 
-def feed_kernel(gain_at, raw, follows, io, gated_ref, x_ref, gains_ref, out_weight, up_columns,
+def feed_kernel(gain_at, follows, io, token_gated, x_ref, gains_ref, out_weight, up_columns,
                 down_weight, *refs):
     refs = list(refs)
     weight_ref, up_in = (refs.pop(0), refs.pop(0)) if follows else (None, None)
-    token_gated, mid_ref, full, next_ref, units, gelus, slopes = refs[:7]
-    refs = refs[7:]
+    mid_ref, full, next_ref, units, gelus, slopes = refs[:6]
+    refs = refs[6:]
     if follows:
         next_full, project_ref, next_up = refs[:3]
         *refs, next_send, next_recv = refs[3:]
-    up_raw, up_columns = (up_columns, refs.pop(0)) if raw else (None, up_columns)
     up_weight, kept, own, *rest = refs
     buffers, sems = rest[:6], rest[6:]
-    send, recv, gather_send, gather_recv, scatter_send, scatter_recv = sems
+    gather_send, gather_recv, scatter_send, scatter_recv = sems
     gather_sems, scatter_sems = (gather_send, gather_recv), (scatter_send, scatter_recv)
     peers = chan_peers()
-    me = peers[0]
+    me, mate, across, _ = peers
     width, tokens = x_ref.shape
     half = tokens // 2
     hidden = down_weight.shape[1]
-    greet(peers[1:])
-    io.ready(0)
-    copies = to_tokens(peers, gated_ref, token_gated, send, recv)
-    io.ready(4)
-    if raw:
-        lax.fori_loop(0, width // 64, split_rows(up_columns, up_raw, 64, True), 0)
-        io.flush(7 + 3 * follows)
-    transpose_columns(up_weight, up_columns, 256)
-    io.ready(1, 2, 3, 5)
+    greet((mate, across))
+    io.ready(0, 1, 2, 3)
     for part in range(2):
-        for copy in copies[part]:
-            copy.wait()
         columns = slice(part * half, (part + 1) * half)
         mid = x_ref[:, columns] + matmul(out_weight[...], token_gated[:, columns])
         mid_ref[:, columns] = mid
@@ -669,7 +655,8 @@
         for kind in range(2):
             gather_copy(block_place(full), peers, gather_sems, kind, part).start()
     io.flush(0)
-    io.flush(1)
+    io.ready(4, 5)
+    transpose_columns(up_weight, up_columns, 256)
 
     def partial(block, step):
         normed = full[block]
@@ -687,7 +674,7 @@
         return matmul(down_weight[...], units[block])
 
     run_blocks(peers, full, gather_sems, scatter_sems, buffers, partial, kept, own)
-    for number in (2, 4, 5, 6):
+    for number in (1, 3, 4, 5):
         io.flush(number)
     if follows:
         io.ready(6, 7)
@@ -708,13 +695,13 @@
             next_full[me * 2 + part] = (normal * gain + bias).astype(BF16)
             for kind in range(2):
                 gather_copy(place, peers, (next_send, next_recv), kind, part).start()
-    io.flush(3)
+    io.flush(2)
     if follows:
-        io.flush(9)
+        io.flush(8)
     drain_gather(peers, full, gather_sems)
     drain_scatter(peers, scatter_sems, buffers)
     if follows:
-        project_blocks(io, peers, next_full, (next_send, next_recv), weight_ref, project_ref, 7, 8)
+        project_blocks(io, peers, next_full, (next_send, next_recv), weight_ref, project_ref, 6, 7)
 
 
 def project_blocks(io, peers, full, sems, weight_ref, project_ref, full_out, project_out):
@@ -744,30 +731,26 @@
             gather(kind, part).wait_send()
 
 
-def feed_forward(gated, values, gains, out_weight, up_columns, down_weight, following, gain_at,
+def feed_forward(token_gated, values, gains, out_weight, up_columns, down_weight, following, gain_at,
                  collective):
     width, tokens = values.shape
     half = tokens // 2
     follows = list(following)
     block = ((8, width, half), BF16)
-    outs = [((width, tokens), BF16), ((width, tokens), F32), block]
+    outs = [((width, tokens), F32), block]
     outs.append(((width, tokens), F32 if follows else BF16))
     hidden = down_weight[0].shape[2]
     outs += [((8, hidden, half), BF16)] * 3
-    parts = [1] * 7
+    parts = [1] * 6
     extra = []
     if follows:
         outs += [block, ((follows[0][0].shape[1], 4 * tokens), F32)]
         outs.append(((width, 2 * hidden), BF16))
         parts += [8, 8, 1]
         extra = [pltpu.SemaphoreType.DMA((3, 2))] * 2
-    raw = up_columns[0].ndim == 4 if isinstance(up_columns, tuple) else False
-    if raw:
-        outs.append(((width, 2 * hidden), BF16))
-        parts.append(1)
     return fused_call(
-        lambda *refs: feed_kernel(gain_at, raw, bool(follows), *refs),
-        [gated, values, gains, out_weight, up_columns, down_weight] + follows,
+        lambda *refs: feed_kernel(gain_at, bool(follows), *refs),
+        [token_gated, values, gains, out_weight, up_columns, down_weight] + follows,
         outs,
         [
             pltpu.VMEM((2 * hidden, width), BF16),
@@ -775,13 +758,11 @@
             pltpu.VMEM((2, width, half), F32),
         ]
         + scatter_buffers(width, half)
-        + [pltpu.SemaphoreType.DMA((2, 3))] * 2
         + [pltpu.SemaphoreType.DMA((3, 2))] * 4
         + extra,
         collective,
         "feed_forward",
         parts,
-        order=(0, 4),
     )
 
 
@@ -916,6 +897,8 @@
     gain = gains_ref[:, gain_at : gain_at + 1]
     for part in range(2):
         feed_grad(part)
+        if rings:
+            ring.advance(2 + part, 4)
         columns = slice(part * half, (part + 1) * half)
         grad = scattered(peers, scatter_sems, buffers, own, part)
         change, product = norm_pullback(grad, mid_ref[:, columns], gain)
@@ -1219,15 +1202,16 @@
 
 
 def conv_forward_kernel(blocks, carries, io, filter_ref, project_ref, columns_ref, keep_ref,
-                        sign_ref, table_ref, seq_ref, carried_in, back_ref, gated_ref, conv_ref, carried,
-                        signal_low, filter_low, signal_bins, filter_spectrum, out_low, convolved,
-                        factor_ref, *sems):
-    shard, slots = gated_ref.shape
+                        sign_ref, table_ref, seq_ref, carried_in, back_ref, token_gated, conv_ref,
+                        carried, gated, signal_low, filter_low, signal_bins, filter_spectrum, out_low,
+                        convolved, factor_ref, send, recv, *sems):
+    shard, slots = gated.shape
     length = slots // blocks
     scale = 1.0 / length
-    steps = shard // 16
+    size = shard // LOADS
     peers = chan_peers()
     me = peers[0]
+    tokens = slots // 4
     parts = carried.shape[0]
     facts = Facts(seq_ref, blocks, length)
     greet(peers[1:])
@@ -1239,7 +1223,7 @@
         )
 
     def forward(first, last):
-        for part in range(parts * first // 8, parts * last // 8):
+        for part in range(parts * first // LOADS, parts * last // LOADS):
             gather(0, part).wait_recv()
             gather(2, part).start()
 
@@ -1254,8 +1238,8 @@
             gather(kind, part).start()
     io.ready(2, 3, 4)
 
-    def prepare(n, carry):
-        rows = n * 16
+    def prepare(base, n, carry):
+        rows = base + n * 16
         signals = []
         for part in range(2):
             here = rows + 8 * part
@@ -1268,28 +1252,17 @@
             _, _, factor = sequence_factor(block_sums(two * two, blocks), cond, facts, blocks)
             for j in range(blocks):
                 factor_ref[eight(here), j : j + 1] = factor[j]
-        store_blocks(signal_low, join(signals), rows, shard, blocks)
+        store_blocks(signal_low, join(signals), n * 16, size, blocks)
         kernel = filter_ref[sixteen(rows), :].astype(BF16)
-        store_blocks(filter_low, kernel, rows, shard, blocks)
+        store_blocks(filter_low, kernel, n * 16, size, blocks)
         return carry
 
-    for n in range(LOADS):
-        io.ready(0, cuts=slice(n, n + 1))
-        io.ready(1, cuts=slice(3 * n, 3 * n + 3))
-        lax.fori_loop(steps * n // LOADS, steps * (n + 1) // LOADS, prepare, 0)
-    io.ready(5)
-    signal_bins[...] = matmul(signal_low[...], table_ref[...])
-    forward(0, 2)
-    filter_spectrum[...] = matmul(filter_low[...], table_ref[...])
-    forward(2, 3)
-
     def combine(n, carry):
-        rows = n * 16
         joined = [[] for _ in range(blocks)]
         for part in range(2):
-            here = rows + 8 * part
-            window = filter_bins(filter_spectrum, sign_ref[0:1, :], here, shard, blocks)
-            signal = plain_bins(signal_bins, here, shard, blocks)
+            here = n * 16 + 8 * part
+            window = filter_bins(filter_spectrum, sign_ref[0:1, :], here, size, blocks)
+            signal = plain_bins(signal_bins, here, size, blocks)
             for i in range(blocks):
                 real = imag = None
                 for j in range(i, -1, -1):
@@ -1303,44 +1276,55 @@
                         real, imag = real + more_real * factor, imag + more_imag * factor
                 joined[i].append(jnp.concatenate([real, imag], axis=1))
         for i in range(blocks):
-            out_low[sixteen(i * shard + rows), :] = join(joined[i])
+            out_low[sixteen(i * size + n * 16), :] = join(joined[i])
         return carry
 
-    lax.fori_loop(0, steps, combine, 0)
-    forward(3, 5)
-    io.ready(8)
-    convolved[...] = matmul(out_low[...], back_ref[...]) * scale
-    forward(5, 6)
-
-    def finish(n, carry):
-        rows = n * 16
-        gated = []
+    def finish(base, n, carry):
+        rows = base + n * 16
+        results = []
         for part in range(2):
             here = rows + 8 * part
             zero = stream_rows(project_ref, columns_ref, keep_ref, here, shard, 0, blocks)
             pieces = []
             for j in range(blocks):
-                source = convolved[eight(j * shard + here), :]
+                source = convolved[eight(j * size + n * 16 + 8 * part), :]
                 columns = slice(j * length, (j + 1) * length)
                 conv_ref[eight(here), columns] = source
                 pieces.append(zero[:, columns] * (source * factor_ref[eight(here), j : j + 1]))
-            gated.append(jnp.concatenate(pieces, axis=1))
-        gated_ref[sixteen(rows), :] = join(gated)
+            results.append(jnp.concatenate(pieces, axis=1))
+        gated[sixteen(rows), :] = join(results)
         return carry
 
-    lax.fori_loop(0, steps // 2, finish, 0)
-    forward(6, 7)
-    top, rest = pl.ds(0, shard // 2), pl.ds(shard // 2, shard // 2)
-    io.flush(0, 0, top)
-    io.flush(1, 0, top)
-    lax.fori_loop(steps // 2, steps, finish, 0)
-    io.flush(0, 1, rest)
-    io.flush(1, 1, rest)
-    forward(7, 8)
+    copies = []
+    for n in range(LOADS):
+        base = n * size
+        io.ready(0, cuts=slice(n, n + 1))
+        io.ready(1, cuts=slice(3 * n, 3 * n + 3))
+        lax.fori_loop(0, size // 16, lambda i, carry: prepare(base, i, carry), 0)
+        if n == 0:
+            io.ready(5)
+        signal_bins[...] = matmul(signal_low[...], table_ref[...])
+        filter_spectrum[...] = matmul(filter_low[...], table_ref[...])
+        lax.fori_loop(0, size // 16, combine, 0)
+        if n == 0:
+            io.ready(8)
+        convolved[...] = matmul(out_low[...], back_ref[...]) * scale
+        lax.fori_loop(0, size // 16, lambda i, carry: finish(base, i, carry), 0)
+        mine = pl.ds(pl.multiple_of(me * shard + base, 16), size)
+        copies += exchange(
+            peers, lambda peer: gated.at[pl.ds(base, size), span(peer, tokens)],
+            lambda: token_gated.at[mine], send.at[n], recv.at[n],
+        )
+        token_gated[mine, :] = gated[base : base + size, span(me, tokens)]
+        io.flush(1, n, pl.ds(base, size))
+        forward(n, n + 1)
     for part in range(parts):
         for kind in (1, 2):
             gather(kind, part).wait_recv()
         io.flush(2, part, part)
+    for copy in copies:
+        copy.wait()
+    io.flush(0)
     for part in range(parts):
         for kind in range(3):
             gather(kind, part).wait_send()
@@ -1351,8 +1335,9 @@
     shard, slots = filter_rows[0].shape[1:]
     width = 4 * shard
     length = slots // blocks
-    low = pltpu.VMEM((blocks * shard, length), BF16)
-    bins = pltpu.VMEM((blocks * shard, 2 * length), F32)
+    rows = blocks * (shard // LOADS)
+    low = pltpu.VMEM((rows, length), BF16)
+    bins = pltpu.VMEM((rows, 2 * length), F32)
     if carries == 1:
         out = ((carried.shape[0], width, width), BF16)
     else:
@@ -1360,20 +1345,22 @@
     return fused_call(
         lambda *refs: conv_forward_kernel(blocks, carries, *refs),
         [filter_rows, project, columns, keep, sign, table, seq_table, carried, back],
-        [((shard, slots), BF16), ((shard, slots), F32), out],
+        [((width, slots // 4), BF16), ((shard, slots), F32), out],
         [
+            pltpu.VMEM((shard, slots), BF16),
             low,
             low,
             bins,
             bins,
-            pltpu.VMEM((blocks * shard, 2 * length), BF16),
-            pltpu.VMEM((blocks * shard, length), F32),
+            pltpu.VMEM((rows, 2 * length), BF16),
+            pltpu.VMEM((rows, length), F32),
             pltpu.VMEM((shard, 128), F32),
         ]
+        + [pltpu.SemaphoreType.DMA((LOADS, 3))] * 2
         + [pltpu.SemaphoreType.DMA((3, out[0][0]))] * 2,
         collective,
         "conv_forward",
-        [2, 2, out[0][0]],
+        [1, LOADS, out[0][0]],
         6,
         (7, 2, 3, 4) + channel_order((1, 0)) + (5, 8),
         {0: channel_cuts(shard, 1), 1: channel_cuts(shard, 3)},
@@ -1854,15 +1841,14 @@
     each = shard // count
     table = jnp.asarray(dft_table(slots // blocks), BF16)
     sign = jnp.asarray(np.tile(1.0 - 2.0 * (np.arange(slots // blocks) % 2), (8, 1)), F32)
-    residual, gains, normed, project, in_rows, columns, keep = first_project(
+    residual, gains, normed, project, in_rows, up_columns, columns, keep = first_project(
         inputs, (mix_gain, mix_bias, glu_gain, glu_bias), in_proj, short_conv, cond_weight,
-        seq_table, 1,
+        (glu_in, 0), seq_table, 1,
     )
-    up_columns = (glu_in, 0)
     constants = (keep, sign, table, seq_table, jnp.asarray(dft_table(slots // blocks).T, BF16))
     kept, state = [], None
     for l in range(layers):
-        gated, conv, carried = conv_forward(
+        token_gated, conv, carried = conv_forward(
             project, (long_filter, l), (columns, l), *constants, cotangent if l else out_proj,
             2 if l else 1, blocks, 10 + l,
         )
@@ -1870,13 +1856,11 @@
             state = carried
         else:
             full_out = carried
-        token_gated, middle, normed_glu, after, *rest = feed_forward(
-            gated, residual, gains, (full_out, l), up_columns, (glu_out, l),
+        middle, normed_glu, after, *rest = feed_forward(
+            token_gated, residual, gains, (full_out, l), up_columns, (glu_out, l),
             ((in_rows, l + 1), (glu_in, l + 1)) if l + 1 < layers else (), 4 * l + 2, 20 + l,
         )
-        saved, follow = rest[:3], rest[3:]
-        up_columns = follow.pop() if l == 0 else up_columns
-        saved = [up_columns] + saved
+        saved, follow = [up_columns] + rest[:3], rest[3:]
         kept.append((residual, normed, project, conv, token_gated, middle, normed_glu, saved))
         residual = after
         if follow:
@@ -1891,8 +1875,8 @@
             saved[1:], waiting, 4 * l + 2, count, 30 + l,
         )
         if waiting:
-            feeds[l + 1], filters[l + 1], packs[l + 1] = large
-        one, two = (count // 4, count // 2) if l else (3 * count // 8, 5 * count // 8)
+            filters[l + 1], packs[l + 1], feeds[l + 1] = large
+        one, two = (3 * count // 8, 5 * count // 8) if l else (count // 2, count - 1)
         project_low, filter_pack, square, row_sums[l], held, *rest = conv_backward(
             gated_grad, project, conv, (long_filter, l), (columns, l), *constants,
             out_grad.reshape(4, shard, width), [Track(feed_grads, 0, one)],
@@ -1900,18 +1884,21 @@
         )
         if top:
             outputs = rest[0]
-        tracks = [Track(feed_grads, one, two, held), Track(filter_pack, 0, two - one)]
+        tracks = [Track(feed_grads, one, two, held), Track(filter_pack, 0, count // 4)]
         state, in_pack, mix_sums, feed_held, held, in_held = project_back(
             project_low, state, before, gains, normed, (in_rows, l), square,
             tracks, 4 * l, 50 + l,
         )
         waiting = [
-            Track(feed_grads, two, count - 1, feed_held),
-            Track(filter_pack, two - one, count - 1, held),
+            Track(filter_pack, count // 4, count - 1, held),
             Track(in_pack, count // 4, count - 1, in_held),
         ]
+        if l:
+            waiting.append(Track(feed_grads, two, count - 1, feed_held))
+        else:
+            feeds[0] = feed_held
         gain_sums[l] = [mix_sums, glu_sums]
-    input_grad, small, feeds[0], filters[0], packs[0] = last_sums(
+    input_grad, small, filters[0], packs[0] = last_sums(
         state, [one for pair in gain_sums for one in pair], row_sums, waiting, 60
     )
     return collect(outputs, input_grad, small, feeds, filters, packs, each)

time: 463 us -> 460 us (level)
  no operation moved by 1% of the time
where the time goes in v3:
time: 460 us; the launch traced here: 452 us
  Pallas kernels  442 us (96%)
  local copies, waits for them, and re-layouts  9.04 us (2%)
    pallas_call x12, Pallas kernels, fused_call(): pl.pallas_call(body, out_shape=tuple((jax.ShapeDtypeStruct(*out) for out...  435 us

profile of v3, /device:TPU:0, one launch (start us, length us, event | category | flops | bytes accessed | tf_op | source)
XLA Modules:
  0.0 451.8 jit_solution(1151154755116619194)
XLA Ops:
  0.6 1.3 copy.31.refs_6_
  2.0 4.4 copy.30.refs_5_
  6.4 29.0 %first_project.1 = (f32[768,512]{1,0:T(8,128)}, f32[768,128]{1,0:T(8,128)}, bf16[8,768,256]{2,1,0:T(8,128)(2,1)}, f32[576,2048]{1,0:T(8,128)}, bf16[2,576,768]{2...) custom-call(bf16[192,2048]{1,0:T(8,128)(2,1)} %refs_0_.3, ...), custom_call_target="tpu_custom_call" | custom-call | tf_op jit(solution)/shard_map/first_project/pallas_call | solution.py:127
  35.4 27.1 %conv_forward.2 = (bf16[768,512]{1,0:T(8,128)(2,1)}, f32[192,2048]{1,0:T(8,128)}, bf16[2,768,768]{2,1,0:T(8,128)(2,1)}) custom-call(f32[2,192,2048]{2,1,0:T(8,128)} %refs_3_.5, f32[576,2048]{1,0:T(8,128)} %get-tuple-element.82.refs_1_, f32[2,192,128]{2,1,0:T(8,128)} %get-tuple-element.83.refs_2_.refs_4_, f32[8,2048]{1,0:T(8,128)} %get-tuple-element.84.refs_3_.refs_5_, ...), custom_call_target="tpu_custom_call" | custom-call | tf_op jit(solution)/shard_map/conv_forward/pallas_call | solution.py:127
  62.5 59.2 %feed_forward.2 = (f32[768,512]{1,0:T(8,128)}, bf16[8,768,256]{2,1,0:T(8,128)(2,1)}, f32[768,512]{1,0:T(8,128)}, bf16[8,768,256]{2,1,0:T(8,128)(2,1)}, bf16[8,76...) custom-call(bf16[768,512]{1,0:T(8,128)(2,1)} %get-tuple-element.85.r, ...), custom_call_target="tpu_custom_call" | custom-call | tf_op jit(solution)/shard_map/feed_forward/pallas_call | solution.py:127
  121.7 33.0 %conv_forward.3 = (bf16[768,512]{1,0:T(8,128)(2,1)}, f32[192,2048]{1,0:T(8,128)}, bf16[8,768,256]{2,1,0:T(8,128)(2,1)}) custom-call(f32[2,192,2048]{2,1,0:T(8,128)} %refs_3_.5, f32[576,2048]{1,0:T(8,128)} %get-tuple-element.91.refs_1_, f32[2,192,128]{2,1,0:T(8,128)} %get-tuple-element.83.refs_2_.refs_4_, f32[8,2048]{1,0:T(8,128)} %get-tuple-element.84.refs_3_.refs_5_, ...), custom_call_target="tpu_custom_call" | custom-call | tf_op jit(solution)/shard_map/conv_forward/pallas_call | solution.py:127
  154.7 40.4 %feed_forward.3 = (f32[768,512]{1,0:T(8,128)}, bf16[8,768,256]{2,1,0:T(8,128)(2,1)}, bf16[768,512]{1,0:T(8,128)(2,1)}, bf16[8,768,256]{2,1,0:T(8,128)(2,1)}, bf1...) custom-call(bf16[768,512]{1,0:T(8,128)(2,1)} %get-tuple-element.93.refs_0_.refs_8_, ...), custom_call_target="tpu_custom_call" | custom-call | tf_op jit(solution)/shard_map/feed_forward/pallas_call | solution.py:127
  195.1 38.0 %feed_back.2 = (f32[768,512]{1,0:T(8,128)}, bf16[192,2048]{1,0:T(8,128)(2,1)}, bf16[8,288,768]{2,1,0:T(8,128)(2,1)}, bf16[768,768]{1,0:T(8,128)(2,1)}, f32[768,8]{1,0:T(8,128)}) custom-call(bf16[8,768,256]{2,1,0:T(8,128)(2,1)} %get-tuple-element.92.refs_0_, bf16[2,768,768]{2,1,0:T(8,128)(2,1)} %refs_1_.5, bf16[8,768,256]{2,1,0:T(8,128)(2,1)} %get-tuple-element.96.refs_2_, ...), custom_call_target="tpu_custom_call" | custom-call | tf_op jit(solution)/shard_map/feed_back/pallas_call | solution.py:127
  233.1 35.4 %conv_backward.2 = (bf16[576,2048]{1,0:T(8,128)(2,1)}, bf16[8,48,1024]{2,1,0:T(8,128)(2,1)}, f32[192,768]{1,0:T(8,128)}, f32[192,128]{1,0:T(8,128)}, bf16[2,288,384]{2,1,0:T(8,128)(2,1)}, /*index=5*/f32[192,2048]{1,0:T(8,128)}) custom-call(bf16[192,2048]{1,0:T(8,128)(2,1)} %get-tuple-element.101.refs_0_, f32[576,2048]{1,0:T(8,128)} %get-tuple-element.91.refs_1_, ...), custom_call_target="tpu_custom_call" | custom-call | tf_op jit(solution)/shard_map/conv_backward/pallas_call | solution.py:127
  268.5 27.0 %project_back.2 = (f32[768,512]{1,0:T(8,128)}, bf16[8,96,768]{2,1,0:T(8,128)(2,1)}, f32[768,8]{1,0:T(8,128)}, bf16[2,288,384]{2,1,0:T(8,128)(2,1)}, bf16[2,48,51...) custom-call(bf16[576,2048]{1,0:T(8,128)(2,1)} %get-tuple-element.107.refs_0_, ...), custom_call_target="tpu_custom_call" | custom-call | tf_op jit(solution)/shard_map/project_back/pallas_call | solution.py:127
  295.5 49.8 %feed_back.3 = (f32[768,512]{1,0:T(8,128)}, bf16[192,2048]{1,0:T(8,128)(2,1)}, bf16[8,288,768]{2,1,0:T(8,128)(2,1)}, bf16[768,768]{1,0:T(8,128)(2,1)}, f32[768,8...) custom-call(f32[768,512]{1,0:T(8,128)} %get-tuple-element.113.refs_0_, ...), custom_call_target="tpu_custom_call" | custom-call | tf_op jit(solution)/shard_map/feed_back/pallas_call | solution.py:127
  345.3 37.5 %conv_backward.3 = (bf16[576,2048]{1,0:T(8,128)(2,1)}, bf16[8,48,1024]{2,1,0:T(8,128)(2,1)}, f32[192,768]{1,0:T(8,128)}, f32[192,128]{1,0:T(8,128)}, bf16[2,288,384]{2,1,0:T(8,128)(2,1)}) custom-call(bf16[192,2048]{1,0:T(8,128)(2,1)} %get-tuple-element.123.refs_0_, f32[576,2048]{1,0:T(8,128)} %get-tuple-element.82.refs_1_, ...), custom_call_target="tpu_custom_call" | custom-call | tf_op jit(solution)/shard_map/conv_backward/pallas_call | solution.py:127
  382.9 30.9 %project_back.3 = (f32[768,512]{1,0:T(8,128)}, bf16[8,96,768]{2,1,0:T(8,128)(2,1)}, f32[768,8]{1,0:T(8,128)}, f32[288,768]{1,0:T(8,128)}, bf16[2,48,512]{2,1,0:T(8,128)(2,1)}, /*index=5*/bf16[2,96,384]{2,1,0:T(8,128)(2,1)}) custom-call(bf16[576,2048]{1,0:T(8,128)(2,1)} %get-tuple-element.127.refs_0_, bf16[2,576,768]{2,1,0:T(8,128)(2,1)} %get-tuple-element.90.refs_6_.refs_1_, ...), custom_call_target="tpu_custom_call" | custom-call | tf_op jit(solution)/shard_map/project_back/pallas_call | solution.py:127
  413.8 27.8 %last_sums.1 = (f32[192,2048]{1,0:T(8,128)}, f32[32,256]{1,0:T(8,128)}, f32[48,1024]{1,0:T(8,128)}, f32[96,768]{1,0:T(8,128)}) custom-call(f32[768,512]{1,0:T(8,128)} %get-tuple-element.133.refs_0_, f32[768,8]{1,0:T(8,128)} %get-tuple-element.134.refs_1_, f32[768,8]{1,0:T(8,128)} %get-tuple-element.135.refs_2_, f32[768,8]{1,0:T(8,128)} %get-tuple-element.136.refs_3_, ...), custom_call_target="tpu_custom_call" | custom-call | tf_op jit(solution)/shard_map/last_sums/pallas_call | solution.py:127
  441.6 6.5 %collect.1 = (f32[192,2048]{1,0:T(8,128)}, f32[192,2048]{1,0:T(8,128)}, f32[2,192]{1,0:T(2,128)}, f32[2,192]{1,0:T(2,128)}, f32[2,24,3,768]{3,2,1,0:T(4,128)}, /...) custom-call(f32[192,2048]{1,0:T(8,128)} %get-tuple-element.106.refs_, ...), custom_call_target="tpu_custom_call" | custom-call | tf_op jit(solution)/shard_map/collect/pallas_call | solution.py:1809
  448.1 1.4 copy.33
  449.5 1.9 copy.32

commit v4 on v3

--- a/solution.py
+++ b/solution.py
@@ -1117,10 +1117,14 @@
 
 
 def eight(rows):
+    if isinstance(rows, int):
+        return pl.ds(rows, 8)
     return pl.ds(pl.multiple_of(rows, 8), 8)
 
 
 def sixteen(rows):
+    if isinstance(rows, int):
+        return pl.ds(rows, 16)
     return pl.ds(pl.multiple_of(rows, 16), 16)
 
 
@@ -1201,10 +1205,29 @@
     return tuple(order)
 
 
+def run_groups(prepare, transform, combine, invert, finish, after):
+    prepare(0)
+    for i in range(LOADS + 1):
+        if i < LOADS:
+            transform(i)
+        if i + 1 < LOADS:
+            prepare(i + 1)
+        if i:
+            invert(i - 1)
+        if i < LOADS:
+            combine(i)
+        if i:
+            finish(i - 1)
+            after(i - 1)
+
+
 def conv_forward_kernel(blocks, carries, io, filter_ref, project_ref, columns_ref, keep_ref,
                         sign_ref, table_ref, seq_ref, carried_in, back_ref, token_gated, conv_ref,
-                        carried, gated, signal_low, filter_low, signal_bins, filter_spectrum, out_low,
-                        convolved, factor_ref, send, recv, *sems):
+                        carried, gated, factor_ref, *refs):
+    signal_low, filter_low, signal_bins, filter_spectrum, out_low, convolved = (
+        refs[2 * n : 2 * n + 2] for n in range(6)
+    )
+    send, recv, *sems = refs[12:]
     shard, slots = gated.shape
     length = slots // blocks
     scale = 1.0 / length
@@ -1238,86 +1261,97 @@
             gather(kind, part).start()
     io.ready(2, 3, 4)
 
-    def prepare(base, n, carry):
-        rows = base + n * 16
-        signals = []
-        for part in range(2):
-            here = rows + 8 * part
-            one, two = (
-                stream_rows(project_ref, columns_ref, keep_ref, here, shard, stream, blocks)
-                for stream in (1, 2)
+    def prepare(group):
+        base, place = group * size, group % 2
+        if group < 2:
+            cuts = slice(0, 1) if group == 0 else slice(1, LOADS)
+            io.ready(0, cuts=cuts)
+            io.ready(1, cuts=slice(3 * cuts.start, 3 * cuts.stop))
+        for n in range(size // 16):
+            rows = base + n * 16
+            signals = []
+            for part in range(2):
+                here = rows + 8 * part
+                one, two = (
+                    stream_rows(project_ref, columns_ref, keep_ref, here, shard, stream, blocks)
+                    for stream in (1, 2)
+                )
+                signals.append(one * two)
+                cond = columns_ref[eight(here), 9:10]
+                _, _, factor = sequence_factor(block_sums(two * two, blocks), cond, facts, blocks)
+                for j in range(blocks):
+                    factor_ref[eight(here), j : j + 1] = factor[j]
+            store_blocks(signal_low[place], join(signals), n * 16, size, blocks)
+            kernel = filter_ref[sixteen(rows), :].astype(BF16)
+            store_blocks(filter_low[place], kernel, n * 16, size, blocks)
+
+    def transform(group):
+        place = group % 2
+        if group == 0:
+            io.ready(5, 8)
+        signal_bins[place][...] = matmul(signal_low[place][...], table_ref[...])
+        filter_spectrum[place][...] = matmul(filter_low[place][...], table_ref[...])
+
+    def combine(group):
+        place = group % 2
+        for n in range(size // 16):
+            joined = [[] for _ in range(blocks)]
+            for part in range(2):
+                here = n * 16 + 8 * part
+                window = filter_bins(filter_spectrum[place], sign_ref[0:1, :], here, size, blocks)
+                signal = plain_bins(signal_bins[place], here, size, blocks)
+                for i in range(blocks):
+                    real = imag = None
+                    for j in range(i, -1, -1):
+                        fr, fi = window[i - j]
+                        sr, si = signal[j]
+                        more_real, more_imag = fr * sr - fi * si, fr * si + fi * sr
+                        if j == i:
+                            real, imag = more_real, more_imag
+                        else:
+                            factor = facts.same[i][j]
+                            real, imag = real + more_real * factor, imag + more_imag * factor
+                    joined[i].append(jnp.concatenate([real, imag], axis=1))
+            for i in range(blocks):
+                out_low[place][sixteen(i * size + n * 16), :] = join(joined[i])
+
+    def invert(group):
+        place = group % 2
+        convolved[place][...] = matmul(out_low[place][...], back_ref[...]) * scale
+
+    def finish(group):
+        base, place = group * size, group % 2
+        for n in range(size // 16):
+            rows = base + n * 16
+            results = []
+            for part in range(2):
+                here = rows + 8 * part
+                zero = stream_rows(project_ref, columns_ref, keep_ref, here, shard, 0, blocks)
+                pieces = []
+                for j in range(blocks):
+                    source = convolved[place][eight(j * size + n * 16 + 8 * part), :]
+                    columns = slice(j * length, (j + 1) * length)
+                    conv_ref[eight(here), columns] = source
+                    pieces.append(zero[:, columns] * (source * factor_ref[eight(here), j : j + 1]))
+                results.append(jnp.concatenate(pieces, axis=1))
+            gated[sixteen(rows), :] = join(results)
+
+    copies = []
+
+    def after(group):
+        base = group * size
+        mine = pl.ds(pl.multiple_of(me * shard + base, 16), size)
+        copies.extend(
+            exchange(
+                peers, lambda peer: gated.at[pl.ds(base, size), span(peer, tokens)],
+                lambda: token_gated.at[mine], send.at[group], recv.at[group],
             )
-            signals.append(one * two)
-            cond = columns_ref[eight(here), 9:10]
-            _, _, factor = sequence_factor(block_sums(two * two, blocks), cond, facts, blocks)
-            for j in range(blocks):
-                factor_ref[eight(here), j : j + 1] = factor[j]
-        store_blocks(signal_low, join(signals), n * 16, size, blocks)
-        kernel = filter_ref[sixteen(rows), :].astype(BF16)
-        store_blocks(filter_low, kernel, n * 16, size, blocks)
-        return carry
-
-    def combine(n, carry):
-        joined = [[] for _ in range(blocks)]
-        for part in range(2):
-            here = n * 16 + 8 * part
-            window = filter_bins(filter_spectrum, sign_ref[0:1, :], here, size, blocks)
-            signal = plain_bins(signal_bins, here, size, blocks)
-            for i in range(blocks):
-                real = imag = None
-                for j in range(i, -1, -1):
-                    fr, fi = window[i - j]
-                    sr, si = signal[j]
-                    more_real, more_imag = fr * sr - fi * si, fr * si + fi * sr
-                    if j == i:
-                        real, imag = more_real, more_imag
-                    else:
-                        factor = facts.same[i][j]
-                        real, imag = real + more_real * factor, imag + more_imag * factor
-                joined[i].append(jnp.concatenate([real, imag], axis=1))
-        for i in range(blocks):
-            out_low[sixteen(i * size + n * 16), :] = join(joined[i])
-        return carry
-
-    def finish(base, n, carry):
-        rows = base + n * 16
-        results = []
-        for part in range(2):
-            here = rows + 8 * part
-            zero = stream_rows(project_ref, columns_ref, keep_ref, here, shard, 0, blocks)
-            pieces = []
-            for j in range(blocks):
-                source = convolved[eight(j * size + n * 16 + 8 * part), :]
-                columns = slice(j * length, (j + 1) * length)
-                conv_ref[eight(here), columns] = source
-                pieces.append(zero[:, columns] * (source * factor_ref[eight(here), j : j + 1]))
-            results.append(jnp.concatenate(pieces, axis=1))
-        gated[sixteen(rows), :] = join(results)
-        return carry
-
-    copies = []
-    for n in range(LOADS):
-        base = n * size
-        io.ready(0, cuts=slice(n, n + 1))
-        io.ready(1, cuts=slice(3 * n, 3 * n + 3))
-        lax.fori_loop(0, size // 16, lambda i, carry: prepare(base, i, carry), 0)
-        if n == 0:
-            io.ready(5)
-        signal_bins[...] = matmul(signal_low[...], table_ref[...])
-        filter_spectrum[...] = matmul(filter_low[...], table_ref[...])
-        lax.fori_loop(0, size // 16, combine, 0)
-        if n == 0:
-            io.ready(8)
-        convolved[...] = matmul(out_low[...], back_ref[...]) * scale
-        lax.fori_loop(0, size // 16, lambda i, carry: finish(base, i, carry), 0)
-        mine = pl.ds(pl.multiple_of(me * shard + base, 16), size)
-        copies += exchange(
-            peers, lambda peer: gated.at[pl.ds(base, size), span(peer, tokens)],
-            lambda: token_gated.at[mine], send.at[n], recv.at[n],
         )
         token_gated[mine, :] = gated[base : base + size, span(me, tokens)]
-        io.flush(1, n, pl.ds(base, size))
-        forward(n, n + 1)
+        io.flush(1, group, pl.ds(base, size))
+        forward(group, group + 1)
+
+    run_groups(prepare, transform, combine, invert, finish, after)
     for part in range(parts):
         for kind in (1, 2):
             gather(kind, part).wait_recv()
@@ -1348,14 +1382,12 @@
         [((width, slots // 4), BF16), ((shard, slots), F32), out],
         [
             pltpu.VMEM((shard, slots), BF16),
-            low,
-            low,
-            bins,
-            bins,
-            pltpu.VMEM((rows, 2 * length), BF16),
-            pltpu.VMEM((rows, length), F32),
             pltpu.VMEM((shard, 128), F32),
         ]
+        + [low] * 4
+        + [bins] * 4
+        + [pltpu.VMEM((rows, 2 * length), BF16)] * 2
+        + [pltpu.VMEM((rows, length), F32)] * 2
         + [pltpu.SemaphoreType.DMA((LOADS, 3))] * 2
         + [pltpu.SemaphoreType.DMA((3, out[0][0]))] * 2,
         collective,
@@ -1385,9 +1417,13 @@
     sources = [io.source[10 + n] for n in range(inputs)]
     ring = Ring(tracks, ring_in, large, refs[-rings - 2 :], sources)
     refs = refs[: -rings - 2]
-    signal_low, filter_low, grad_low, signal_bins, filter_spectrum, grad_bins, *refs = refs
-    signal_out, filter_out, mixed, energy_ref, square_land, square_send, square_recv = refs
-    signal_grad = filter_spectrum.at[:, : filter_spectrum.shape[1] // 2]
+    mixed, energy_ref, square_land, square_send, square_recv, *pairs = refs
+    signal_low, filter_low, grad_low, signal_bins, filter_spectrum, grad_bins = (
+        pairs[2 * n : 2 * n + 2] for n in range(6)
+    )
+    signal_out, filter_out, signal_grad, filter_grad = (
+        pairs[2 * n : 2 * n + 2] for n in range(6, 10)
+    )
     peers = chan_peers()
     greet(peers[1:], ring.toward)
     ring.start()
@@ -1406,163 +1442,178 @@
     steps = shard // 16
     facts = Facts(seq_ref, blocks, length)
 
-    def prepare(n, carry):
-        rows = n * 16
-        signals, scaled = [], []
-        grads = grad_ref[sixteen(rows), :].astype(F32)
-        for part in range(2):
-            here = rows + 8 * part
-            zero, one, two = (
-                stream_rows(project_ref, columns_ref, keep_ref, here, shard, stream, blocks)
-                for stream in range(3)
-            )
-            mixed[0, eight(here), :] = one
-            mixed[1, eight(here), :] = two
-            signals.append(one * two)
-            cond = columns_ref[eight(here), 9:10]
-            power = block_sums(two * two, blocks)
-            energy, logs, factor = sequence_factor(power, cond, facts, blocks)
-            conv_grad = grads[8 * part : 8 * part + 8] * zero
-            factor_grad = block_sums(conv_grad * conv_ref[eight(here), :], blocks)
-            cond_grad = 0.0
+    size = shard // LOADS
+
+    def prepare(group):
+        base, place = group * size, group % 2
+        if group < 2:
+            cuts = slice(0, 1) if group == 0 else slice(1, LOADS)
+            for number, each in ((0, 1), (1, 3), (2, 1), (3, 1)):
+                io.ready(number, cuts=slice(each * cuts.start, each * cuts.stop))
+        for n in range(size // 16):
+            rows = base + n * 16
+            signals, scaled = [], []
+            grads = grad_ref[sixteen(rows), :].astype(F32)
+            for part in range(2):
+                here = rows + 8 * part
+                zero, one, two = (
+                    stream_rows(project_ref, columns_ref, keep_ref, here, shard, stream, blocks)
+                    for stream in range(3)
+                )
+                mixed[0, eight(here), :] = one
+                mixed[1, eight(here), :] = two
+                signals.append(one * two)
+                cond = columns_ref[eight(here), 9:10]
+                power = block_sums(two * two, blocks)
+                energy, logs, factor = sequence_factor(power, cond, facts, blocks)
+                conv_grad = grads[8 * part : 8 * part + 8] * zero
+                factor_grad = block_sums(conv_grad * conv_ref[eight(here), :], blocks)
+                cond_grad = 0.0
+                for j in range(blocks):
+                    cond_grad = cond_grad + factor_grad[j] * logs[j]
+                sums_ref[eight(here), 9:10] = cond_grad
+                for i in range(blocks):
+                    total = 0.0
+                    for j in range(blocks):
+                        total = total + factor_grad[j] * facts.same[i][j]
+                    energy_ref[eight(here), i : i + 1] = (
+                        total * cond / (1.0 + energy[i]) * (2.0 * facts.inverse)
+                    )
+                    energy_ref[eight(here), blocks + i : blocks + i + 1] = factor[i]
+                scaled.append(
+                    conv_grad * spread_blocks([value * scale for value in factor], length)
+                )
+            store_blocks(signal_low[place], join(signals), n * 16, size, blocks)
+            store_blocks(grad_low[place], join(scaled), n * 16, size, blocks)
+            kernel = filter_ref[sixteen(rows), :].astype(BF16)
+            store_blocks(filter_low[place], kernel, n * 16, size, blocks)
+
+    def transform(group):
+        place = group % 2
+        if group == 0:
+            io.ready(7, 10 + inputs + with_outputs)
+        grad_bins[place][...] = matmul(grad_low[place][...], table_ref[...])
+        signal_bins[place][...] = matmul(signal_low[place][...], table_ref[...])
+        filter_spectrum[place][...] = matmul(filter_low[place][...], table_ref[...])
+
+    def combine(group):
+        place = group % 2
+        sign = sign_ref[0:1, :]
+        for n in range(size // 16):
+            joined = [[] for _ in range(blocks)]
+            windows = [[] for _ in range(blocks)]
+            for part in range(2):
+                here = n * 16 + 8 * part
+                window = filter_bins(filter_spectrum[place], sign, here, size, blocks)
+                signal = plain_bins(signal_bins[place], here, size, blocks)
+                grads = plain_bins(grad_bins[place], here, size, blocks)
+                for j in range(blocks):
+                    for i in range(j, blocks):
+                        fr, fi = window[i - j]
+                        gr, gi = grads[i]
+                        more_real, more_imag = fr * gr + fi * gi, fr * gi - fi * gr
+                        if i == j:
+                            real, imag = more_real, more_imag
+                        else:
+                            factor = facts.same[i][j]
+                            real, imag = real + more_real * factor, imag + more_imag * factor
+                    joined[j].append(jnp.concatenate([real, imag], axis=1))
+                after = None
+                for k in reversed(range(blocks)):
+                    real = imag = None
+                    for j in range(blocks - k):
+                        sr, si = signal[j]
+                        gr, gi = grads[j + k]
+                        more_real, more_imag = sr * gr + si * gi, sr * gi - si * gr
+                        if k:
+                            factor = facts.same[j + k][j]
+                            more_real, more_imag = more_real * factor, more_imag * factor
+                        real = more_real if real is None else real + more_real
+                        imag = more_imag if imag is None else imag + more_imag
+                    if after is None:
+                        whole = (real, imag)
+                    else:
+                        whole = (real + sign * after[1], imag - sign * after[0])
+                    windows[k].append(jnp.concatenate(whole, axis=1))
+                    after = (real, imag)
             for j in range(blocks):
-                cond_grad = cond_grad + factor_grad[j] * logs[j]
-            sums_ref[eight(here), 9:10] = cond_grad
-            for i in range(blocks):
-                total = 0.0
-                for j in range(blocks):
-                    total = total + factor_grad[j] * facts.same[i][j]
-                energy_ref[eight(here), i : i + 1] = (
-                    total * cond / (1.0 + energy[i]) * (2.0 * facts.inverse)
-                )
-                energy_ref[eight(here), blocks + i : blocks + i + 1] = factor[i]
-            scaled.append(conv_grad * spread_blocks([one * scale for one in factor], length))
-        store_blocks(signal_low, join(signals), rows, shard, blocks)
-        store_blocks(grad_low, join(scaled), rows, shard, blocks)
-        kernel = filter_ref[sixteen(rows), :].astype(BF16)
-        store_blocks(filter_low, kernel, rows, shard, blocks)
-        return carry
-
-    for n in range(LOADS):
-        for number, each in ((0, 1), (1, 3), (2, 1), (3, 1)):
-            io.ready(number, cuts=slice(n * each, (n + 1) * each))
-        lax.fori_loop(steps * n // LOADS, steps * (n + 1) // LOADS, prepare, 0)
-    io.ready(7)
-    io.ready(*range(10, 10 + rings))
-    grad_bins[...] = matmul(grad_low[...], table_ref[...])
-    signal_bins[...] = matmul(signal_low[...], table_ref[...])
-    filter_spectrum[...] = matmul(filter_low[...], table_ref[...])
-    ring.advance(0, 3)
-
-    def combine(n, carry):
-        rows = n * 16
-        sign = sign_ref[0:1, :]
-        joined = [[] for _ in range(blocks)]
-        windows = [[] for _ in range(blocks)]
-        for part in range(2):
-            here = rows + 8 * part
-            window = filter_bins(filter_spectrum, sign, here, shard, blocks)
-            signal = plain_bins(signal_bins, here, shard, blocks)
-            grads = plain_bins(grad_bins, here, shard, blocks)
-            for j in range(blocks):
-                for i in range(j, blocks):
-                    fr, fi = window[i - j]
-                    gr, gi = grads[i]
-                    more_real, more_imag = fr * gr + fi * gi, fr * gi - fi * gr
-                    if i == j:
-                        real, imag = more_real, more_imag
-                    else:
-                        factor = facts.same[i][j]
-                        real, imag = real + more_real * factor, imag + more_imag * factor
-                joined[j].append(jnp.concatenate([real, imag], axis=1))
-            after = None
-            for k in reversed(range(blocks)):
-                real = imag = None
-                for j in range(blocks - k):
-                    sr, si = signal[j]
-                    gr, gi = grads[j + k]
-                    more_real, more_imag = sr * gr + si * gi, sr * gi - si * gr
-                    if k:
-                        factor = facts.same[j + k][j]
-                        more_real, more_imag = more_real * factor, more_imag * factor
-                    real = more_real if real is None else real + more_real
-                    imag = more_imag if imag is None else imag + more_imag
-                if after is None:
-                    whole = (real, imag)
-                else:
-                    whole = (real + sign * after[1], imag - sign * after[0])
-                windows[k].append(jnp.concatenate(whole, axis=1))
-                after = (real, imag)
-        for j in range(blocks):
-            signal_out[sixteen(j * shard + rows), :] = join(joined[j])
-            filter_out[sixteen(j * shard + rows), :] = join(windows[j])
-        return carry
-
-    lax.fori_loop(0, steps, combine, 0)
-    io.ready(10 + inputs + with_outputs)
-    signal_grad[...] = matmul(signal_out[...], back_ref[...])
-    ring.advance(1, 3)
-    filter_rows = matmul(filter_out[...], back_ref[...])
+                signal_out[place][sixteen(j * size + n * 16), :] = join(joined[j])
+                filter_out[place][sixteen(j * size + n * 16), :] = join(windows[j])
+
     count, pack_rows, lanes = filter_pack.shape
     each = shard // count
     stack = slots // lanes
     if pack_rows > stack * each:
         filter_pack[...] = jnp.zeros_like(filter_pack)
-    for chunk in range(count):
-        lags = [
-            filter_rows[j * shard + chunk * each : j * shard + (chunk + 1) * each]
-            for j in range(blocks)
-        ]
-        layers = [
-            jnp.concatenate(lags[n * blocks // stack : (n + 1) * blocks // stack], axis=1)
-            for n in range(stack)
-        ]
-        value = layers[0] if stack == 1 else jnp.concatenate(layers, axis=0)
-        filter_pack[chunk, : stack * each] = value.astype(BF16)
+
+    def invert(group):
+        place = group % 2
+        signal_grad[place][...] = matmul(signal_out[place][...], back_ref[...])
+        filter_grad[place][...] = matmul(filter_out[place][...], back_ref[...])
+
+    def finish(group):
+        base, place = group * size, group % 2
+        for chunk in range(size // each):
+            lags = [
+                filter_grad[place][j * size + chunk * each : j * size + (chunk + 1) * each, :]
+                for j in range(blocks)
+            ]
+            layers = [
+                jnp.concatenate(lags[n * blocks // stack : (n + 1) * blocks // stack], axis=1)
+                for n in range(stack)
+            ]
+            value = layers[0] if stack == 1 else jnp.concatenate(layers, axis=0)
+            filter_pack[base // each + chunk, : stack * each] = value.astype(BF16)
+        for n in range(size // 16):
+            rows = base + n * 16
+            totals = [[] for _ in range(3)]
+            outer = grad_ref[sixteen(rows), :].astype(F32)
+            for part in range(2):
+                here = rows + 8 * part
+                local = eight(here)
+                factor = [energy_ref[local, blocks + i : blocks + i + 1] for i in range(blocks)]
+                energy = [energy_ref[local, i : i + 1] for i in range(blocks)]
+                signal = jnp.concatenate(
+                    [
+                        signal_grad[place][eight(j * size + n * 16 + 8 * part), :]
+                        for j in range(blocks)
+                    ],
+                    axis=1,
+                )
+                for stream in range(3):
+                    if stream == 0:
+                        value = outer[8 * part : 8 * part + 8] * (
+                            conv_ref[local, :] * spread_blocks(factor, length)
+                        )
+                    elif stream == 1:
+                        value = signal * mixed[1, local, :]
+                    else:
+                        value = signal * mixed[0, local, :] + (
+                            spread_blocks(energy, length) * mixed[1, local, :]
+                        )
+                    plain = project_ref[eight(stream * shard + here), :]
+                    total = value * columns_ref[local, stream : stream + 1]
+                    sums_ref[local, stream : stream + 1] = lane_sums(value * plain)
+                    for offset in (1, 2):
+                        column = 3 * offset + stream
+                        moved = pltpu.roll(
+                            mask_heads(value, keep_ref[offset - 1 : offset, :], blocks),
+                            slots - offset, 1,
+                        )
+                        sums_ref[local, column : column + 1] = lane_sums(moved * plain)
+                        total = total + moved * columns_ref[local, column : column + 1]
+                    totals[stream].append(total)
+            for stream in range(3):
+                project_grad[sixteen(stream * shard + rows), :] = join(totals[stream])
+
+    def after(group):
+        if group == 0:
+            io.ready(*range(10, 10 + rings))
+        if group < 3:
+            ring.advance(group, 3)
+
+    run_groups(prepare, transform, combine, invert, finish, after)
     io.flush(1)
-
-    def finish(n, carry):
-        rows = n * 16
-        totals = [[] for _ in range(3)]
-        outer = grad_ref[sixteen(rows), :].astype(F32)
-        for part in range(2):
-            here = rows + 8 * part
-            local = eight(here)
-            factor = [energy_ref[local, blocks + i : blocks + i + 1] for i in range(blocks)]
-            energy = [energy_ref[local, i : i + 1] for i in range(blocks)]
-            signal = jnp.concatenate(
-                [signal_grad[eight(j * shard + here), :] for j in range(blocks)], axis=1
-            )
-            for stream in range(3):
-                if stream == 0:
-                    value = outer[8 * part : 8 * part + 8] * (
-                        conv_ref[local, :] * spread_blocks(factor, length)
-                    )
-                elif stream == 1:
-                    value = signal * mixed[1, local, :]
-                else:
-                    value = signal * mixed[0, local, :] + (
-                        spread_blocks(energy, length) * mixed[1, local, :]
-                    )
-                plain = project_ref[eight(stream * shard + here), :]
-                total = value * columns_ref[local, stream : stream + 1]
-                sums_ref[local, stream : stream + 1] = lane_sums(value * plain)
-                for offset in (1, 2):
-                    column = 3 * offset + stream
-                    moved = pltpu.roll(
-                        mask_heads(value, keep_ref[offset - 1 : offset, :], blocks),
-                        slots - offset, 1,
-                    )
-                    sums_ref[local, column : column + 1] = lane_sums(moved * plain)
-                    total = total + moved * columns_ref[local, column : column + 1]
-                totals[stream].append(total)
-        for stream in range(3):
-            project_grad[sixteen(stream * shard + rows), :] = join(totals[stream])
-        return carry
-
-    lax.fori_loop(0, steps // 2, finish, 0)
-    ring.advance(2, 3)
-    lax.fori_loop(steps // 2, steps, finish, 0)
     for stream in range(3):
         io.flush(0, stream, pl.ds(stream * shard, shard))
     for copy in copies:
@@ -1595,9 +1646,11 @@
                   tracks, residual, blocks, collective):
     shard, slots = filter_rows[0].shape[1:]
     length = slots // blocks
-    low = pltpu.VMEM((blocks * shard, length), BF16)
-    bins = pltpu.VMEM((blocks * shard, 2 * length), F32)
-    out = pltpu.VMEM((blocks * shard, 2 * length), BF16)
+    rows = blocks * (shard // LOADS)
+    low = pltpu.VMEM((rows, length), BF16)
+    bins = pltpu.VMEM((rows, 2 * length), F32)
+    out = pltpu.VMEM((rows, 2 * length), BF16)
+    back_out = pltpu.VMEM((rows, length), F32)
     outs, extra = [], []
     if residual:
         outs = [((shard, slots), F32)]
@@ -1616,10 +1669,13 @@
         ]
         + [one.out() for one in tracks]
         + outs,
-        [low, low, low, bins, bins, bins, out, out]
-        + [pltpu.VMEM((2, shard, slots), F32), pltpu.VMEM((shard, 128), F32)]
+        [pltpu.VMEM((2, shard, slots), F32), pltpu.VMEM((shard, 128), F32)]
         + [pltpu.VMEM(square.shape, BF16)]
         + [pltpu.SemaphoreType.DMA((3,))] * 2
+        + [low] * 6
+        + [bins] * 6
+        + [out] * 4
+        + [back_out] * 4
         + ring_scratch(tracks)
         + extra,
         collective,

time: 460 us -> 462 us (level)
  no operation moved by 1% of the time
where the time goes in v4:
time: 462 us; the launch traced here: 453 us
  Pallas kernels  443 us (96%)
  local copies, waits for them, and re-layouts  9.04 us (2%)
    pallas_call x12, Pallas kernels, fused_call(): pl.pallas_call(body, out_shape=tuple((jax.ShapeDtypeStruct(*out) for out...  436 us

profile of v4, /device:TPU:0, one launch (start us, length us, event | category | flops | bytes accessed | tf_op | source)
XLA Modules:
  0.0 452.9 jit_solution(10647509589845574415)
XLA Ops:
  0.6 1.3 copy.31.refs_6_
  2.0 4.4 copy.30.refs_5_
  6.4 29.1 %first_project.1 = (f32[768,512]{1,0:T(8,128)}, f32[768,128]{1,0:T(8,128)}, bf16[8,768,256]{2,1,0:T(8,128)(2,1)}, f32[576,2048]{1,0:T(8,128)}, bf16[2,576,768]{2...) custom-call(bf16[192,2048]{1,0:T(8,128)(2,1)} %refs_0_.3, ...), custom_call_target="tpu_custom_call" | custom-call | tf_op jit(solution)/shard_map/first_project/pallas_call | solution.py:127
  35.6 27.1 %conv_forward.2 = (bf16[768,512]{1,0:T(8,128)(2,1)}, f32[192,2048]{1,0:T(8,128)}, bf16[2,768,768]{2,1,0:T(8,128)(2,1)}) custom-call(f32[2,192,2048]{2,1,0:T(8,128)} %refs_3_.5, f32[576,2048]{1,0:T(8,128)} %get-tuple-element.82.refs_1_, f32[2,192,128]{2,1,0:T(8,128)} %get-tuple-element.83.refs_2_.refs_4_, f32[8,2048]{1,0:T(8,128)} %get-tuple-element.84.refs_3_.refs_5_, ...), custom_call_target="tpu_custom_call" | custom-call | tf_op jit(solution)/shard_map/conv_forward/pallas_call | solution.py:127
  62.7 59.2 %feed_forward.2 = (f32[768,512]{1,0:T(8,128)}, bf16[8,768,256]{2,1,0:T(8,128)(2,1)}, f32[768,512]{1,0:T(8,128)}, bf16[8,768,256]{2,1,0:T(8,128)(2,1)}, bf16[8,76...) custom-call(bf16[768,512]{1,0:T(8,128)(2,1)} %get-tuple-element.85.r, ...), custom_call_target="tpu_custom_call" | custom-call | tf_op jit(solution)/shard_map/feed_forward/pallas_call | solution.py:127
  121.9 33.1 %conv_forward.3 = (bf16[768,512]{1,0:T(8,128)(2,1)}, f32[192,2048]{1,0:T(8,128)}, bf16[8,768,256]{2,1,0:T(8,128)(2,1)}) custom-call(f32[2,192,2048]{2,1,0:T(8,128)} %refs_3_.5, f32[576,2048]{1,0:T(8,128)} %get-tuple-element.91.refs_1_, f32[2,192,128]{2,1,0:T(8,128)} %get-tuple-element.83.refs_2_.refs_4_, f32[8,2048]{1,0:T(8,128)} %get-tuple-element.84.refs_3_.refs_5_, ...), custom_call_target="tpu_custom_call" | custom-call | tf_op jit(solution)/shard_map/conv_forward/pallas_call | solution.py:127
  155.0 40.5 %feed_forward.3 = (f32[768,512]{1,0:T(8,128)}, bf16[8,768,256]{2,1,0:T(8,128)(2,1)}, bf16[768,512]{1,0:T(8,128)(2,1)}, bf16[8,768,256]{2,1,0:T(8,128)(2,1)}, bf1...) custom-call(bf16[768,512]{1,0:T(8,128)(2,1)} %get-tuple-element.93.refs_0_.refs_8_, ...), custom_call_target="tpu_custom_call" | custom-call | tf_op jit(solution)/shard_map/feed_forward/pallas_call | solution.py:127
  195.5 38.4 %feed_back.2 = (f32[768,512]{1,0:T(8,128)}, bf16[192,2048]{1,0:T(8,128)(2,1)}, bf16[8,288,768]{2,1,0:T(8,128)(2,1)}, bf16[768,768]{1,0:T(8,128)(2,1)}, f32[768,8]{1,0:T(8,128)}) custom-call(bf16[8,768,256]{2,1,0:T(8,128)(2,1)} %get-tuple-element.92.refs_0_, bf16[2,768,768]{2,1,0:T(8,128)(2,1)} %refs_1_.5, bf16[8,768,256]{2,1,0:T(8,128)(2,1)} %get-tuple-element.96.refs_2_, ...), custom_call_target="tpu_custom_call" | custom-call | tf_op jit(solution)/shard_map/feed_back/pallas_call | solution.py:127
  233.9 37.4 %conv_backward.2 = (bf16[576,2048]{1,0:T(8,128)(2,1)}, bf16[8,48,1024]{2,1,0:T(8,128)(2,1)}, f32[192,768]{1,0:T(8,128)}, f32[192,128]{1,0:T(8,128)}, bf16[2,288,384]{2,1,0:T(8,128)(2,1)}, /*index=5*/f32[192,2048]{1,0:T(8,128)}) custom-call(bf16[192,2048]{1,0:T(8,128)(2,1)} %get-tuple-element.101.refs_0_, f32[576,2048]{1,0:T(8,128)} %get-tuple-element.91.refs_1_, ...), custom_call_target="tpu_custom_call" | custom-call | tf_op jit(solution)/shard_map/conv_backward/pallas_call | solution.py:127
  271.2 27.3 %project_back.2 = (f32[768,512]{1,0:T(8,128)}, bf16[8,96,768]{2,1,0:T(8,128)(2,1)}, f32[768,8]{1,0:T(8,128)}, bf16[2,288,384]{2,1,0:T(8,128)(2,1)}, bf16[2,48,51...) custom-call(bf16[576,2048]{1,0:T(8,128)(2,1)} %get-tuple-element.107.refs_0_, ...), custom_call_target="tpu_custom_call" | custom-call | tf_op jit(solution)/shard_map/project_back/pallas_call | solution.py:127
  298.6 49.8 %feed_back.3 = (f32[768,512]{1,0:T(8,128)}, bf16[192,2048]{1,0:T(8,128)(2,1)}, bf16[8,288,768]{2,1,0:T(8,128)(2,1)}, bf16[768,768]{1,0:T(8,128)(2,1)}, f32[768,8...) custom-call(f32[768,512]{1,0:T(8,128)} %get-tuple-element.113.refs_0_, ...), custom_call_target="tpu_custom_call" | custom-call | tf_op jit(solution)/shard_map/feed_back/pallas_call | solution.py:127
  348.4 35.6 %conv_backward.3 = (bf16[576,2048]{1,0:T(8,128)(2,1)}, bf16[8,48,1024]{2,1,0:T(8,128)(2,1)}, f32[192,768]{1,0:T(8,128)}, f32[192,128]{1,0:T(8,128)}, bf16[2,288,384]{2,1,0:T(8,128)(2,1)}) custom-call(bf16[192,2048]{1,0:T(8,128)(2,1)} %get-tuple-element.123.refs_0_, f32[576,2048]{1,0:T(8,128)} %get-tuple-element.82.refs_1_, ...), custom_call_target="tpu_custom_call" | custom-call | tf_op jit(solution)/shard_map/conv_backward/pallas_call | solution.py:127
  384.0 30.8 %project_back.3 = (f32[768,512]{1,0:T(8,128)}, bf16[8,96,768]{2,1,0:T(8,128)(2,1)}, f32[768,8]{1,0:T(8,128)}, f32[288,768]{1,0:T(8,128)}, bf16[2,48,512]{2,1,0:T(8,128)(2,1)}, /*index=5*/bf16[2,96,384]{2,1,0:T(8,128)(2,1)}) custom-call(bf16[576,2048]{1,0:T(8,128)(2,1)} %get-tuple-element.127.refs_0_, bf16[2,576,768]{2,1,0:T(8,128)(2,1)} %get-tuple-element.90.refs_6_.refs_1_, ...), custom_call_target="tpu_custom_call" | custom-call | tf_op jit(solution)/shard_map/project_back/pallas_call | solution.py:127
  414.8 28.1 %last_sums.1 = (f32[192,2048]{1,0:T(8,128)}, f32[32,256]{1,0:T(8,128)}, f32[48,1024]{1,0:T(8,128)}, f32[96,768]{1,0:T(8,128)}) custom-call(f32[768,512]{1,0:T(8,128)} %get-tuple-element.133.refs_0_, f32[768,8]{1,0:T(8,128)} %get-tuple-element.134.refs_1_, f32[768,8]{1,0:T(8,128)} %get-tuple-element.135.refs_2_, f32[768,8]{1,0:T(8,128)} %get-tuple-element.136.refs_3_, ...), custom_call_target="tpu_custom_call" | custom-call | tf_op jit(solution)/shard_map/last_sums/pallas_call | solution.py:127
  442.9 6.5 %collect.1 = (f32[192,2048]{1,0:T(8,128)}, f32[192,2048]{1,0:T(8,128)}, f32[2,192]{1,0:T(2,128)}, f32[2,192]{1,0:T(2,128)}, f32[2,24,3,768]{3,2,1,0:T(4,128)}, /...) custom-call(f32[192,2048]{1,0:T(8,128)} %get-tuple-element.106.refs_, ...), custom_call_target="tpu_custom_call" | custom-call | tf_op jit(solution)/shard_map/collect/pallas_call | solution.py:1865
  449.4 1.4 copy.33
  450.8 1.9 copy.32

commit v5 on v4

--- a/solution.py
+++ b/solution.py
@@ -378,25 +378,21 @@
     return -(-rows // 16) * 16
 
 
-def split_rows(target, source, unit, joined):
-    rows, kinds, lanes = source.shape
+def split_rows(target, source, unit):
+    _, kinds, lanes = source.shape
 
     def one(n, carry):
         here = span(n, unit)
         for kind in range(kinds):
-            values = source[here, kind, :]
-            if joined:
-                target[here, kind * lanes : (kind + 1) * lanes] = values
-            else:
-                target[pl.ds(pl.multiple_of(kind * rows + n * unit, unit), unit), :] = values
+            target[here, kind * lanes : (kind + 1) * lanes] = source[here, kind, :]
         return carry
 
     return one
 
 
 def first_project_kernel(
-    io, inputs_ref, mix_gain, mix_bias, glu_gain, glu_bias, weight_in, short_in, cond_in, up_in,
-    seq_ref, x_ref, gains_ref, full, project_ref, weight_ref, up_ref, columns_ref, keep_ref,
+    io, inputs_ref, mix_gain, mix_bias, glu_gain, glu_bias, weight_ref, short_in, cond_in, up_in,
+    seq_ref, x_ref, gains_ref, full, project_ref, up_ref, columns_ref, keep_ref,
     raw, gains_low, gains_land, turn, send, recv, gains_send, gains_recv,
 ):
     peers = chan_peers()
@@ -425,21 +421,19 @@
         raw[part, span(me, shard, 32), :] = inputs_ref[:, part * half : (part + 1) * half]
         for kind in range(2):
             gather(kind, part).start()
-    io.ready(5, 6, 7)
+    io.ready(6, 7)
     for layer in range(layers):
-        lax.fori_loop(0, shard // 48, split_rows(weight_ref.at[layer], weight_in.at[layer], 48, False), 0)
         turn[...] = jnp.zeros_like(turn)
-        for tap in range(3):
-            turn[3 * tap : 3 * tap + 3, :shard] = short_in[layer, tap]
+        for row in range(9):
+            turn[row : row + 1, :shard] = short_in[row // 3, row % 3, layer : layer + 1, :]
         turn[9:10, :shard] = cond_in[layer : layer + 1, :]
         columns_ref[layer] = turn[...].T[:shard]
     slot = lax.broadcasted_iota(jnp.int32, keep_ref.shape, 1)
     row = lax.broadcasted_iota(jnp.int32, keep_ref.shape, 0)
     within = slot & (seq_ref[0, 0] - 1)
     keep_ref[...] = jnp.where(within > row, 1.0, 0.0)
-    io.flush(4)
+    io.flush(5)
     io.flush(6)
-    io.flush(7)
     for copy in copies:
         copy.wait()
     turn[...] = jnp.zeros_like(turn)
@@ -447,7 +441,7 @@
         turn[: 4 * layers, :shard] = gains_land[owner]
         gains_ref[owner * shard : (owner + 1) * shard, :] = turn[...].T[:shard]
     io.flush(1)
-    io.ready(8)
+    io.ready(5, 8)
     gather(0, 0).wait_recv()
     gather(2, 0).start()
     for part in range(parts):
@@ -466,34 +460,34 @@
         full[part] = (normal * gains_ref[:, 0:1] + gains_ref[:, 1:2]).astype(BF16)
         io.flush(2, part, part)
         columns = slice(part * half, (part + 1) * half)
-        project_ref[:, columns] = matmul(weight_ref[0], full[part])
+        project_ref[:, columns] = matmul(weight_ref[...], full[part])
         io.flush(3, part, (slice(None), pl.ds(part * half, half)))
         cuts = width // 64
         lax.fori_loop(
-            cuts * part // parts, cuts * (part + 1) // parts, split_rows(up_ref, up_in, 64, True), 0
+            cuts * part // parts, cuts * (part + 1) // parts, split_rows(up_ref, up_in, 64), 0
         )
     io.flush(0)
-    io.flush(5)
+    io.flush(4)
     for part in range(parts):
         for kind in range(3):
             gather(kind, part).wait_send()
 
 
-def first_project(inputs, gain_arrays, in_proj, short_conv, cond_weight, glu_in, seq_table,
+def first_project(inputs, gain_arrays, weight, short_conv, cond_weight, glu_in, seq_table,
                   collective):
     shard, slots = inputs.shape
-    layers, _, streams, width = in_proj.shape
+    layers = len(gain_arrays[0])
+    rows, width = weight[0].shape[1:]
     hidden = glu_in[0].shape[3]
     tokens = slots // 4
     return fused_call(
         first_project_kernel,
-        [inputs, *gain_arrays, in_proj, short_conv, cond_weight, glu_in, seq_table],
+        [inputs, *gain_arrays, weight, short_conv, cond_weight, glu_in, seq_table],
         [
             ((width, tokens), F32),
             ((width, 128), F32),
             ((8, width, tokens // 2), BF16),
-            ((streams * shard, slots), F32),
-            ((layers, streams * shard, width), BF16),
+            ((rows, slots), F32),
             ((width, 2 * hidden), BF16),
             ((layers, shard, 128), F32),
             ((8, slots), F32),
@@ -508,7 +502,7 @@
         + [pltpu.SemaphoreType.DMA((3,))] * 2,
         collective,
         "first_project",
-        (1, 1, 8, 8, 1, 1, 1, 1),
+        (1, 1, 8, 8, 1, 1, 1),
         9,
     )
 
@@ -661,10 +655,11 @@
     def partial(block, step):
         normed = full[block]
         tile = 256
+        gates = matmul(up_weight[:hidden], normed)
+        ups = matmul(up_weight[hidden:], normed)
         for n in range(hidden // tile):
-            gate = matmul(up_weight[n * tile : (n + 1) * tile], normed)
-            up = matmul(up_weight[hidden + n * tile : hidden + (n + 1) * tile], normed)
             rows = slice(n * tile, (n + 1) * tile)
+            gate, up = gates[rows], ups[rows]
             cdf = 0.5 * (1.0 + lax.erf(gate * math.sqrt(0.5)))
             density = jnp.exp(-0.5 * gate * gate) * (1.0 / math.sqrt(2.0 * math.pi))
             gelu = gate * cdf
@@ -683,7 +678,7 @@
         if follows:
             cuts = width // 64
             lax.fori_loop(
-                cuts * part // 2, cuts * (part + 1) // 2, split_rows(next_up, up_in, 64, True), 0
+                cuts * part // 2, cuts * (part + 1) // 2, split_rows(next_up, up_in, 64), 0
             )
         columns = slice(part * half, (part + 1) * half)
         value = mid_ref[:, columns] + scattered(peers, scatter_sems, buffers, own, part)
@@ -840,10 +835,10 @@
     def partial(block, step):
         for copy in loads(step, block):
             copy.wait()
-        grad = full[block]
+        unit_grads = matmul(down_rows[...], full[block])
         for n in range(hidden // tile):
             rows = slice(n * tile, (n + 1) * tile)
-            unit_grad = matmul(down_rows[rows], grad)
+            unit_grad = unit_grads[rows]
             slopes[block, rows] = (unit_grad * slopes[block, rows].astype(F32)).astype(BF16)
             gelus[block, rows] = (unit_grad * gelus[block, rows].astype(F32)).astype(BF16)
         return matmul(up_columns[:, :hidden], slopes[block]) + matmul(
@@ -1820,7 +1815,7 @@
     ]
     for copy in loads:
         copy.start()
-    each = in_grad.shape[1]
+    each = in_grad.shape[2]
     shard = cond.shape[1]
     lanes = filters[0].shape[1]
     for layer in range(layers):
@@ -1828,11 +1823,11 @@
             row = 4 * layer + kind
             out[layer : layer + 1, :] = small[row : row + 1, :shard]
         row = 4 * layers + 10 * layer
-        for tap in range(3):
-            short[layer, tap] = small[row + 3 * tap : row + 3 * tap + 3, :shard]
+        for n in range(9):
+            short[n // 3, n % 3, layer : layer + 1, :] = small[row + n : row + n + 1, :shard]
         cond[layer : layer + 1, :] = small[row + 9 : row + 10, :shard]
         for stream in range(3):
-            in_grad[layer, :, stream, :] = packs[layer][stream * each : (stream + 1) * each]
+            in_grad[layer, stream] = packs[layer][stream * each : (stream + 1) * each]
         out_grad[layer] = packs[layer][3 * each : 4 * each]
         for n in range(filter_grad.shape[2] // lanes):
             filter_grad[layer, :, n * lanes : (n + 1) * lanes] = filters[layer][
@@ -1858,8 +1853,8 @@
     operands = [outputs, input_grad, small, *feeds, *filters, *packs]
     small_shape = (layers, shard)
     shapes = [
-        (shard, slots), (shard, slots), small_shape, small_shape, (layers, each, 3, width),
-        (layers, 3, 3, shard), (layers, each, slots), small_shape, (layers, each, width),
+        (shard, slots), (shard, slots), small_shape, small_shape, (layers, 3, each, width),
+        (3, 3, layers, shard), (layers, each, slots), small_shape, (layers, each, width),
         small_shape, small_shape, (layers, rows, 2, hidden), (layers, rows, hidden),
     ]
     return pl.pallas_call(
@@ -1897,8 +1892,10 @@
     each = shard // count
     table = jnp.asarray(dft_table(slots // blocks), BF16)
     sign = jnp.asarray(np.tile(1.0 - 2.0 * (np.arange(slots // blocks) % 2), (8, 1)), F32)
-    residual, gains, normed, project, in_rows, up_columns, columns, keep = first_project(
-        inputs, (mix_gain, mix_bias, glu_gain, glu_bias), in_proj, short_conv, cond_weight,
+    in_rows = in_proj.transpose(0, 2, 1, 3).reshape(layers, 3 * shard, width)
+    taps = short_conv.transpose(1, 2, 0, 3)
+    residual, gains, normed, project, up_columns, columns, keep = first_project(
+        inputs, (mix_gain, mix_bias, glu_gain, glu_bias), (in_rows, 0), taps, cond_weight,
         (glu_in, 0), seq_table, 1,
     )
     constants = (keep, sign, table, seq_table, jnp.asarray(dft_table(slots // blocks).T, BF16))
@@ -1957,7 +1954,10 @@
     input_grad, small, filters[0], packs[0] = last_sums(
         state, [one for pair in gain_sums for one in pair], row_sums, waiting, 60
     )
-    return collect(outputs, input_grad, small, feeds, filters, packs, each)
+    results = list(collect(outputs, input_grad, small, feeds, filters, packs, each))
+    results[4] = results[4].transpose(0, 2, 1, 3)
+    results[5] = results[5].transpose(2, 0, 1, 3)
+    return tuple(results)
 
 
 def solution(mesh):

time: 462 us -> 454 us (0.983)
  local copies, waits for them, and re-layouts: 9.04 us -> 0 us
    unnamed x2 -> x0, local copies, waits for them, and re-layouts: 5.77 us -> none
where the time goes in v5:
time: 454 us; the launch traced here: 447 us
  Pallas kernels  446 us (98%)
    pallas_call x12, Pallas kernels, fused_call(): pl.pallas_call(body, out_shape=tuple((jax.ShapeDtypeStruct(*out) for out...  439 us

profile of v5, /device:TPU:0, one launch (start us, length us, event | category | flops | bytes accessed | tf_op | source)
XLA Modules:
  0.0 446.6 jit_solution(10122573474848903693)
XLA Ops:
  0.6 29.0 %first_project.1 = (f32[768,512]{1,0:T(8,128)}, f32[768,128]{1,0:T(8,128)}, bf16[8,768,256]{2,1,0:T(8,128)(2,1)}, f32[576,2048]{1,0:T(8,128)}, bf16[768,1536]{1,...) custom-call(bf16[192,2048]{1,0:T(8,128)(2,1)} %refs_0_.3, f32[2,192]{1,0:T(2,128)} %refs_1_.3, ...), custom_call_target="tpu_custom_call" | custom-call | tf_op jit(solution)/shard_map/first_project/pallas_call | solution.py:127
  29.7 27.2 %conv_forward.2 = (bf16[768,512]{1,0:T(8,128)(2,1)}, f32[192,2048]{1,0:T(8,128)}, bf16[2,768,768]{2,1,0:T(8,128)(2,1)}) custom-call(f32[2,192,2048]{2,1,0:T(8,128)} %refs_3_.5, f32[576,2048]{1,0:T(8,128)} %get-tuple-element.94.refs_1_, f32[2,192,128]{2,1,0:T(8,128)} %get-tuple-element.95.refs_2_.refs_4_, f32[8,2048]{1,0:T(8,128)} %get-tuple-element.96.refs_3_.refs_5_, ...), custom_call_target="tpu_custom_call" | custom-call | tf_op jit(solution)/shard_map/conv_forward/pallas_call | solution.py:127
  56.8 59.2 %feed_forward.2 = (f32[768,512]{1,0:T(8,128)}, bf16[8,768,256]{2,1,0:T(8,128)(2,1)}, f32[768,512]{1,0:T(8,128)}, bf16[8,768,256]{2,1,0:T(8,128)(2,1)}, bf16[8,76...) custom-call(bf16[768,512]{1,0:T(8,128)(2,1)} %get-tuple-element.97.r, ...), custom_call_target="tpu_custom_call" | custom-call | tf_op jit(solution)/shard_map/feed_forward/pallas_call | solution.py:127
  116.0 33.1 %conv_forward.3 = (bf16[768,512]{1,0:T(8,128)(2,1)}, f32[192,2048]{1,0:T(8,128)}, bf16[8,768,256]{2,1,0:T(8,128)(2,1)}) custom-call(f32[2,192,2048]{2,1,0:T(8,128)} %refs_3_.5, f32[576,2048]{1,0:T(8,128)} %get-tuple-element.102.refs_1_, f32[2,192,128]{2,1,0:T(8,128)} %get-tuple-element.95.refs_2_.refs_4_, f32[8,2048]{1,0:T(8,128)} %get-tuple-element.96.refs_3_.refs_5_, ...), custom_call_target="tpu_custom_call" | custom-call | tf_op jit(solution)/shard_map/conv_forward/pallas_call | solution.py:127
  149.1 40.5 %feed_forward.3 = (f32[768,512]{1,0:T(8,128)}, bf16[8,768,256]{2,1,0:T(8,128)(2,1)}, bf16[768,512]{1,0:T(8,128)(2,1)}, bf16[8,768,256]{2,1,0:T(8,128)(2,1)}, bf1...) custom-call(bf16[768,512]{1,0:T(8,128)(2,1)} %get-tuple-element.104.refs_0_.refs_8_, ...), custom_call_target="tpu_custom_call" | custom-call | tf_op jit(solution)/shard_map/feed_forward/pallas_call | solution.py:127
  189.6 40.8 %feed_back.2 = (f32[768,512]{1,0:T(8,128)}, bf16[192,2048]{1,0:T(8,128)(2,1)}, bf16[8,288,768]{2,1,0:T(8,128)(2,1)}, bf16[768,768]{1,0:T(8,128)(2,1)}, f32[768,8]{1,0:T(8,128)}) custom-call(bf16[8,768,256]{2,1,0:T(8,128)(2,1)} %get-tuple-element.103.refs_0_, bf16[2,768,768]{2,1,0:T(8,128)(2,1)} %refs_1_.5, bf16[8,768,256]{2,1,0:T(8,128)(2,1)} %get-tuple-element.107.refs_2_, ...), custom_call_target="tpu_custom_call" | custom-call | tf_op jit(solution)/shard_map/feed_back/pallas_call | solution.py:127
  230.5 37.4 %conv_backward.2 = (bf16[576,2048]{1,0:T(8,128)(2,1)}, bf16[8,48,1024]{2,1,0:T(8,128)(2,1)}, f32[192,768]{1,0:T(8,128)}, f32[192,128]{1,0:T(8,128)}, bf16[2,288,384]{2,1,0:T(8,128)(2,1)}, /*index=5*/f32[192,2048]{1,0:T(8,128)}) custom-call(bf16[192,2048]{1,0:T(8,128)(2,1)} %get-tuple-element.112.refs_0_, f32[576,2048]{1,0:T(8,128)} %get-tuple-element.102.refs_1_, ...), custom_call_target="tpu_custom_call" | custom-call | tf_op jit(solution)/shard_map/conv_backward/pallas_call | solution.py:127
  267.9 27.2 %project_back.2 = (f32[768,512]{1,0:T(8,128)}, bf16[8,96,768]{2,1,0:T(8,128)(2,1)}, f32[768,8]{1,0:T(8,128)}, bf16[2,288,384]{2,1,0:T(8,128)(2,1)}, bf16[2,48,51...) custom-call(bf16[576,2048]{1,0:T(8,128)(2,1)} %get-tuple-element.118.refs_0_, bf16[2,576,768]{2,1,0:T(8,128)(2,1)} %bitcast.10, ...), custom_call_target="tpu_custom_call" | custom-call | tf_op jit(solution)/shard_map/project_back/pallas_call | solution.py:127
  295.1 49.6 %feed_back.3 = (f32[768,512]{1,0:T(8,128)}, bf16[192,2048]{1,0:T(8,128)(2,1)}, bf16[8,288,768]{2,1,0:T(8,128)(2,1)}, bf16[768,768]{1,0:T(8,128)(2,1)}, f32[768,8...) custom-call(f32[768,512]{1,0:T(8,128)} %get-tuple-element.124.refs_0_, ...), custom_call_target="tpu_custom_call" | custom-call | tf_op jit(solution)/shard_map/feed_back/pallas_call | solution.py:127
  344.7 36.4 %conv_backward.3 = (bf16[576,2048]{1,0:T(8,128)(2,1)}, bf16[8,48,1024]{2,1,0:T(8,128)(2,1)}, f32[192,768]{1,0:T(8,128)}, f32[192,128]{1,0:T(8,128)}, bf16[2,288,384]{2,1,0:T(8,128)(2,1)}) custom-call(bf16[192,2048]{1,0:T(8,128)(2,1)} %get-tuple-element.134.refs_0_, f32[576,2048]{1,0:T(8,128)} %get-tuple-element.94.refs_1_, ...), custom_call_target="tpu_custom_call" | custom-call | tf_op jit(solution)/shard_map/conv_backward/pallas_call | solution.py:127
  381.1 31.1 %project_back.3 = (f32[768,512]{1,0:T(8,128)}, bf16[8,96,768]{2,1,0:T(8,128)(2,1)}, f32[768,8]{1,0:T(8,128)}, f32[288,768]{1,0:T(8,128)}, bf16[2,48,512]{2,1,0:T(8,128)(2,1)}, /*index=5*/bf16[2,96,384]{2,1,0:T(8,128)(2,1)}) custom-call(bf16[576,2048]{1,0:T(8,128)(2,1)} %get-tuple-element.138.refs_0_, bf16[2,576,768]{2,1,0:T(8,128)(2,1)} %bitcast.11, ...), custom_call_target="tpu_custom_call" | custom-call | tf_op jit(solution)/shard_map/project_back/pallas_call | solution.py:127
  412.2 27.9 %last_sums.1 = (f32[192,2048]{1,0:T(8,128)}, f32[32,256]{1,0:T(8,128)}, f32[48,1024]{1,0:T(8,128)}, f32[96,768]{1,0:T(8,128)}) custom-call(f32[768,512]{1,0:T(8,128)} %get-tuple-element.144.refs_0_, f32[768,8]{1,0:T(8,128)} %get-tuple-element.145.refs_1_, f32[768,8]{1,0:T(8,128)} %get-tuple-element.146.refs_2_, f32[768,8]{1,0:T(8,128)} %get-tuple-element.147.refs_3_, ...), custom_call_target="tpu_custom_call" | custom-call | tf_op jit(solution)/shard_map/last_sums/pallas_call | solution.py:127
  440.0 6.4 %collect.1 = (f32[192,2048]{1,0:T(8,128)}, f32[192,2048]{1,0:T(8,128)}, f32[2,192]{1,0:T(2,128)}, f32[2,192]{1,0:T(2,128)}, f32[2,3,24,768]{3,2,1,0:T(8,128)}, /...) custom-call(f32[192,2048]{1,0:T(8,128)} %get-tuple-element.117.refs_, ...), custom_call_target="tpu_custom_call" | custom-call | tf_op jit(solution)/shard_map/collect/pallas_call | solution.py:1860

commit v6 on v5

--- a/solution.py
+++ b/solution.py
@@ -835,10 +835,10 @@
     def partial(block, step):
         for copy in loads(step, block):
             copy.wait()
-        unit_grads = matmul(down_rows[...], full[block])
+        grad = full[block]
         for n in range(hidden // tile):
             rows = slice(n * tile, (n + 1) * tile)
-            unit_grad = unit_grads[rows]
+            unit_grad = matmul(down_rows[rows], grad)
             slopes[block, rows] = (unit_grad * slopes[block, rows].astype(F32)).astype(BF16)
             gelus[block, rows] = (unit_grad * gelus[block, rows].astype(F32)).astype(BF16)
         return matmul(up_columns[:, :hidden], slopes[block]) + matmul(

time: 454 us -> 451 us (level)
  no operation moved by 1% of the time
where the time goes in v6:
time: 451 us; the launch traced here: 444 us
  Pallas kernels  443 us (98%)
    pallas_call x12, Pallas kernels, fused_call(): pl.pallas_call(body, out_shape=tuple((jax.ShapeDtypeStruct(*out) for out...  437 us

profile of v6, /device:TPU:0, one launch (start us, length us, event | category | flops | bytes accessed | tf_op | source)
XLA Modules:
  0.0 443.9 jit_solution(7210612994495634126)
XLA Ops:
  0.6 29.0 %first_project.1 = (f32[768,512]{1,0:T(8,128)}, f32[768,128]{1,0:T(8,128)}, bf16[8,768,256]{2,1,0:T(8,128)(2,1)}, f32[576,2048]{1,0:T(8,128)}, bf16[768,1536]{1,...) custom-call(bf16[192,2048]{1,0:T(8,128)(2,1)} %refs_0_.3, f32[2,192]{1,0:T(2,128)} %refs_1_.3, ...), custom_call_target="tpu_custom_call" | custom-call | tf_op jit(solution)/shard_map/first_project/pallas_call | solution.py:127
  29.7 27.2 %conv_forward.2 = (bf16[768,512]{1,0:T(8,128)(2,1)}, f32[192,2048]{1,0:T(8,128)}, bf16[2,768,768]{2,1,0:T(8,128)(2,1)}) custom-call(f32[2,192,2048]{2,1,0:T(8,128)} %refs_3_.5, f32[576,2048]{1,0:T(8,128)} %get-tuple-element.94.refs_1_, f32[2,192,128]{2,1,0:T(8,128)} %get-tuple-element.95.refs_2_.refs_4_, f32[8,2048]{1,0:T(8,128)} %get-tuple-element.96.refs_3_.refs_5_, ...), custom_call_target="tpu_custom_call" | custom-call | tf_op jit(solution)/shard_map/conv_forward/pallas_call | solution.py:127
  56.8 59.2 %feed_forward.2 = (f32[768,512]{1,0:T(8,128)}, bf16[8,768,256]{2,1,0:T(8,128)(2,1)}, f32[768,512]{1,0:T(8,128)}, bf16[8,768,256]{2,1,0:T(8,128)(2,1)}, bf16[8,76...) custom-call(bf16[768,512]{1,0:T(8,128)(2,1)} %get-tuple-element.97.r, ...), custom_call_target="tpu_custom_call" | custom-call | tf_op jit(solution)/shard_map/feed_forward/pallas_call | solution.py:127
  116.0 33.1 %conv_forward.3 = (bf16[768,512]{1,0:T(8,128)(2,1)}, f32[192,2048]{1,0:T(8,128)}, bf16[8,768,256]{2,1,0:T(8,128)(2,1)}) custom-call(f32[2,192,2048]{2,1,0:T(8,128)} %refs_3_.5, f32[576,2048]{1,0:T(8,128)} %get-tuple-element.102.refs_1_, f32[2,192,128]{2,1,0:T(8,128)} %get-tuple-element.95.refs_2_.refs_4_, f32[8,2048]{1,0:T(8,128)} %get-tuple-element.96.refs_3_.refs_5_, ...), custom_call_target="tpu_custom_call" | custom-call | tf_op jit(solution)/shard_map/conv_forward/pallas_call | solution.py:127
  149.1 40.5 %feed_forward.3 = (f32[768,512]{1,0:T(8,128)}, bf16[8,768,256]{2,1,0:T(8,128)(2,1)}, bf16[768,512]{1,0:T(8,128)(2,1)}, bf16[8,768,256]{2,1,0:T(8,128)(2,1)}, bf1...) custom-call(bf16[768,512]{1,0:T(8,128)(2,1)} %get-tuple-element.104.refs_0_.refs_8_, ...), custom_call_target="tpu_custom_call" | custom-call | tf_op jit(solution)/shard_map/feed_forward/pallas_call | solution.py:127
  189.6 38.2 %feed_back.2 = (f32[768,512]{1,0:T(8,128)}, bf16[192,2048]{1,0:T(8,128)(2,1)}, bf16[8,288,768]{2,1,0:T(8,128)(2,1)}, bf16[768,768]{1,0:T(8,128)(2,1)}, f32[768,8]{1,0:T(8,128)}) custom-call(bf16[8,768,256]{2,1,0:T(8,128)(2,1)} %get-tuple-element.103.refs_0_, bf16[2,768,768]{2,1,0:T(8,128)(2,1)} %refs_1_.5, bf16[8,768,256]{2,1,0:T(8,128)(2,1)} %get-tuple-element.107.refs_2_, ...), custom_call_target="tpu_custom_call" | custom-call | tf_op jit(solution)/shard_map/feed_back/pallas_call | solution.py:127
  227.8 37.7 %conv_backward.2 = (bf16[576,2048]{1,0:T(8,128)(2,1)}, bf16[8,48,1024]{2,1,0:T(8,128)(2,1)}, f32[192,768]{1,0:T(8,128)}, f32[192,128]{1,0:T(8,128)}, bf16[2,288,384]{2,1,0:T(8,128)(2,1)}, /*index=5*/f32[192,2048]{1,0:T(8,128)}) custom-call(bf16[192,2048]{1,0:T(8,128)(2,1)} %get-tuple-element.112.refs_0_, f32[576,2048]{1,0:T(8,128)} %get-tuple-element.102.refs_1_, ...), custom_call_target="tpu_custom_call" | custom-call | tf_op jit(solution)/shard_map/conv_backward/pallas_call | solution.py:127
  265.5 27.1 %project_back.2 = (f32[768,512]{1,0:T(8,128)}, bf16[8,96,768]{2,1,0:T(8,128)(2,1)}, f32[768,8]{1,0:T(8,128)}, bf16[2,288,384]{2,1,0:T(8,128)(2,1)}, bf16[2,48,51...) custom-call(bf16[576,2048]{1,0:T(8,128)(2,1)} %get-tuple-element.118.refs_0_, bf16[2,576,768]{2,1,0:T(8,128)(2,1)} %bitcast.10, ...), custom_call_target="tpu_custom_call" | custom-call | tf_op jit(solution)/shard_map/project_back/pallas_call | solution.py:127
  292.6 50.0 %feed_back.3 = (f32[768,512]{1,0:T(8,128)}, bf16[192,2048]{1,0:T(8,128)(2,1)}, bf16[8,288,768]{2,1,0:T(8,128)(2,1)}, bf16[768,768]{1,0:T(8,128)(2,1)}, f32[768,8...) custom-call(f32[768,512]{1,0:T(8,128)} %get-tuple-element.124.refs_0_, ...), custom_call_target="tpu_custom_call" | custom-call | tf_op jit(solution)/shard_map/feed_back/pallas_call | solution.py:127
  342.6 36.1 %conv_backward.3 = (bf16[576,2048]{1,0:T(8,128)(2,1)}, bf16[8,48,1024]{2,1,0:T(8,128)(2,1)}, f32[192,768]{1,0:T(8,128)}, f32[192,128]{1,0:T(8,128)}, bf16[2,288,384]{2,1,0:T(8,128)(2,1)}) custom-call(bf16[192,2048]{1,0:T(8,128)(2,1)} %get-tuple-element.134.refs_0_, f32[576,2048]{1,0:T(8,128)} %get-tuple-element.94.refs_1_, ...), custom_call_target="tpu_custom_call" | custom-call | tf_op jit(solution)/shard_map/conv_backward/pallas_call | solution.py:127
  378.6 31.0 %project_back.3 = (f32[768,512]{1,0:T(8,128)}, bf16[8,96,768]{2,1,0:T(8,128)(2,1)}, f32[768,8]{1,0:T(8,128)}, f32[288,768]{1,0:T(8,128)}, bf16[2,48,512]{2,1,0:T(8,128)(2,1)}, /*index=5*/bf16[2,96,384]{2,1,0:T(8,128)(2,1)}) custom-call(bf16[576,2048]{1,0:T(8,128)(2,1)} %get-tuple-element.138.refs_0_, bf16[2,576,768]{2,1,0:T(8,128)(2,1)} %bitcast.11, ...), custom_call_target="tpu_custom_call" | custom-call | tf_op jit(solution)/shard_map/project_back/pallas_call | solution.py:127
  409.6 27.7 %last_sums.1 = (f32[192,2048]{1,0:T(8,128)}, f32[32,256]{1,0:T(8,128)}, f32[48,1024]{1,0:T(8,128)}, f32[96,768]{1,0:T(8,128)}) custom-call(f32[768,512]{1,0:T(8,128)} %get-tuple-element.144.refs_0_, f32[768,8]{1,0:T(8,128)} %get-tuple-element.145.refs_1_, f32[768,8]{1,0:T(8,128)} %get-tuple-element.146.refs_2_, f32[768,8]{1,0:T(8,128)} %get-tuple-element.147.refs_3_, ...), custom_call_target="tpu_custom_call" | custom-call | tf_op jit(solution)/shard_map/last_sums/pallas_call | solution.py:127
  437.4 6.4 %collect.1 = (f32[192,2048]{1,0:T(8,128)}, f32[192,2048]{1,0:T(8,128)}, f32[2,192]{1,0:T(2,128)}, f32[2,192]{1,0:T(2,128)}, f32[2,3,24,768]{3,2,1,0:T(8,128)}, /...) custom-call(f32[192,2048]{1,0:T(8,128)} %get-tuple-element.117.refs_, ...), custom_call_target="tpu_custom_call" | custom-call | tf_op jit(solution)/shard_map/collect/pallas_call | solution.py:1860
